TPU v7x, 128 devices: a whole 4x4x4 slice. The times are simulated.
128 devices in a mesh: seq: 32 (over x, y, core), tp: 4 (over z).
Axes of the slice: x: 4, y: 4, z: 4, core: 2. Of those that a mesh axis runs over, the one named last changes fastest.
Arguments:
- tokens: bfloat16 [12288, 2560], P('seq', 'tp'), may hold values from -6 to 6
- w_query: bfloat16 [2560, 2560], P(None, 'tp'), may hold values from -0.125 to 0.125
- w_key: bfloat16 [2560, 2560], P(None, 'tp'), may hold values from -0.125 to 0.125
- w_value: bfloat16 [2560, 2560], P(None, 'tp'), may hold values from -0.125 to 0.125
- w_out: bfloat16 [2560, 2560], P('tp'), may hold values from -0.125 to 0.125
- shift_filter: float32 [64, 2560], P(None, 'tp'), may hold values from -0.75 to 0.75
- log_decay: float32 [64, 2560], P(None, 'tp'), may hold values from 8.138021e-05 to 0.03
- readout: float32 [64, 2560], P(None, 'tp'), may hold values from -3 to 3
- skip_gain: float32 [2560], P('tp'), may hold values from 0.5 to 1.5
- init_state: float32 [64, 2560], P(None, 'tp'), may hold values from -6 to 6
- cotangent: bfloat16 [12288, 2560], P('seq', 'tp'), may hold values from -6 to 6
Outputs:
- mixed: bfloat16 [12288, 2560], P('seq', 'tp')
- grad_input: bfloat16 [12288, 2560], P('seq', 'tp')
- grad_query: float32 [2560, 2560], P('seq', 'tp')
- grad_key: float32 [2560, 2560], P('seq', 'tp')
- grad_value: float32 [2560, 2560], P('seq', 'tp')
- grad_out: float32 [2560, 2560], P('tp', 'seq')
- grad_filter: float32 [64, 2560], P(None, 'tp')
- grad_init: float32 [64, 2560], P(None, 'tp')
All inputs are finite; a program needn't handle non-finite values.
Results may differ from a plain program's by a relative error of at most 0.025.
Values may be sent and summed in bfloat16 or wider, within the bound.
No kernel may reach another device: no remote copies, remote signals or barrier semaphores. Data moves between devices by JAX's collectives and lax.ppermute only.
A program may use at most 192 MiB of HBM per device.

v0:
```python
import functools

import jax
import jax.numpy as jnp
from jax import lax
from jax.experimental import pallas as pl
from jax.experimental.pallas import tpu as pltpu
from jax.sharding import PartitionSpec as P

LANE = 128
F32 = jnp.float32
BF16 = jnp.bfloat16


def dot_nn(left, right):
    return lax.dot_general(left, right, (((1,), (0,)), ((), ())), preferred_element_type=F32)


def dot_nt(left, right):
    return lax.dot_general(left, right, (((1,), (1,)), ((), ())), preferred_element_type=F32)


def dot_tn(left, right):
    return lax.dot_general(left, right, (((0,), (0,)), ((), ())), preferred_element_type=F32)


def dot_tt(left, right):
    return lax.dot_general(left, right, (((0,), (1,)), ((), ())), preferred_element_type=F32)


def split_pair(value):
    high = value.astype(BF16)
    return high, (value - high.astype(F32)).astype(BF16)


SIDE = 4
MIB = 1024 * 1024


def call_cost(flops, bytes_accessed, transcendentals=0):
    return pl.CostEstimate(
        flops=flops, bytes_accessed=bytes_accessed, transcendentals=transcendentals
    )


def params(mebibytes):
    return pltpu.CompilerParams(vmem_limit_bytes=mebibytes * MIB)


def in_vmem(count):
    return [pl.BlockSpec(memory_space=pltpu.VMEM)] * count


def in_smem(count):
    return [pl.BlockSpec(memory_space=pltpu.SMEM)] * count


def anywhere(count):
    return [pl.BlockSpec(memory_space=pl.ANY)] * count


def padded(rows):
    return -(-rows // 8) * 8


def later(value, steps, source_at):
    at = source_at[:, : value.shape[1]]
    return jnp.where(at >= steps, pltpu.roll(value, steps, 0), 0.0)


def earlier(value, steps, source_at):
    sources = value.shape[0]
    at = source_at[:, : value.shape[1]]
    return jnp.where(at < sources - steps, pltpu.roll(value, sources - steps, 0), 0.0)


def circulant(row):
    return pltpu.roll(jnp.broadcast_to(row, (LANE, LANE)), 0, 1, stride=1, stride_axis=0)


def iotas(sources):
    lane_at = lax.broadcasted_iota(jnp.int32, (LANE, LANE), 1)
    row_at = lax.broadcasted_iota(jnp.int32, (LANE, LANE), 0)
    source_at = lax.broadcasted_iota(jnp.int32, (sources, LANE), 0)
    return lane_at, row_at, source_at


def decay_tables(cols_ref, channel, lane_at):
    rate = cols_ref[0, channel]
    read = cols_ref[1, channel]
    lanes = lane_at[: rate.shape[0]].astype(F32)
    step_decay = jnp.exp(-rate)
    inflow = 1.0 - step_decay
    rising = jnp.exp(-rate * lanes)
    falling = jnp.exp(-rate * (LANE - 1.0 - lanes))
    reading = (read * step_decay) * rising
    feeding = inflow * falling
    weight = read * inflow
    kernel_row = jnp.sum(weight * rising, axis=0, keepdims=True)
    wrapped = jnp.where(lanes > 0.0, step_decay * falling, 1.0)
    kernel_turned = jnp.sum(weight * wrapped, axis=0, keepdims=True)
    return reading.astype(BF16), feeding.astype(BF16), kernel_row, kernel_turned


def part_rows(value, sources):
    return [value[at : at + sources] for at in range(0, value.shape[0], sources)]


def load_rows(ref, row, sources, pad, parts):
    return [
        ref[pl.ds(row + part * sources * pad, sources, stride=pad), :] for part in range(parts)
    ]


def store_rows(ref, row, sources, pad, value):
    for part, piece in enumerate(part_rows(value, sources)):
        ref[pl.ds(row + part * sources * pad, sources, stride=pad), :] = piece


def spread(block_ref, rows_ref, pad):
    sources, count, width = block_ref.shape

    def step(source, carry):
        for part in range(width // LANE):
            row = pl.multiple_of((part * sources + source) * pad, 8)
            rows_ref[pl.ds(row, count), :] = block_ref[
                source, :, LANE * part : LANE * (part + 1)
            ].astype(F32)
        return carry

    lax.fori_loop(0, sources, step, 0)


def channel_body(
    channel, sources, parts, group, at, in_rows, out_rows, small_rows, rows_ref, cols_ref,
    taps_ref, skip_ref,
):
    lane_at, row_at, source_at = at
    in_pad, out_pad = padded(3 * group), padded(2 * group) + padded(group)
    key = load_rows(in_rows, channel, sources, in_pad, parts)
    value = jnp.concatenate(load_rows(in_rows, channel + group, sources, in_pad, parts), 0)
    grads = jnp.concatenate(load_rows(in_rows, channel + 2 * group, sources, in_pad, parts), 0)
    rate_row = rows_ref[0, pl.ds(channel, 1), :]
    start_row = rows_ref[1, pl.ds(channel, 1), :]
    states = rate_row.shape[1]
    reading, feeding, kernel_row, kernel_turned = decay_tables(cols_ref, channel, lane_at)
    ahead, behind = lane_at >= row_at, lane_at <= row_at
    local = jnp.where(ahead, circulant(kernel_row), 0.0).astype(BF16)
    local_turned = jnp.where(behind, circulant(kernel_turned), 0.0).astype(BF16)
    taps = circulant(taps_ref[0, pl.ds(channel, 1), :])
    taps_turned = circulant(taps_ref[1, pl.ds(channel, 1), :])
    taps_forward = jnp.concatenate(
        [jnp.where(ahead, 0.0, taps), jnp.where(ahead, taps, 0.0)], 0
    ).astype(BF16)
    taps_back = jnp.concatenate(
        [jnp.where(behind, taps_turned, 0.0), jnp.where(behind, 0.0, taps_turned)], 0
    ).astype(BF16)
    skip = skip_ref[channel]
    part_decay = jnp.exp(-rate_row * LANE)
    row_decay = jnp.exp(-rate_row * (LANE * parts))

    key_now = jnp.concatenate(key, 0)
    key_before = jnp.concatenate([later(key[-1], 1, source_at)] + key[:-1], 0)
    key_pair = jnp.concatenate([key_before, key_now], 1).astype(BF16)
    shifted = dot_nn(key_pair, taps_forward)
    drive = shifted * value
    drive_short = drive.astype(BF16)

    fed = part_rows(dot_nt(drive_short, feeding), sources)
    whole = fed[0]
    for part in range(1, parts):
        whole = part_decay * whole + fed[part]
    scan = jnp.where(source_at[:, :states] >= 1, pltpu.roll(whole, 1, 0), start_row)
    step, decay = 1, row_decay
    while step < sources:
        scan = scan + decay * later(scan, step, source_at)
        step, decay = 2 * step, decay * decay
    entering = [scan]
    for part in range(1, parts):
        entering.append(part_decay * entering[-1] + fed[part - 1])
    state_high, state_low = split_pair(jnp.concatenate(entering, 0))
    response = (
        dot_nn(
            jnp.concatenate([drive_short, state_high, state_low], 1),
            jnp.concatenate([local, reading, reading], 0),
        )
        + skip * drive
    )

    grad_short = grads.astype(BF16)
    read = part_rows(dot_nt(grad_short, reading), sources)
    whole = read[-1]
    for part in range(parts - 2, -1, -1):
        whole = part_decay * whole + read[part]
    scan = earlier(whole, 1, source_at)
    step, decay = 1, row_decay
    while step < sources:
        scan = scan + decay * earlier(scan, step, source_at)
        step, decay = 2 * step, decay * decay
    leaving = [scan]
    for part in range(parts - 1, 0, -1):
        leaving.insert(0, part_decay * leaving[0] + read[part])
    start_grad = (part_decay * leaving[0] + read[0])[0:1]
    carry_high, carry_low = split_pair(jnp.concatenate(leaving, 0))
    back_drive = (
        dot_nn(
            jnp.concatenate([grad_short, carry_high, carry_low], 1),
            jnp.concatenate([local_turned, feeding, feeding], 0),
        )
        + skip * grads
    )
    back_value = back_drive * shifted
    back_shifted = back_drive * value
    pieces = part_rows(back_shifted, sources)
    back_after = jnp.concatenate(pieces[1:] + [earlier(pieces[0], 1, source_at)], 0)
    back_short = back_shifted.astype(BF16)
    back_pair = jnp.concatenate([back_short, back_after.astype(BF16)], 1)
    back_key = dot_nn(back_pair, taps_back)

    gram = dot_tn(key_pair, back_short)
    gram = jnp.where(ahead, gram[LANE:], gram[:LANE])
    aligned = gram[:8]
    for first in range(8, LANE, 8):
        aligned = aligned + pltpu.roll(gram[first : first + 8], LANE - first, 1)
    for bit in (1, 2, 4):
        aligned = jnp.where((row_at[:8] & bit) > 0, pltpu.roll(aligned, LANE - bit, 1), aligned)
    filter_grad = jnp.sum(aligned, axis=0, keepdims=True)[:, : LANE - states]
    small_rows[pl.ds(channel, 1), :] = jnp.concatenate([filter_grad, start_grad], 1)
    for index, result in enumerate((response, back_value, back_key)):
        store_rows(out_rows, channel + index * group, sources, out_pad, result)


UNROLL = 4


def sequence_kernel(
    group, in_ref, rows_ref, cols_ref, taps_ref, skip_ref, out_ref, in_rows, out_rows, small_rows,
):
    sources, _, width = in_ref.shape
    parts = width // LANE
    spread(in_ref, in_rows, padded(3 * group))
    small_rows[...] = jnp.zeros_like(small_rows)
    at = iotas(sources)

    def step(index, carry):
        for inner in range(UNROLL):
            channel_body(
                index * UNROLL + inner, sources, parts, group, at, in_rows, out_rows, small_rows,
                rows_ref, cols_ref, taps_ref, skip_ref,
            )
        return carry

    lax.fori_loop(0, group // UNROLL, step, 0)
    out_pad = padded(2 * group) + padded(group)
    extra = out_ref.shape[1] - 3 * group

    def pack(source, carry):
        for part in range(parts):
            row = pl.multiple_of((part * sources + source) * out_pad, 8)
            columns = slice(LANE * part, LANE * (part + 1))
            out_ref[source, : 3 * group, columns] = out_rows[pl.ds(row, 3 * group), :].astype(
                BF16
            )
            out_ref[source, 3 * group :, columns] = small_rows[
                extra * part : extra * (part + 1)
            ].astype(BF16)
        return carry

    lax.fori_loop(0, sources, pack, 0)


def sequence_part(value, rows, cols, taps, skip):
    sources, triple, width = value.shape
    group = triple // 3
    parts = width // LANE
    lines = sources * parts
    extra = -(-group // parts)
    return pl.pallas_call(
        functools.partial(sequence_kernel, group),
        out_shape=jax.ShapeDtypeStruct((sources, triple + extra, width), BF16),
        in_specs=in_vmem(4) + in_smem(1),
        out_specs=in_vmem(1)[0],
        scratch_shapes=[
            pltpu.VMEM((lines * padded(triple), LANE), F32),
            pltpu.VMEM((lines * (padded(2 * group) + padded(group)), LANE), F32),
            pltpu.VMEM((padded(extra * parts), LANE), F32),
        ],
        compiler_params=params(24),
        cost_estimate=call_cost(22_000_000_000, 5_000_000),
    )(value, rows, cols, taps, skip)


def tiles_of(count, body):
    def step(tile, carry):
        body(tile)
        return carry

    lax.fori_loop(0, count, step, 0)


def columns_of(tile, width):
    return pl.ds(pl.multiple_of(tile * width, LANE), width)


def rows_of(tile, height):
    return pl.ds(pl.multiple_of(tile * height, 16), height)


def projected(shards_ref, ids_ref, weight_ref, total_ref):
    count, _, depth = shards_ref.shape
    total_ref[...] = jnp.zeros_like(total_ref)

    def add(tile):
        total_ref[...] += dot_nn(
            shards_ref[tile], weight_ref[rows_of(ids_ref[tile], depth), :]
        )

    tiles_of(count, add)


def key_value_kernel(
    group, shards_ref, key_ref, value_ref, ids_ref, kv_ref, total, across, packed,
):
    pad = padded(2 * group)
    owners = kv_ref.shape[0]
    for index, weight_ref in enumerate((key_ref, value_ref)):
        projected(shards_ref, ids_ref, weight_ref, total)
        across[...] = total[...].T
        for owner in range(owners):
            first = owner * pad + index * group
            packed[first : first + group] = across[owner * group : (owner + 1) * group]
    for owner in range(owners):
        kv_ref[owner] = packed[owner * pad : owner * pad + 2 * group].astype(BF16)


def key_value_part(shards, ids, w_key, w_value, owners):
    count, rows, depth = shards.shape
    channels = w_key.shape[1]
    group = channels // owners
    return pl.pallas_call(
        functools.partial(key_value_kernel, group),
        in_specs=in_vmem(3) + in_smem(1),
        out_specs=in_vmem(1)[0],
        out_shape=jax.ShapeDtypeStruct((owners, 2 * group, rows), BF16),
        scratch_shapes=[
            pltpu.VMEM((rows, channels), F32),
            pltpu.VMEM((channels, rows), F32),
            pltpu.VMEM((owners * padded(2 * group), rows), F32),
        ],
        compiler_params=params(24),
        cost_estimate=call_cost(4 * count * rows * depth * channels, 12_000_000),
    )(shards, w_key, w_value, ids)


def query_kernel(after_ref, shards_ref, weight_ref, ids_ref, query_ref, total):
    projected(shards_ref, ids_ref, weight_ref, total)
    query_ref[...] = total[...].astype(BF16)


def query_part(after, shards, ids, w_query):
    count, rows, depth = shards.shape
    channels = w_query.shape[1]
    return pl.pallas_call(
        query_kernel,
        in_specs=anywhere(1) + in_vmem(2) + in_smem(1),
        out_specs=in_vmem(1)[0],
        out_shape=jax.ShapeDtypeStruct((rows, channels), BF16),
        scratch_shapes=[pltpu.VMEM((rows, channels), F32)],
        compiler_params=params(14),
        cost_estimate=call_cost(2 * count * rows * depth * channels, 6_000_000),
    )(after, shards, w_query, ids)


def gated_grad_kernel(
    group, kv_ref, shards_ref, weight_ref, query_ref, ids_ref, gated_ref, grouped_ref, total, across,
):
    count, _, depth = shards_ref.shape
    total[...] = jnp.zeros_like(total)

    def add(tile):
        first = pl.multiple_of(ids_ref[tile] * depth, LANE)
        total[...] += dot_nt(shards_ref[tile], weight_ref[:, pl.ds(first, depth)])

    tiles_of(count, add)
    gated = total[...].astype(BF16)
    gated_ref[...] = gated
    across[...] = (gated.astype(F32) * query_ref[...].astype(F32)).T
    for owner in range(grouped_ref.shape[0]):
        grouped_ref[owner, : 2 * group] = kv_ref[owner]
        grouped_ref[owner, 2 * group :] = across[owner * group : (owner + 1) * group].astype(BF16)


def gated_grad_part(kv, shards, ids, w_out, query):
    count, rows, depth = shards.shape
    channels = w_out.shape[0]
    owners = kv.shape[0]
    group = channels // owners
    return pl.pallas_call(
        functools.partial(gated_grad_kernel, group),
        in_specs=in_vmem(4) + in_smem(1),
        out_specs=tuple(in_vmem(2)),
        out_shape=(
            jax.ShapeDtypeStruct((rows, channels), BF16),
            jax.ShapeDtypeStruct((owners, 3 * group, rows), BF16),
        ),
        scratch_shapes=[pltpu.VMEM((rows, channels), F32), pltpu.VMEM((channels, rows), F32)],
        compiler_params=params(18),
        cost_estimate=call_cost(2 * count * rows * depth * channels, 9_000_000),
    )(kv, shards, w_out, query, ids)


def unpack_kernel(
    group, returned_ref, query_ref, gated_ref, forward_ref, query_grad_ref, key_ref, value_ref,
    response_rows, value_rows, key_rows,
):
    for owner in range(returned_ref.shape[0]):
        piece = returned_ref[owner].astype(F32)
        at = slice(owner * group, (owner + 1) * group)
        response_rows[at] = piece[:group]
        value_rows[at] = piece[group : 2 * group]
        key_rows[at] = piece[2 * group : 3 * group]
    response = response_rows[...].T
    forward_ref[...] = (query_ref[...].astype(F32) * response).astype(BF16)
    query_grad_ref[...] = (gated_ref[...].astype(F32) * response).astype(BF16)
    value_ref[...] = value_rows[...].T.astype(BF16)
    key_ref[...] = key_rows[...].T.astype(BF16)


def unpack_part(returned, query, gated):
    rows, channels = query.shape
    return pl.pallas_call(
        functools.partial(unpack_kernel, channels // returned.shape[0]),
        in_specs=in_vmem(3),
        out_specs=tuple(in_vmem(4)),
        out_shape=(jax.ShapeDtypeStruct((rows, channels), BF16),) * 4,
        scratch_shapes=[pltpu.VMEM((channels, rows), F32)] * 3,
        compiler_params=params(12),
        cost_estimate=call_cost(4 * rows * channels, 5_000_000),
    )(returned, query, gated)


def turn_kernel(after_ref, first_ref, second_ref, first_out, second_out, first, second, sems):
    count = first.shape[0]

    def copy_out(index, tile):
        held, target = ((first, first_out), (second, second_out))[index]
        return pltpu.make_async_copy(held.at[tile], target.at[tile], sems.at[index, tile])

    def turn(tile):
        first[tile] = first_ref[tile].T
        copy_out(0, tile).start()
        second[tile] = second_ref[tile].T
        copy_out(1, tile).start()

    def finish(tile):
        copy_out(0, tile).wait()
        copy_out(1, tile).wait()

    tiles_of(count, turn)
    tiles_of(count, finish)


def turn_part(after, first, second):
    count, rows, depth = first.shape
    out = jax.ShapeDtypeStruct((count, depth, rows), BF16)
    return pl.pallas_call(
        turn_kernel,
        in_specs=anywhere(1) + in_vmem(2),
        out_specs=tuple(anywhere(2)),
        out_shape=(out, out),
        scratch_shapes=[pltpu.VMEM(out.shape, BF16)] * 2 + [pltpu.SemaphoreType.DMA((2, count))],
        compiler_params=params(16),
        cost_estimate=call_cost(2 * count * depth * rows, 8_000_000),
    )(after, first, second)


def weight_kernel(rows, unread, *refs):
    (
        wide_ref, narrow_ref, ids_ref, core_ref, keep_out, send_out, keep, send, keep_sems,
        send_sems,
    ) = refs[unread:]
    tiles, held = keep.shape[:2]

    def copies(tile):
        at = pl.ds(ids_ref[tile] * held, held)
        return (
            pltpu.make_async_copy(send.at[tile], send_out.at[at], send_sems.at[tile]),
            pltpu.make_async_copy(keep.at[tile], keep_out.at[at], keep_sems.at[tile]),
        )

    def multiply(tile):
        result = dot_nn(wide_ref[tile], narrow_ref[...]).astype(BF16)
        for core in range(2):

            @pl.when(core_ref[0] == core)
            def _():
                for chip in range(held):
                    at = (2 * chip + core) * rows
                    other = (2 * chip + 1 - core) * rows
                    keep[tile, chip] = result[at : at + rows]
                    send[tile, chip] = result[other : other + rows]

        for copy in copies(tile):
            copy.start()

    def finish(tile):
        for copy in copies(tile):
            copy.wait()

    tiles_of(tiles, multiply)
    tiles_of(tiles, finish)


def weight_partial(after, wide, ids, narrow, core, chips):
    tiles, height, depth = wide.shape
    width = narrow.shape[1]
    total = tiles * height
    rows = total // (2 * chips)
    halves = pltpu.VMEM((tiles, chips // tiles, rows, width), BF16)
    return pl.pallas_call(
        functools.partial(weight_kernel, rows, len(after)),
        in_specs=anywhere(len(after)) + in_vmem(2) + in_smem(2),
        out_specs=tuple(anywhere(2)),
        out_shape=(jax.ShapeDtypeStruct((chips, rows, width), BF16),) * 2,
        scratch_shapes=[halves, halves]
        + [pltpu.SemaphoreType.DMA((tiles,)), pltpu.SemaphoreType.DMA((tiles,))],
        compiler_params=params(16),
        cost_estimate=call_cost(2 * total * depth * width, 6_000_000),
    )(*after, wide, narrow, ids, core)


def mixed_kernel(after_ref, gated_ref, weight_ref, out_ref, result, sems):
    count, _, width = out_ref.shape

    def copy_out(tile):
        return pltpu.make_async_copy(result.at[tile], out_ref.at[tile], sems.at[tile])

    def multiply(tile):
        result[tile] = dot_nn(gated_ref[...], weight_ref[:, columns_of(tile, width)]).astype(BF16)
        copy_out(tile).start()

    tiles_of(count, multiply)
    tiles_of(count, lambda tile: copy_out(tile).wait())


def mixed_part(after, gated, w_out, count):
    rows, depth = gated.shape
    width = w_out.shape[1] // count
    return pl.pallas_call(
        mixed_kernel,
        in_specs=anywhere(1) + in_vmem(2),
        out_specs=anywhere(1)[0],
        out_shape=jax.ShapeDtypeStruct((count, rows, width), BF16),
        scratch_shapes=[
            pltpu.VMEM((count, rows, width), BF16), pltpu.SemaphoreType.DMA((count,)),
        ],
        compiler_params=params(14),
        cost_estimate=call_cost(2 * rows * depth * width * count, 6_000_000),
    )(after, gated, w_out)


def input_kernel(unread, *refs):
    *pairs, out_ref, result, sems = refs[unread:]
    half = len(pairs) // 2
    count, _, width = out_ref.shape

    def copy_out(tile):
        return pltpu.make_async_copy(result.at[tile], out_ref.at[tile], sems.at[tile])

    def multiply(tile):
        at = rows_of(tile, width)
        total = dot_nt(pairs[0][...], pairs[half][at, :])
        for index in range(1, half):
            total += dot_nt(pairs[index][...], pairs[half + index][at, :])
        result[tile] = total.astype(BF16)
        copy_out(tile).start()

    tiles_of(count, multiply)
    tiles_of(count, lambda tile: copy_out(tile).wait())


def input_part(after, backs, weights, count):
    rows, depth = backs[0].shape
    width = weights[0].shape[0] // count
    return pl.pallas_call(
        functools.partial(input_kernel, len(after)),
        in_specs=anywhere(len(after)) + in_vmem(len(backs) + len(weights)),
        out_specs=anywhere(1)[0],
        out_shape=jax.ShapeDtypeStruct((count, rows, width), BF16),
        scratch_shapes=[
            pltpu.VMEM((count, rows, width), BF16), pltpu.SemaphoreType.DMA((count,)),
        ],
        compiler_params=params(22),
        cost_estimate=call_cost(6 * rows * depth * width * count, 14_000_000),
    )(*after, *backs, *weights)


def moved(value, axis, steps):
    by_core = steps if isinstance(steps, tuple) else (steps, steps)
    pairs = []
    for x in range(SIDE):
        for y in range(SIDE):
            for core in range(2):
                for z in range(SIDE):
                    goal = [x, y, core, z]
                    if axis == "core":
                        goal[2] = 1 - core
                    else:
                        at = {"x": 0, "y": 1, "z": 3}[axis]
                        goal[at] = (goal[at] + by_core[core]) % SIDE
                    pairs.append(
                        tuple(
                            ((a * SIDE + b) * 2 + c) * SIDE + d
                            for a, b, c, d in ((x, y, core, z), goal)
                        )
                    )
    return lax.ppermute(value, ("seq", "tp"), pairs)


def added(left, right):
    return (left.astype(F32) + right.astype(F32)).astype(BF16)


def picked(value, axis=0):
    return lambda index: lax.dynamic_index_in_dim(value, index, axis, keepdims=False)


def ring_sum(travelling, block, place, up, axis, steps):
    for step in steps:
        travelling = added(moved(travelling, axis, (1, -1)), block((place - step * up) % SIDE))
    return travelling


class SeqSum:
    def __init__(self, halves, first, places, up):
        keep, send = halves
        _, rows, width = keep.shape
        grid = (SIDE, SIDE, rows, width)
        axis = "xy".index(first)
        self.first, self.second = first, "yx"[axis]
        self.places, self.up = places, up
        self.keep = picked(keep.reshape(grid), axis)
        self.came = picked(moved(send, "core", 1).reshape(grid), axis)
        self.start = self.block((places[first] - up) % SIDE)
        self.held = None

    def block(self, index):
        return added(self.keep(index), self.came(index))

    def ring(self, travelling, steps):
        return ring_sum(
            travelling, self.block, self.places[self.first], self.up, self.first, steps
        )

    def step(self):
        if self.held is None:
            self.held = self.ring(self.start, (2,))
        return self.held

    def total(self):
        half = self.ring(self.step(), range(3, SIDE + 1))
        place = self.places[self.second]
        block = picked(half)
        start = block((place - self.up) % SIDE)
        return ring_sum(start, block, place, self.up, self.second, range(2, SIDE + 1)).astype(F32)


def per_device(
    tokens,
    w_query,
    w_key,
    w_value,
    w_out,
    shift_filter,
    log_decay,
    readout,
    skip_gain,
    init_state,
    cotangent,
):
    row_count = tokens.shape[0]
    channels = w_query.shape[1]
    tap_count = shift_filter.shape[0]
    seq_count = lax.axis_size("seq")
    group = channels // seq_count
    position = lax.axis_index("seq")
    core = position % 2
    chip_z = lax.axis_index("tp")
    places = {"x": position // (2 * SIDE), "y": (position // 2) % SIDE}
    core_word = core.reshape(1)

    token_sides = moved(tokens, "z", 1), moved(tokens, "z", -1)
    grad_sides = moved(cotangent, "z", 1), moved(cotangent, "z", -1)

    def all_shards(mine, sides):
        below, above = sides
        far = moved(jnp.where(core == 0, below, above), "z", (1, -1))
        return jnp.stack([mine, below, above, far])

    shards = all_shards(tokens, token_sides)
    grad_shards = all_shards(cotangent, grad_sides)
    ids = (chip_z + jnp.array([0, SIDE - 1, 1, 2], jnp.int32)) % SIDE

    def own(value):
        return lax.dynamic_slice_in_dim(value, position * group, group, value.ndim - 1)

    own_rate, own_read, own_init, own_taps = (
        own(value).T for value in (log_decay, readout, init_state, shift_filter)
    )
    own_taps = jnp.pad(own_taps, ((0, 0), (0, LANE - tap_count)))
    taps = jnp.stack([own_taps, jnp.roll(own_taps[:, ::-1], 1, axis=1)])
    rows = jnp.stack([own_rate, own_init])
    cols = jnp.stack([own_rate, own_read])[..., None]
    skip = own(skip_gain)

    def exchanged(value):
        return lax.all_to_all(value, "seq", 0, 0, tiled=True)

    kv = key_value_part(shards, ids, w_key, w_value, seq_count)
    query = query_part(kv, shards, ids, w_query)
    gated_grad, packed = gated_grad_part(kv, grad_shards, ids, w_out, query)
    results = sequence_part(exchanged(packed), rows, cols, taps, skip)
    shards_turned, grad_turned = turn_part(results, shards, grad_shards)
    returned = exchanged(results)
    gated, back_query, back_key, back_value = unpack_part(returned, query, gated_grad)
    chips = SIDE * SIDE
    up = 1 - 2 * core

    def weight(after, wide, narrow):
        return weight_partial(after, wide, ids, narrow, core_word, chips)

    out_halves = weight((gated,), grad_turned, gated)
    out_sum = SeqSum(out_halves, "x", places, up)
    query_halves = weight((out_halves[1],), shards_turned, back_query)
    query_sum = SeqSum(query_halves, "y", places, up)
    partial_mixed = mixed_part(query_halves[1], gated, w_out, SIDE)
    mixed = lax.psum_scatter(partial_mixed, "tp", scatter_dimension=0, tiled=True)[0]
    key_halves = weight((partial_mixed,), shards_turned, back_key)
    key_sum = SeqSum(key_halves, "x", places, up)
    value_halves = weight((key_halves[1], out_sum.start), shards_turned, back_value)
    value_sum = SeqSum(value_halves, "y", places, up)
    out_first, query_first = out_sum.step(), query_sum.step()
    out_first, value_sum.start = lax.optimization_barrier((out_first, value_sum.start))
    out_sum.held = out_first
    partial_input = input_part(
        (value_halves[1], out_first, query_first, key_sum.start, value_sum.start),
        (back_query, back_key, back_value),
        (w_query, w_key, w_value),
        SIDE,
    )
    returned, query_sum.held, partial_input = lax.optimization_barrier(
        (returned, query_first, partial_input)
    )
    grad_input = lax.psum_scatter(partial_input, "tp", scatter_dimension=0, tiled=True)[0]
    small = returned[:, 3 * group :].reshape(seq_count, -1, row_count // LANE, LANE)
    small = small.transpose(0, 2, 1, 3).reshape(seq_count, -1, LANE)[:, :group]
    small = small.reshape(channels, LANE).T.astype(F32)
    grad_filter, grad_init = small[:tap_count], small[tap_count:]

    grad_out, grad_query, grad_key, grad_value = (
        each.total() for each in (out_sum, query_sum, key_sum, value_sum)
    )
    grad_out = grad_out.T
    return (mixed, grad_input, grad_query, grad_key, grad_value, grad_out, grad_filter, grad_init)


def solution(mesh):
    return jax.shard_map(
        per_device,
        mesh=mesh,
        in_specs=(
            P("seq", "tp"),
            P(None, "tp"),
            P(None, "tp"),
            P(None, "tp"),
            P("tp", None),
            P(None, "tp"),
            P(None, "tp"),
            P(None, "tp"),
            P("tp"),
            P(None, "tp"),
            P("seq", "tp"),
        ),
        out_specs=(
            P("seq", "tp"),
            P("seq", "tp"),
            P("seq", "tp"),
            P("seq", "tp"),
            P("seq", "tp"),
            P("tp", "seq"),
            P(None, "tp"),
            P(None, "tp"),
        ),
        check_vma=False,
    )
```

profile of v0, /device:TPU:0, one launch (start us, length us, event | category | flops | bytes accessed | tf_op | source)
XLA Modules:
  0.0 301.5 jit_solution(8122164557290953198)
XLA Ops:
  7.2 4.2 %collective-permute-start.1 = (bf16[384,640]{1,0:T(8,128)(2,1)}, bf16[384,640]{1,0:T(8,128)(2,1)S(1)}, u32[]{:S(2)}, u32[]{:S(2)}) collective-permute-start(bf16[384,640]{1,0:T(8,128)(2,1)} %param.12), channel_id=1, source_target_pairs={{0,3},{1,0},{2,1},{3,2},{4,7},{5,4},{6,5},{7,6},{8,11},{9,8},{10,9... | collective-permute-start | bytes 1474568 | tf_op jit(solution)/shard_map/ppermute | solution.py:617
  11.4 3.2 %collective-permute-start.4 = (bf16[384,640]{1,0:T(8,128)(2,1)}, bf16[384,640]{1,0:T(8,128)(2,1)S(1)}, u32[]{:S(2)}, u32[]{:S(2)}) collective-permute-start(bf16[384,640]{1,0:T(8,128)(2,1)} %param.22), channel_id=1, source_target_pairs={{0,3},{1,0},{2,1},{3,2},{4,7},{5,4},{6,5},{7,6},{8,11},{9,8},{10,9... | collective-permute-start | bytes 1474568 | tf_op jit(solution)/shard_map/ppermute | solution.py:617
  14.6 8.7 %collective-permute-done.1 = bf16[384,640]{1,0:T(8,128)(2,1)S(1)} collective-permute-done((bf16[384,640]{1,0:T(8,128)(2,1)}, bf16[384,640]{1,0:T(8,128)(2,1)S(1)}, u32[]{:S(2)}, u32[]{:S(2)}) %collective-permute-start.1) | collective-permute-done | bytes 491552 | tf_op jit(solution)/shard_map/ppermute | solution.py:617
  23.3 3.6 %collective-permute-done = bf16[384,640]{1,0:T(8,128)(2,1)S(1)} collective-permute-done((bf16[384,640]{1,0:T(8,128)(2,1)}, bf16[384,640]{1,0:T(8,128)(2,1)S(1)}, u32[]{:S(2)}, u32[]{:S(2)}) %collective-permute-start) | collective-permute-done | bytes 491552 | tf_op jit(solution)/shard_map/ppermute | solution.py:617
  27.8 6.0 %collective-permute-done.4 = bf16[384,640]{1,0:T(8,128)(2,1)S(1)} collective-permute-done((bf16[384,640]{1,0:T(8,128)(2,1)}, bf16[384,640]{1,0:T(8,128)(2,1)S(1)}, u32[]{:S(2)}, u32[]{:S(2)}) %collective-permute-start.4) | collective-permute-done | bytes 491552 | tf_op jit(solution)/shard_map/ppermute | solution.py:617
  33.8 2.2 collective-permute-done.3
  36.1 5.1 %collective-permute-done.2 = bf16[384,640]{1,0:T(8,128)(2,1)S(1)} collective-permute-done((bf16[384,640]{1,0:T(8,128)(2,1)S(1)}, bf16[384,640]{1,0:T(8,128)(2,1)S(1)}, u32[]{:S(2)}, u32[]{:S(2)}) %collective-permute-start.2) | collective-permute-done | bytes 491552 | tf_op jit(solution)/shard_map/ppermute | solution.py:617
  42.0 1.6 pad_maximum_fusion.shards_ref.first_ref
  44.3 1.9 copy-done.6
  46.2 6.2 %shard_map.179.after_ref.kv_ref = bf16[32,40,384]{2,1,0:T(8,128)(2,1)S(1)} custom-call(bf16[4,384,640]{2,1,0:T(8,128)(2,1)S(1)} %pad_maximum_fusion.shards_ref.first_ref, bf16[2560,640]{1,0:T(8,128)(2,1)S(1)} %copy-done.4, bf16[2560,640]{1,0:T(8,128)(2,1)S(1)} %copy-done.6, s32[4]{0:T(128)S(1)} %and_select_fusion.ids_ref.refs_3_.refs_4_), custom_call_target="tpu_custom_call" | custom-call | flops 2516582400 | bytes 12000000 | tf_op jit(solution)/shard_map/pallas_call | solution.py:340
  52.5 3.1 %shard_map.180.query_ref = bf16[384,640]{1,0:T(8,128)(2,1)S(1)} custom-call(bf16[32,40,384]{2,1,0:T(8,128)(2,1)S(1)} %shard_map.179.after_ref.kv_ref, bf16[4,384,640]{2,1,0:T(8,128)(2,1)S(1)} %pad_maximum_fusion.shards_ref.first_ref, bf16[2560,640]{1,0:T(8,128)(2,1)S(1)} %copy-done.8, s32[4]{0:T(128)S(1)} %and_select_fusion.ids_ref.refs_3_.refs_4_), custom_call_target="tpu_custom_call" | custom-call | flops 1258291200 | bytes 6000000 | tf_op jit(solution)/shard_map/pallas_call | solution.py:363
  55.9 1.6 copy-done.2
  57.5 3.5 %shard_map.181 = (bf16[384,640]{1,0:T(8,128)(2,1)S(1)}, bf16[32,60,384]{2,1,0:T(8,128)(2,1)S(1)}) custom-call(bf16[32,40,384]{2,1,0:T(8,128)(2,1)S(1)} %shard_map.179.after_ref.kv_ref, bf16[4,384,640]{2,1,0:T(8,128)(2,1)S(1)} %pad_maximum_fusion.1.shards_ref.second_ref, bf16[640,2560]{1,0:T(8,128)(2,1)S(1)} %copy-done.2, ...), custom_call_target="tpu_custom_call" | custom-call | flops 1258291200 | bytes 9000000 | tf_op jit(solution)/shard_map/pallas_call | solution.py:398
  62.2 7.4 %all-to-all-start = ((bf16[32,60,384]{2,1,0:T(8,128)(2,1)}), bf16[32,60,384]{2,1,0:T(8,128)(2,1)}, u32[]{:S(2)}, u32[]{:S(2)}) async-start(bf16[32,60,384]{2,1,0:T(8,128)(2,1)} %copy-done.18), calls=%async_computation | async-start | bytes 3145728 | tf_op jit(solution)/shard_map/all_to_all | solution.py:717
  72.8 1.5 copy.29.cols_ref
  74.5 18.3 %all-to-all-done.in_ref = bf16[32,60,384]{2,1,0:T(8,128)(2,1)} async-done(((bf16[32,60,384]{2,1,0:T(8,128)(2,1)}), bf16[32,60,384]{2,1,0:T(8,128)(2,1)}, u32[]{:S(2)}, u32[]{:S(2)}) %all-to-all-start) | async-done | bytes 1474592 | tf_op jit(solution)/shard_map/all_to_all | solution.py:717
  92.8 1.3 copy-done.19
  94.1 18.4 %shard_map.182.after_ref = bf16[32,67,384]{2,1,0:T(8,128)(2,1)S(1)} custom-call(bf16[32,60,384]{2,1,0:T(8,128)(2,1)} %all-to-all-done.in_ref, f32[2,20,64]{2,1,0:T(8,128)S(1)} %get-tuple-element.61.rows_ref, f32[2,20,64,1]{3,2,1,0:T(8,128)S(1)} %copy-done.19, f32[2,20,128]{2,1,0:T(8,128)S(1)} %pad_maximum_fusion.4.taps_ref, f32[20]{0:T(128)S(1)} %dynamic_slice.166.skip_ref), custom_call_target="tpu_custom_call" | custom-call | flops 22000001024 | bytes 5000000 | tf_op jit(solution)/shard_map/pallas_call | solution.py:278
  112.5 1.3 copy-done.10
  113.8 4.7 %all-to-all-start.1 = ((bf16[32,67,384]{2,1,0:T(8,128)(2,1)}), bf16[32,67,384]{2,1,0:T(8,128)(2,1)}, u32[]{:S(2)}, u32[]{:S(2)}) async-start(bf16[32,67,384]{2,1,0:T(8,128)(2,1)} %copy-done.10), calls=%async_computation.1 | async-start | bytes 3538944 | tf_op jit(solution)/shard_map/all_to_all | solution.py:717
  118.8 1.5 copy-done.1
  120.3 1.5 copy-done.11
  121.8 4.2 %shard_map.184 = (bf16[4,640,384]{2,1,0:T(8,128)(2,1)S(1)}, bf16[4,640,384]{2,1,0:T(8,128)(2,1)S(1)}) custom-call(bf16[32,67,384]{2,1,0:T(8,128)(2,1)S(1)} %copy-done.11, bf16[4,384,640]{2,1,0:T(8,128)(2,1)S(1)} %pad_maximum_fusion.shards_ref.first_ref, bf16[4,384,640]{2,1,0:T(8,128)(2,1)S(1)} %copy-done.1), custom_call_target="tpu_custom_call" | custom-call | flops 1966080 | bytes 8000000 | tf_op jit(solution)/shard_map/pallas_call | solution.py:466
  126.0 1.3 copy-done.28
  128.6 15.2 %all-to-all-done.1.returned_ref = bf16[32,67,384]{2,1,0:T(8,128)(2,1)} async-done(((bf16[32,67,384]{2,1,0:T(8,128)(2,1)}), bf16[32,67,384]{2,1,0:T(8,128)(2,1)}, u32[]{:S(2)}, u32[]{:S(2)}) %all-to-all-start.1) | async-done | bytes 1646624 | tf_op jit(solution)/shard_map/all_to_all | solution.py:717
  143.8 2.4 shard_map.183
  147.7 4.8 %shard_map.185 = (bf16[16,80,640]{2,1,0:T(8,128)(2,1)S(1)}, bf16[16,80,640]{2,1,0:T(8,128)(2,1)}) custom-call(bf16[384,640]{1,0:T(8,128)(2,1)S(1)} %get-tuple-element.31.refs_0_.refs_2_.gated_ref, bf16[4,640,384]{2,1,0:T(8,128)(2,1)S(1)} %copy-done.33, bf16[384,640]{1,0:T(8,128)(2,1)S(1)} %get-tuple-element.31.refs_0_.refs_2_.gated_ref, ...), custom_call_target="tpu_custom_call" | custom-call | flops 1258291200 | bytes 6000000 | tf_op jit(solution)/shard_map/pallas_call | solution.py:520
  153.8 5.1 %shard_map.186 = (bf16[16,80,640]{2,1,0:T(8,128)(2,1)S(1)}, bf16[16,80,640]{2,1,0:T(8,128)(2,1)S(1)}) custom-call(bf16[16,80,640]{2,1,0:T(8,128)(2,1)} %get-tuple-element.33.refs_0_, bf16[4,640,384]{2,1,0:T(8,128)(2,1)S(1)} %copy-done.29, bf16[384,640]{1,0:T(8,128)(2,1)S(1)} %get-tuple-element.35.refs_2_.refs_5_, ...), custom_call_target="tpu_custom_call" | custom-call | flops 1258291200 | bytes 6000000 | tf_op jit(solution)/shard_map/pallas_call | solution.py:520
  158.9 3.3 %shard_map.187.refs_0_ = bf16[4,384,640]{2,1,0:T(8,128)(2,1)} custom-call(bf16[16,80,640]{2,1,0:T(8,128)(2,1)S(1)} %get-tuple-element.36.after_ref, bf16[384,640]{1,0:T(8,128)(2,1)S(1)} %get-tuple-element.31.refs_0_.refs_2_.gated_ref, bf16[640,2560]{1,0:T(8,128)(2,1)S(1)} %copy-done.3), custom_call_target="tpu_custom_call" | custom-call | flops 1258291200 | bytes 6000000 | tf_op jit(solution)/shard_map/pallas_call | solution.py:549
  163.2 1.5 copy-done.30
  164.8 4.8 %shard_map.188 = (bf16[16,80,640]{2,1,0:T(8,128)(2,1)S(1)}, bf16[16,80,640]{2,1,0:T(8,128)(2,1)}) custom-call(bf16[4,384,640]{2,1,0:T(8,128)(2,1)} %shard_map.187.refs_0_, bf16[4,640,384]{2,1,0:T(8,128)(2,1)S(1)} %copy-done.30, bf16[384,640]{1,0:T(8,128)(2,1)S(1)} %copy-done.23, s32[4]{0:T(128)S(1)} %and_select_fusion.ids_ref.refs_3_.refs_4_, ...), custom_call_target="tpu_custom_call" | custom-call | flops 1258291200 | bytes 6000000 | tf_op jit(solution)/shard_map/pallas_call | solution.py:520
  171.3 3.3 %collective-permute-done.11 = bf16[16,80,640]{2,1,0:T(8,128)(2,1)} collective-permute-done((bf16[16,80,640]{2,1,0:T(8,128)(2,1)}, bf16[16,80,640]{2,1,0:T(8,128)(2,1)}, u32[]{:S(2)}, u32[]{:S(2)}) %collective-permute-start.11) | collective-permute-done | bytes 1638432 | tf_op jit(solution)/shard_map/ppermute | solution.py:617
  174.6 2.0 fusion.17.refs_3_
  177.3 8.8 %collective-permute-done.17 = bf16[4,80,640]{2,1,0:T(8,128)(2,1)} collective-permute-done((bf16[4,80,640]{2,1,0:T(8,128)(2,1)}, bf16[4,80,640]{2,1,0:T(8,128)(2,1)}, u32[]{:S(2)}, u32[]{:S(2)}) %collective-permute-start.17) | collective-permute-done | bytes 409632 | tf_op jit(solution)/shard_map/ppermute | solution.py:617
  186.1 2.2 fusion.7
  188.2 9.5 %collective-permute-done.18 = bf16[4,80,640]{2,1,0:T(8,128)(2,1)} collective-permute-done((bf16[4,80,640]{2,1,0:T(8,128)(2,1)}, bf16[4,80,640]{2,1,0:T(8,128)(2,1)}, u32[]{:S(2)}, u32[]{:S(2)}) %collective-permute-start.18) | collective-permute-done | bytes 409632 | tf_op jit(solution)/shard_map/ppermute | solution.py:617
  197.7 2.2 fusion.6
  202.2 1.6 copy-done.31
  203.8 5.1 %shard_map.189 = (bf16[16,80,640]{2,1,0:T(8,128)(2,1)S(1)}, bf16[16,80,640]{2,1,0:T(8,128)(2,1)S(1)}) custom-call(bf16[16,80,640]{2,1,0:T(8,128)(2,1)} %get-tuple-element.39.refs_0_, bf16[4,80,640]{2,1,0:T(8,128)(2,1)S(1)} %fusion.14.refs_1_, bf16[4,640,384]{2,1,0:T(8,128)(2,1)S(1)} %copy-done.31, bf16[384,640]{1,0:T(8,128)(2,1)S(1)} %copy-done.26, ...), custom_call_target="tpu_custom_call" | custom-call | flops 1258291200 | bytes 6000000 | tf_op jit(solution)/shard_map/pallas_call | solution.py:520
  209.4 1.6 fusion.5
  211.1 1.3 fusion.12
  213.4 3.5 %collective-permute-done.20 = bf16[80,640]{1,0:T(8,128)(2,1)S(1)} collective-permute-done((bf16[80,640]{1,0:T(8,128)(2,1)S(1)}, bf16[80,640]{1,0:T(8,128)(2,1)S(1)}, u32[]{:S(2)}, u32[]{:S(2)}) %collective-permute-start.20) | collective-permute-done | bytes 102432 | tf_op jit(solution)/shard_map/ppermute | solution.py:617
  217.0 2.0 fusion.10.refs_1_
  219.1 3.8 %collective-permute-done.21 = bf16[80,640]{1,0:T(8,128)(2,1)S(1)} collective-permute-done((bf16[80,640]{1,0:T(8,128)(2,1)S(1)}, bf16[80,640]{1,0:T(8,128)(2,1)S(1)}, u32[]{:S(2)}, u32[]{:S(2)}) %collective-permute-start.21) | collective-permute-done | bytes 102432 | tf_op jit(solution)/shard_map/ppermute | solution.py:617
  223.0 1.3 fusion.11.refs_2_
  224.4 4.5 %collective-permute-done.22 = bf16[80,640]{1,0:T(8,128)(2,1)S(1)} collective-permute-done((bf16[80,640]{1,0:T(8,128)(2,1)S(1)}, bf16[80,640]{1,0:T(8,128)(2,1)S(1)}, u32[]{:S(2)}, u32[]{:S(2)}) %collective-permute-start.22) | collective-permute-done | bytes 102432 | tf_op jit(solution)/shard_map/ppermute | solution.py:617
  232.0 6.8 %shard_map.190 = bf16[4,384,640]{2,1,0:T(8,128)(2,1)} custom-call(bf16[16,80,640]{2,1,0:T(8,128)(2,1)S(1)} %get-tuple-element.42.refs_0_, bf16[4,80,640]{2,1,0:T(8,128)(2,1)} %fusion.10.refs_1_, bf16[4,80,640]{2,1,0:T(8,128)(2,1)S(1)} %fusion.11.refs_2_, bf16[4,80,640]{2,1,0:T(8,128)(2,1)} %fusion.17.refs_3_, bf16[4,80,640]{2,1,0:T(8,128)(2,1)} %fusion.16.refs_4_, ...), custom_call_target="tpu_custom_call" | custom-call | flops 3774873600 | bytes 14000000 | tf_op jit(solution)/shard_map/pallas_call | solution.py:585
  241.2 1.9 copy.50
  243.1 1.8 copy.49
  245.0 1.4 fusion.1
  246.4 3.7 %collective-permute-start.30 = (bf16[4,80,640]{2,1,0:T(8,128)(2,1)S(1)}, bf16[4,80,640]{2,1,0:T(8,128)(2,1)S(1)}, u32[]{:S(2)}, u32[]{:S(2)}) collective-permute-start(bf16[4,80,640]{2,1,0:T(8,128)(2,1)S(1)} %fusion.1), channel_id=1, source_target_pairs={{0,32},{1,33},{2,34},{3,35},{4,100},{5,101},{6,102},{7,103},{8,40}... | collective-permute-start | bytes 1228808 | tf_op jit(solution)/shard_map/ppermute | solution.py:617
  250.1 1.3 fusion.4
  251.4 2.0 collective-permute-start.24
  254.4 1.4 fusion.9
  255.8 1.7 collective-permute-start.13
  258.8 1.8 collective-permute-done.24
  261.8 3.3 %collective-permute-done.13 = bf16[4,80,640]{2,1,0:T(8,128)(2,1)S(1)} collective-permute-done((bf16[4,80,640]{2,1,0:T(8,128)(2,1)S(1)}, bf16[4,80,640]{2,1,0:T(8,128)(2,1)S(1)}, u32[]{:S(2)}, u32[]{:S(2)}) %collective-permute-start.13) | collective-permute-done | bytes 409632 | tf_op jit(solution)/shard_map/ppermute | solution.py:617
  266.2 3.6 %collective-permute-start.14 = (bf16[80,640]{1,0:T(8,128)(2,1)S(1)}, bf16[80,640]{1,0:T(8,128)(2,1)S(1)}, u32[]{:S(2)}, u32[]{:S(2)}) collective-permute-start(bf16[80,640]{1,0:T(8,128)(2,1)S(1)} %dynamic-slice_bitcast_fusion.3), channel_id=1, source_target_pairs={{0,32},{1,33},{2,34},{3,35},{4,100},{5,101},{6,102},{7,103},{8,40}... | collective-permute-start | bytes 307208 | tf_op jit(solution)/shard_map/ppermute | solution.py:617
  269.9 2.3 collective-permute-done.14
  272.2 2.3 collective-permute-start.15
  276.2 2.0 collective-permute-done.15
  279.3 2.7 collective-permute-done.26
  282.8 5.1 %collective-permute-done.27 = bf16[80,640]{1,0:T(8,128)(2,1)S(1)} collective-permute-done((bf16[80,640]{1,0:T(8,128)(2,1)S(1)}, bf16[80,640]{1,0:T(8,128)(2,1)S(1)}, u32[]{:S(2)}, u32[]{:S(2)}) %collective-permute-start.27) | collective-permute-done | bytes 102432 | tf_op jit(solution)/shard_map/ppermute | solution.py:617
  288.8 5.1 %collective-permute-done.28 = bf16[80,640]{1,0:T(8,128)(2,1)S(1)} collective-permute-done((bf16[80,640]{1,0:T(8,128)(2,1)S(1)}, bf16[80,640]{1,0:T(8,128)(2,1)S(1)}, u32[]{:S(2)}, u32[]{:S(2)}) %collective-permute-start.28) | collective-permute-done | bytes 102432 | tf_op jit(solution)/shard_map/ppermute | solution.py:617
  (171 shorter events, 34.1 us)
Async XLA Ops:
  7.2 16.1 %collective-permute-start.1 = (bf16[384,640]{1,0:T(8,128)(2,1)}, bf16[384,640]{1,0:T(8,128)(2,1)S(1)}, u32[]{:S(2)}, u32[]{:S(2)}) collective-permute-start(bf16[384,640]{1,0:T(8,128)(2,1)} %param.12), channel_id=1, source_target_pairs={{0,3},{1,0},{2,1},{3,2},{4,7},{5,4},{6,5},{7,6},{8,11},{9,8},{10,9... | collective-permute-start | bytes 1474568 | tf_op jit(solution)/shard_map/ppermute | solution.py:617
  11.4 15.6 %collective-permute-start = (bf16[384,640]{1,0:T(8,128)(2,1)}, bf16[384,640]{1,0:T(8,128)(2,1)S(1)}, u32[]{:S(2)}, u32[]{:S(2)}) collective-permute-start(bf16[384,640]{1,0:T(8,128)(2,1)} %param.12), channel_id=1, source_target_pairs={{0,1},{1,2},{2,3},{3,0},{4,5},{5,6},{6,7},{7,4},{8,9},{9,10},{10,1... | collective-permute-start | bytes 1474568 | tf_op jit(solution)/shard_map/ppermute | solution.py:617
  11.4 22.5 %collective-permute-start.4 = (bf16[384,640]{1,0:T(8,128)(2,1)}, bf16[384,640]{1,0:T(8,128)(2,1)S(1)}, u32[]{:S(2)}, u32[]{:S(2)}) collective-permute-start(bf16[384,640]{1,0:T(8,128)(2,1)} %param.22), channel_id=1, source_target_pairs={{0,3},{1,0},{2,1},{3,2},{4,7},{5,4},{6,5},{7,6},{8,11},{9,8},{10,9... | collective-permute-start | bytes 1474568 | tf_op jit(solution)/shard_map/ppermute | solution.py:617
  14.6 21.4 %collective-permute-start.3 = (bf16[384,640]{1,0:T(8,128)(2,1)}, bf16[384,640]{1,0:T(8,128)(2,1)S(1)}, u32[]{:S(2)}, u32[]{:S(2)}) collective-permute-start(bf16[384,640]{1,0:T(8,128)(2,1)} %param.22), channel_id=1, source_target_pairs={{0,1},{1,2},{2,3},{3,0},{4,5},{5,6},{6,7},{7,4},{8,9},{9,10},{10,1... | collective-permute-start | bytes 1474568 | tf_op jit(solution)/shard_map/ppermute | solution.py:617
  26.9 14.3 %copy-start.36 = (bf16[384,640]{1,0:T(8,128)(2,1)}, bf16[384,640]{1,0:T(8,128)(2,1)S(1)}, u32[]{:S(2)}) copy-start(bf16[384,640]{1,0:T(8,128)(2,1)S(1)} %collective-permute-done) | copy-start | bytes 1474564
  27.0 14.3 %collective-permute-start.2 = (bf16[384,640]{1,0:T(8,128)(2,1)S(1)}, bf16[384,640]{1,0:T(8,128)(2,1)S(1)}, u32[]{:S(2)}, u32[]{:S(2)}) collective-permute-start(bf16[384,640]{1,0:T(8,128)(2,1)S(1)} %broadcast_select_fusion.1), channel_id=1, source_target_pairs={{0,1},{1,2},{2,3},{3,0},{4,7},{5,4},{6,5},{7,6},{8,9},{9,10},{10,1... | collective-permute-start | bytes 1474568 | tf_op jit(solution)/shard_map/ppermute | solution.py:617
  27.1 15.0 %copy-start.39 = (bf16[384,640]{1,0:T(8,128)(2,1)S(1)}, bf16[384,640]{1,0:T(8,128)(2,1)}, u32[]{:S(2)}) copy-start(bf16[384,640]{1,0:T(8,128)(2,1)} %param.12) | copy-start | bytes 1474564
  36.0 5.3 %copy-start.34 = (bf16[384,640]{1,0:T(8,128)(2,1)}, bf16[384,640]{1,0:T(8,128)(2,1)S(1)}, u32[]{:S(2)}) copy-start(bf16[384,640]{1,0:T(8,128)(2,1)S(1)} %collective-permute-done.3) | copy-start | bytes 1474564
  36.1 19.5 %collective-permute-start.5 = (bf16[384,640]{1,0:T(8,128)(2,1)S(1)}, bf16[384,640]{1,0:T(8,128)(2,1)S(1)}, u32[]{:S(2)}, u32[]{:S(2)}) collective-permute-start(bf16[384,640]{1,0:T(8,128)(2,1)S(1)} %broadcast_select_fusion), channel_id=1, source_target_pairs={{0,1},{1,2},{2,3},{3,0},{4,7},{5,4},{6,5},{7,6},{8,9},{9,10},{10,1... | collective-permute-start | bytes 1474568 | tf_op jit(solution)/shard_map/ppermute | solution.py:617
  42.0 2.2 copy-start.4
  44.3 1.9 copy-start.6
  46.2 6.2 %copy-start.8 = (bf16[2560,640]{1,0:T(8,128)(2,1)S(1)}, bf16[2560,640]{1,0:T(8,128)(2,1)}, u32[]{:S(2)}) copy-start(bf16[2560,640]{1,0:T(8,128)(2,1)} %refs_8_.1) | copy-start | bytes 9830404
  52.4 3.1 %copy-start.35 = (bf16[384,640]{1,0:T(8,128)(2,1)S(1)}, bf16[384,640]{1,0:T(8,128)(2,1)}, u32[]{:S(2)}) copy-start(bf16[384,640]{1,0:T(8,128)(2,1)} %copy-done.34) | copy-start | bytes 1474564
  52.4 3.1 %copy-start.40 = (bf16[384,640]{1,0:T(8,128)(2,1)S(1)}, bf16[384,640]{1,0:T(8,128)(2,1)}, u32[]{:S(2)}) copy-start(bf16[384,640]{1,0:T(8,128)(2,1)} %param.22) | copy-start | bytes 1474564
  55.6 1.9 copy-start.2
  57.5 3.5 %copy-start = (bf16[4,384,640]{2,1,0:T(8,128)(2,1)}, bf16[4,384,640]{2,1,0:T(8,128)(2,1)S(1)}, u32[]{:S(2)}) copy-start(bf16[4,384,640]{2,1,0:T(8,128)(2,1)S(1)} %pad_maximum_fusion.1.shards_ref.second_ref) | copy-start | bytes 5898244
  62.2 30.6 %all-to-all-start = ((bf16[32,60,384]{2,1,0:T(8,128)(2,1)}), bf16[32,60,384]{2,1,0:T(8,128)(2,1)}, u32[]{:S(2)}, u32[]{:S(2)}) async-start(bf16[32,60,384]{2,1,0:T(8,128)(2,1)} %copy-done.18), calls=%async_computation | async-start | bytes 3145728 | tf_op jit(solution)/shard_map/all_to_all | solution.py:717
  113.8 30.0 %all-to-all-start.1 = ((bf16[32,67,384]{2,1,0:T(8,128)(2,1)}), bf16[32,67,384]{2,1,0:T(8,128)(2,1)}, u32[]{:S(2)}, u32[]{:S(2)}) async-start(bf16[32,67,384]{2,1,0:T(8,128)(2,1)} %copy-done.10), calls=%async_computation.1 | async-start | bytes 3538944 | tf_op jit(solution)/shard_map/all_to_all | solution.py:717
  118.5 176.1 %reduce-scatter.3.cloned.1.call-start = ((), (), s32[]{:S(2)}) async-start(), calls=%async_computation.4 | async-start | bytes 2457600 | tf_op jit(solution)/shard_map/reduce_scatter | solution.py:737
  143.8 4.0 %copy-start.33 = (bf16[4,640,384]{2,1,0:T(8,128)(2,1)S(1)}, bf16[4,640,384]{2,1,0:T(8,128)(2,1)}, u32[]{:S(2)}) copy-start(bf16[4,640,384]{2,1,0:T(8,128)(2,1)} %copy-done.32) | copy-start | bytes 5898244
  147.7 6.0 %copy-start.20 = (bf16[384,640]{1,0:T(8,128)(2,1)}, bf16[384,640]{1,0:T(8,128)(2,1)S(1)}, u32[]{:S(2)}) copy-start(bf16[384,640]{1,0:T(8,128)(2,1)S(1)} %get-tuple-element.35.refs_2_.refs_5_) | copy-start | bytes 1474564
  147.7 6.0 %copy-start.29 = (bf16[4,640,384]{2,1,0:T(8,128)(2,1)S(1)}, bf16[4,640,384]{2,1,0:T(8,128)(2,1)}, u32[]{:S(2)}) copy-start(bf16[4,640,384]{2,1,0:T(8,128)(2,1)} %copy-done.28) | copy-start | bytes 5898244
  153.8 5.1 %copy-start.3 = (bf16[640,2560]{1,0:T(8,128)(2,1)S(1)}, bf16[640,2560]{1,0:T(8,128)(2,1)}, u32[]{:S(2)}) copy-start(bf16[640,2560]{1,0:T(8,128)(2,1)} %weight_ref.5) | copy-start | bytes 9830404
  170.8 3.8 %collective-permute-start.11 = (bf16[16,80,640]{2,1,0:T(8,128)(2,1)}, bf16[16,80,640]{2,1,0:T(8,128)(2,1)}, u32[]{:S(2)}, u32[]{:S(2)}) collective-permute-start(bf16[16,80,640]{2,1,0:T(8,128)(2,1)} %get-tuple-element.39.refs_0_), channel_id=1, source_target_pairs={{0,4},{1,5},{2,6},{3,7},{4,0},{5,1},{6,2},{7,3},{8,12},{9,13},{10,... | collective-permute-start | bytes 4915208 | tf_op jit(solution)/shard_map/ppermute | solution.py:617
  170.8 29.1 %collective-permute-start.8 = (bf16[16,80,640]{2,1,0:T(8,128)(2,1)}, bf16[16,80,640]{2,1,0:T(8,128)(2,1)}, u32[]{:S(2)}, u32[]{:S(2)}) collective-permute-start(bf16[16,80,640]{2,1,0:T(8,128)(2,1)} %get-tuple-element.33.refs_0_), channel_id=1, source_target_pairs={{0,4},{1,5},{2,6},{3,7},{4,0},{5,1},{6,2},{7,3},{8,12},{9,13},{10,... | collective-permute-start | bytes 4915208 | tf_op jit(solution)/shard_map/ppermute | solution.py:617
  176.6 9.5 %collective-permute-start.17 = (bf16[4,80,640]{2,1,0:T(8,128)(2,1)}, bf16[4,80,640]{2,1,0:T(8,128)(2,1)}, u32[]{:S(2)}, u32[]{:S(2)}) collective-permute-start(bf16[4,80,640]{2,1,0:T(8,128)(2,1)} %fusion.17.refs_3_), channel_id=1, source_target_pairs={{0,32},{1,33},{2,34},{3,35},{4,100},{5,101},{6,102},{7,103},{8,40}... | collective-permute-start | bytes 1228808 | tf_op jit(solution)/shard_map/ppermute | solution.py:617
  176.6 118.0 %reduce-scatter.5.cloned.1.call-start = ((), (), s32[]{:S(2)}) async-start(), calls=%async_computation.5 | async-start | bytes 2457600 | tf_op jit(solution)/shard_map/reduce_scatter | solution.py:754
  176.7 34.4 %collective-permute-start.6 = (bf16[16,80,640]{2,1,0:T(8,128)(2,1)S(1)}, bf16[16,80,640]{2,1,0:T(8,128)(2,1)}, u32[]{:S(2)}, u32[]{:S(2)}) collective-permute-start(bf16[16,80,640]{2,1,0:T(8,128)(2,1)S(1)} %get-tuple-element.36.after_ref), channel_id=1, source_target_pairs={{0,4},{1,5},{2,6},{3,7},{4,0},{5,1},{6,2},{7,3},{8,12},{9,13},{10,... | collective-permute-start | bytes 4915208 | tf_op jit(solution)/shard_map/ppermute | solution.py:617
  188.2 9.5 %collective-permute-start.18 = (bf16[4,80,640]{2,1,0:T(8,128)(2,1)}, bf16[4,80,640]{2,1,0:T(8,128)(2,1)}, u32[]{:S(2)}, u32[]{:S(2)}) collective-permute-start(bf16[4,80,640]{2,1,0:T(8,128)(2,1)} %fusion.7), channel_id=1, source_target_pairs={{0,32},{1,33},{2,34},{3,35},{4,100},{5,101},{6,102},{7,103},{8,40}... | collective-permute-start | bytes 1228808 | tf_op jit(solution)/shard_map/ppermute | solution.py:617
  199.9 9.5 %collective-permute-start.19 = (bf16[4,80,640]{2,1,0:T(8,128)(2,1)}, bf16[4,80,640]{2,1,0:T(8,128)(2,1)}, u32[]{:S(2)}, u32[]{:S(2)}) collective-permute-start(bf16[4,80,640]{2,1,0:T(8,128)(2,1)} %fusion.6), channel_id=1, source_target_pairs={{0,32},{1,33},{2,34},{3,35},{4,100},{5,101},{6,102},{7,103},{8,40}... | collective-permute-start | bytes 1228808 | tf_op jit(solution)/shard_map/ppermute | solution.py:617
  201.1 15.9 %collective-permute-start.9 = (bf16[4,80,640]{2,1,0:T(8,128)(2,1)S(1)}, bf16[4,80,640]{2,1,0:T(8,128)(2,1)S(1)}, u32[]{:S(2)}, u32[]{:S(2)}) collective-permute-start(bf16[4,80,640]{2,1,0:T(8,128)(2,1)S(1)} %fusion.14.refs_1_), channel_id=1, source_target_pairs={{0,32},{1,33},{2,34},{3,35},{4,100},{5,101},{6,102},{7,103},{8,40}... | collective-permute-start | bytes 1228808 | tf_op jit(solution)/shard_map/ppermute | solution.py:617
  202.2 1.6 copy-start.31
  203.8 28.1 %copy-start.9 = (bf16[2560,640]{1,0:T(8,128)(2,1)S(1)}, bf16[2560,640]{1,0:T(8,128)(2,1)}, u32[]{:S(2)}) copy-start(bf16[2560,640]{1,0:T(8,128)(2,1)} %refs_8_.1) | copy-start | bytes 9830404
  208.9 20.6 %copy-start.15 = (bf16[16,80,640]{2,1,0:T(8,128)(2,1)}, bf16[16,80,640]{2,1,0:T(8,128)(2,1)S(1)}, u32[]{:S(2)}) copy-start(bf16[16,80,640]{2,1,0:T(8,128)(2,1)S(1)} %get-tuple-element.43) | copy-start | bytes 4915204
  209.0 20.6 %collective-permute-start.10 = (bf16[16,80,640]{2,1,0:T(8,128)(2,1)S(1)}, bf16[16,80,640]{2,1,0:T(8,128)(2,1)S(1)}, u32[]{:S(2)}, u32[]{:S(2)}) collective-permute-start(bf16[16,80,640]{2,1,0:T(8,128)(2,1)S(1)} %get-tuple-element.42.refs_0_), channel_id=1, source_target_pairs={{0,4},{1,5},{2,6},{3,7},{4,0},{5,1},{6,2},{7,3},{8,12},{9,13},{10,... | collective-permute-start | bytes 4915208 | tf_op jit(solution)/shard_map/ppermute | solution.py:617
  209.4 22.6 %copy-start.21 = (bf16[384,640]{1,0:T(8,128)(2,1)S(1)}, bf16[384,640]{1,0:T(8,128)(2,1)}, u32[]{:S(2)}) copy-start(bf16[384,640]{1,0:T(8,128)(2,1)} %copy-done.20) | copy-start | bytes 1474564
  209.4 22.6 %copy-start.24 = (bf16[384,640]{1,0:T(8,128)(2,1)S(1)}, bf16[384,640]{1,0:T(8,128)(2,1)}, u32[]{:S(2)}) copy-start(bf16[384,640]{1,0:T(8,128)(2,1)} %copy-done.22) | copy-start | bytes 1474564
  209.4 22.6 %copy-start.27 = (bf16[384,640]{1,0:T(8,128)(2,1)S(1)}, bf16[384,640]{1,0:T(8,128)(2,1)}, u32[]{:S(2)}) copy-start(bf16[384,640]{1,0:T(8,128)(2,1)} %copy-done.25) | copy-start | bytes 1474564
  211.0 5.9 %collective-permute-start.20 = (bf16[80,640]{1,0:T(8,128)(2,1)S(1)}, bf16[80,640]{1,0:T(8,128)(2,1)S(1)}, u32[]{:S(2)}, u32[]{:S(2)}) collective-permute-start(bf16[80,640]{1,0:T(8,128)(2,1)S(1)} %dynamic-slice_bitcast_fusion.2), channel_id=1, source_target_pairs={{0,8},{1,9},{2,10},{3,11},{4,28},{5,29},{6,30},{7,31},{8,16},{9,17... | collective-permute-start | bytes 307208 | tf_op jit(solution)/shard_map/ppermute | solution.py:617
  211.1 20.9 %copy-start.7 = (bf16[2560,640]{1,0:T(8,128)(2,1)S(1)}, bf16[2560,640]{1,0:T(8,128)(2,1)}, u32[]{:S(2)}) copy-start(bf16[2560,640]{1,0:T(8,128)(2,1)} %refs_10_.1) | copy-start | bytes 9830404
  212.4 10.7 %collective-permute-start.7 = (bf16[4,80,640]{2,1,0:T(8,128)(2,1)S(1)}, bf16[4,80,640]{2,1,0:T(8,128)(2,1)S(1)}, u32[]{:S(2)}, u32[]{:S(2)}) collective-permute-start(bf16[4,80,640]{2,1,0:T(8,128)(2,1)S(1)} %fusion.12), channel_id=1, source_target_pairs={{0,8},{1,9},{2,10},{3,11},{4,28},{5,29},{6,30},{7,31},{8,16},{9,17... | collective-permute-start | bytes 1228808 | tf_op jit(solution)/shard_map/ppermute | solution.py:617
  216.9 5.9 %collective-permute-start.21 = (bf16[80,640]{1,0:T(8,128)(2,1)S(1)}, bf16[80,640]{1,0:T(8,128)(2,1)S(1)}, u32[]{:S(2)}, u32[]{:S(2)}) collective-permute-start(bf16[80,640]{1,0:T(8,128)(2,1)S(1)} %fusion.36), channel_id=1, source_target_pairs={{0,8},{1,9},{2,10},{3,11},{4,28},{5,29},{6,30},{7,31},{8,16},{9,17... | collective-permute-start | bytes 307208 | tf_op jit(solution)/shard_map/ppermute | solution.py:617
  222.9 9.1 %copy-start.5 = (bf16[2560,640]{1,0:T(8,128)(2,1)S(1)}, bf16[2560,640]{1,0:T(8,128)(2,1)}, u32[]{:S(2)}) copy-start(bf16[2560,640]{1,0:T(8,128)(2,1)} %refs_9_.1) | copy-start | bytes 9830404
  222.9 5.9 %collective-permute-start.22 = (bf16[80,640]{1,0:T(8,128)(2,1)S(1)}, bf16[80,640]{1,0:T(8,128)(2,1)S(1)}, u32[]{:S(2)}, u32[]{:S(2)}) collective-permute-start(bf16[80,640]{1,0:T(8,128)(2,1)S(1)} %fusion.35), channel_id=1, source_target_pairs={{0,8},{1,9},{2,10},{3,11},{4,28},{5,29},{6,30},{7,31},{8,16},{9,17... | collective-permute-start | bytes 307208 | tf_op jit(solution)/shard_map/ppermute | solution.py:617
  224.4 7.6 %copy-start.17 = (bf16[4,80,640]{2,1,0:T(8,128)(2,1)}, bf16[4,80,640]{2,1,0:T(8,128)(2,1)S(1)}, u32[]{:S(2)}) copy-start(bf16[4,80,640]{2,1,0:T(8,128)(2,1)S(1)} %fusion.11.refs_2_) | copy-start | bytes 1228804
  230.9 14.1 %collective-permute-start.29 = (bf16[4,80,640]{2,1,0:T(8,128)(2,1)}, bf16[4,80,640]{2,1,0:T(8,128)(2,1)}, u32[]{:S(2)}, u32[]{:S(2)}) collective-permute-start(bf16[4,80,640]{2,1,0:T(8,128)(2,1)} %fusion.10.refs_1_), channel_id=1, source_target_pairs={{0,32},{1,33},{2,34},{3,35},{4,100},{5,101},{6,102},{7,103},{8,40}... | collective-permute-start | bytes 1228808 | tf_op jit(solution)/shard_map/ppermute | solution.py:617
  231.9 18.1 %collective-permute-start.23 = (bf16[4,80,640]{2,1,0:T(8,128)(2,1)}, bf16[4,80,640]{2,1,0:T(8,128)(2,1)}, u32[]{:S(2)}, u32[]{:S(2)}) collective-permute-start(bf16[4,80,640]{2,1,0:T(8,128)(2,1)} %fusion.16.refs_4_), channel_id=1, source_target_pairs={{0,8},{1,9},{2,10},{3,11},{4,28},{5,29},{6,30},{7,31},{8,16},{9,17... | collective-permute-start | bytes 1228808 | tf_op jit(solution)/shard_map/ppermute | solution.py:617
  241.2 3.8 %copy-start.13 = (bf16[16,80,640]{2,1,0:T(8,128)(2,1)S(1)}, bf16[16,80,640]{2,1,0:T(8,128)(2,1)}, u32[]{:S(2)}) copy-start(bf16[16,80,640]{2,1,0:T(8,128)(2,1)} %copy-done.12) | copy-start | bytes 4915204
  244.9 9.5 %collective-permute-start.12 = (bf16[4,80,640]{2,1,0:T(8,128)(2,1)}, bf16[4,80,640]{2,1,0:T(8,128)(2,1)}, u32[]{:S(2)}, u32[]{:S(2)}) collective-permute-start(bf16[4,80,640]{2,1,0:T(8,128)(2,1)} %copy-done.17), channel_id=1, source_target_pairs={{0,8},{1,9},{2,10},{3,11},{4,28},{5,29},{6,30},{7,31},{8,16},{9,17... | collective-permute-start | bytes 1228808 | tf_op jit(solution)/shard_map/ppermute | solution.py:617
  244.9 5.1 %copy-start.16 = (bf16[16,80,640]{2,1,0:T(8,128)(2,1)S(1)}, bf16[16,80,640]{2,1,0:T(8,128)(2,1)}, u32[]{:S(2)}) copy-start(bf16[16,80,640]{2,1,0:T(8,128)(2,1)} %copy-done.15) | copy-start | bytes 4915204
  246.4 11.2 %collective-permute-start.30 = (bf16[4,80,640]{2,1,0:T(8,128)(2,1)S(1)}, bf16[4,80,640]{2,1,0:T(8,128)(2,1)S(1)}, u32[]{:S(2)}, u32[]{:S(2)}) collective-permute-start(bf16[4,80,640]{2,1,0:T(8,128)(2,1)S(1)} %fusion.1), channel_id=1, source_target_pairs={{0,32},{1,33},{2,34},{3,35},{4,100},{5,101},{6,102},{7,103},{8,40}... | collective-permute-start | bytes 1228808 | tf_op jit(solution)/shard_map/ppermute | solution.py:617
  251.4 9.2 %copy-start.38 = (bf16[16,80,640]{2,1,0:T(8,128)(2,1)S(1)}, bf16[16,80,640]{2,1,0:T(8,128)(2,1)}, u32[]{:S(2)}) copy-start(bf16[16,80,640]{2,1,0:T(8,128)(2,1)} %copy-done.37) | copy-start | bytes 4915204
  251.4 9.2 %collective-permute-start.24 = (bf16[4,80,640]{2,1,0:T(8,128)(2,1)S(1)}, bf16[4,80,640]{2,1,0:T(8,128)(2,1)S(1)}, u32[]{:S(2)}, u32[]{:S(2)}) collective-permute-start(bf16[4,80,640]{2,1,0:T(8,128)(2,1)S(1)} %fusion.4), channel_id=1, source_target_pairs={{0,8},{1,9},{2,10},{3,11},{4,28},{5,29},{6,30},{7,31},{8,16},{9,17... | collective-permute-start | bytes 1228808 | tf_op jit(solution)/shard_map/ppermute | solution.py:617
  255.8 9.2 %collective-permute-start.13 = (bf16[4,80,640]{2,1,0:T(8,128)(2,1)S(1)}, bf16[4,80,640]{2,1,0:T(8,128)(2,1)S(1)}, u32[]{:S(2)}, u32[]{:S(2)}) collective-permute-start(bf16[4,80,640]{2,1,0:T(8,128)(2,1)S(1)} %fusion.9), channel_id=1, source_target_pairs={{0,8},{1,9},{2,10},{3,11},{4,28},{5,29},{6,30},{7,31},{8,16},{9,17... | collective-permute-start | bytes 1228808 | tf_op jit(solution)/shard_map/ppermute | solution.py:617
  258.7 11.1 %collective-permute-start.31 = (bf16[80,640]{1,0:T(8,128)(2,1)S(1)}, bf16[80,640]{1,0:T(8,128)(2,1)S(1)}, u32[]{:S(2)}, u32[]{:S(2)}) collective-permute-start(bf16[80,640]{1,0:T(8,128)(2,1)S(1)} %dynamic-slice_bitcast_fusion), channel_id=1, source_target_pairs={{0,8},{1,9},{2,10},{3,11},{4,28},{5,29},{6,30},{7,31},{8,16},{9,17... | collective-permute-start | bytes 307208 | tf_op jit(solution)/shard_map/ppermute | solution.py:617
  260.8 15.1 %collective-permute-start.25 = (bf16[4,80,640]{2,1,0:T(8,128)(2,1)S(1)}, bf16[4,80,640]{2,1,0:T(8,128)(2,1)S(1)}, u32[]{:S(2)}, u32[]{:S(2)}) collective-permute-start(bf16[4,80,640]{2,1,0:T(8,128)(2,1)S(1)} %fusion.3), channel_id=1, source_target_pairs={{0,8},{1,9},{2,10},{3,11},{4,28},{5,29},{6,30},{7,31},{8,16},{9,17... | collective-permute-start | bytes 1228808 | tf_op jit(solution)/shard_map/ppermute | solution.py:617
  266.2 5.9 %collective-permute-start.14 = (bf16[80,640]{1,0:T(8,128)(2,1)S(1)}, bf16[80,640]{1,0:T(8,128)(2,1)S(1)}, u32[]{:S(2)}, u32[]{:S(2)}) collective-permute-start(bf16[80,640]{1,0:T(8,128)(2,1)S(1)} %dynamic-slice_bitcast_fusion.3), channel_id=1, source_target_pairs={{0,32},{1,33},{2,34},{3,35},{4,100},{5,101},{6,102},{7,103},{8,40}... | collective-permute-start | bytes 307208 | tf_op jit(solution)/shard_map/ppermute | solution.py:617
  269.8 5.9 %collective-permute-start.32 = (bf16[80,640]{1,0:T(8,128)(2,1)S(1)}, bf16[80,640]{1,0:T(8,128)(2,1)S(1)}, u32[]{:S(2)}, u32[]{:S(2)}) collective-permute-start(bf16[80,640]{1,0:T(8,128)(2,1)S(1)} %fusion.30), channel_id=1, source_target_pairs={{0,8},{1,9},{2,10},{3,11},{4,28},{5,29},{6,30},{7,31},{8,16},{9,17... | collective-permute-start | bytes 307208 | tf_op jit(solution)/shard_map/ppermute | solution.py:617
  272.2 5.9 %collective-permute-start.15 = (bf16[80,640]{1,0:T(8,128)(2,1)S(1)}, bf16[80,640]{1,0:T(8,128)(2,1)S(1)}, u32[]{:S(2)}, u32[]{:S(2)}) collective-permute-start(bf16[80,640]{1,0:T(8,128)(2,1)S(1)} %fusion.39), channel_id=1, source_target_pairs={{0,32},{1,33},{2,34},{3,35},{4,100},{5,101},{6,102},{7,103},{8,40}... | collective-permute-start | bytes 307208 | tf_op jit(solution)/shard_map/ppermute | solution.py:617
  275.8 6.3 %collective-permute-start.33 = (bf16[80,640]{1,0:T(8,128)(2,1)S(1)}, bf16[80,640]{1,0:T(8,128)(2,1)S(1)}, u32[]{:S(2)}, u32[]{:S(2)}) collective-permute-start(bf16[80,640]{1,0:T(8,128)(2,1)S(1)} %fusion.29), channel_id=1, source_target_pairs={{0,8},{1,9},{2,10},{3,11},{4,28},{5,29},{6,30},{7,31},{8,16},{9,17... | collective-permute-start | bytes 307208 | tf_op jit(solution)/shard_map/ppermute | solution.py:617
  276.1 5.9 %collective-permute-start.26 = (bf16[80,640]{1,0:T(8,128)(2,1)S(1)}, bf16[80,640]{1,0:T(8,128)(2,1)S(1)}, u32[]{:S(2)}, u32[]{:S(2)}) collective-permute-start(bf16[80,640]{1,0:T(8,128)(2,1)S(1)} %dynamic-slice_bitcast_fusion.1), channel_id=1, source_target_pairs={{0,32},{1,33},{2,34},{3,35},{4,100},{5,101},{6,102},{7,103},{8,40}... | collective-permute-start | bytes 307208 | tf_op jit(solution)/shard_map/ppermute | solution.py:617
  278.2 9.9 %collective-permute-start.16 = (bf16[80,640]{1,0:T(8,128)(2,1)S(1)}, bf16[80,640]{1,0:T(8,128)(2,1)S(1)}, u32[]{:S(2)}, u32[]{:S(2)}) collective-permute-start(bf16[80,640]{1,0:T(8,128)(2,1)S(1)} %fusion.38), channel_id=1, source_target_pairs={{0,32},{1,33},{2,34},{3,35},{4,100},{5,101},{6,102},{7,103},{8,40}... | collective-permute-start | bytes 307208 | tf_op jit(solution)/shard_map/ppermute | solution.py:617
  282.0 5.9 %collective-permute-start.27 = (bf16[80,640]{1,0:T(8,128)(2,1)S(1)}, bf16[80,640]{1,0:T(8,128)(2,1)S(1)}, u32[]{:S(2)}, u32[]{:S(2)}) collective-permute-start(bf16[80,640]{1,0:T(8,128)(2,1)S(1)} %fusion.33), channel_id=1, source_target_pairs={{0,32},{1,33},{2,34},{3,35},{4,100},{5,101},{6,102},{7,103},{8,40}... | collective-permute-start | bytes 307208 | tf_op jit(solution)/shard_map/ppermute | solution.py:617
  288.0 5.9 %collective-permute-start.28 = (bf16[80,640]{1,0:T(8,128)(2,1)S(1)}, bf16[80,640]{1,0:T(8,128)(2,1)S(1)}, u32[]{:S(2)}, u32[]{:S(2)}) collective-permute-start(bf16[80,640]{1,0:T(8,128)(2,1)S(1)} %fusion.32), channel_id=1, source_target_pairs={{0,32},{1,33},{2,34},{3,35},{4,100},{5,101},{6,102},{7,103},{8,40}... | collective-permute-start | bytes 307208 | tf_op jit(solution)/shard_map/ppermute | solution.py:617
  (16 other events, 19.0 us)
Sparse Core Ops, SparseCore 0:
  176.7 25.7 reduce-scatter.2
  245.0 29.8 reduce-scatter.4
where the time goes:
time: 303 us; the launch traced here: 302 us
  waiting for transfers between devices  117 us (39%)
  Pallas kernels  67.8 us (22%)
  starting transfers between devices  39.6 us (13%)
  local copies, waits for them, and re-layouts  34.5 us (11%)
  other arithmetic  27.4 us (9%)
  between operations  14.8 us (5%)
    ppermute x34, waiting for transfers between devices, moved(): return lax.ppermute(value, ('seq', 'tp'), pairs)  83.8 us
    all_to_all x2, waiting for transfers between devices, exchanged(): return lax.all_to_all(value, 'seq', 0, 0, tiled=True)  33.5 us
    unnamed x90, local copies, waits for them, and re-layouts  27.7 us
    ppermute x34, starting transfers between devices, moved(): return lax.ppermute(value, ('seq', 'tp'), pairs)  27.2 us
    convert_element_type x24, other arithmetic, added(): return (left.astype(F32) + right.astype(F32)).astype(BF16)  21.7 us
    pallas_call x4, Pallas kernels, weight_partial(): pl.pallas_call(functools.partial(weight_kernel, rows, len(after)), in_spe...  19.9 us
    pallas_call x1, Pallas kernels, sequence_part(): pl.pallas_call(functools.partial(sequence_kernel, group), out_shape=jax.S...  18.4 us
    all_to_all x2, starting transfers between devices, exchanged(): return lax.all_to_all(value, 'seq', 0, 0, tiled=True)  12.1 us
  transfers between devices with their start and end apart: 38, of which 23 were waited for; matrix products, arithmetic and copies ran while one was open for 13% of the time, Pallas kernels for 8%

commit v1 on v0

--- a/solution.py
+++ b/solution.py
@@ -53,6 +53,10 @@
 
 def in_smem(count):
     return [pl.BlockSpec(memory_space=pltpu.SMEM)] * count
+
+
+def in_hbm(count):
+    return [pl.BlockSpec(memory_space=pltpu.HBM)] * count
 
 
 def anywhere(count):
@@ -306,83 +310,109 @@
     return pl.ds(pl.multiple_of(tile * height, 16), height)
 
 
-def projected(shards_ref, ids_ref, weight_ref, total_ref):
-    count, _, depth = shards_ref.shape
-    total_ref[...] = jnp.zeros_like(total_ref)
-
-    def add(tile):
-        total_ref[...] += dot_nn(
-            shards_ref[tile], weight_ref[rows_of(ids_ref[tile], depth), :]
-        )
-
-    tiles_of(count, add)
-
-
-def key_value_kernel(
-    group, shards_ref, key_ref, value_ref, ids_ref, kv_ref, total, across, packed,
+def weight_rows(weight_ref, ids_ref, tile, depth):
+    return weight_ref[rows_of(ids_ref[tile], depth), :]
+
+
+def near_kernel(shard_count, *refs):
+    shards, rest = refs[:shard_count], refs[shard_count:]
+    half = (len(rest) - 1) // 2
+    weights, ids_ref, sums = rest[:half], rest[half], rest[half + 1 :]
+    depth = shards[0].shape[1]
+    for weight_ref, sum_ref in zip(weights, sums):
+        total = dot_nn(shards[0][...], weight_rows(weight_ref, ids_ref, 0, depth))
+        for tile in range(1, shard_count):
+            total += dot_nn(shards[tile][...], weight_rows(weight_ref, ids_ref, tile, depth))
+        sum_ref[...] = total
+
+
+def near_part(shards, weights, ids):
+    rows, depth = shards[0].shape
+    channels = weights[0].shape[1]
+    return pl.pallas_call(
+        functools.partial(near_kernel, len(shards)),
+        in_specs=in_vmem(len(shards) + len(weights)) + in_smem(1),
+        out_specs=tuple(in_vmem(len(weights))),
+        out_shape=(jax.ShapeDtypeStruct((rows, channels), F32),) * len(weights),
+        compiler_params=params(24),
+        cost_estimate=call_cost(
+            2 * len(shards) * len(weights) * rows * depth * channels, 12_000_000
+        ),
+    )(*shards, *weights, ids)
+
+
+def far_kernel(
+    group, shard_ref, key_ref, value_ref, query_ref, key_sum, value_sum, query_sum, ids_ref,
+    kv_ref, query_out, across, packed,
 ):
+    depth = shard_ref.shape[1]
+    tile = ids_ref.shape[0] - 1
     pad = padded(2 * group)
     owners = kv_ref.shape[0]
-    for index, weight_ref in enumerate((key_ref, value_ref)):
-        projected(shards_ref, ids_ref, weight_ref, total)
-        across[...] = total[...].T
+    for index, (weight_ref, sum_ref) in enumerate(((key_ref, key_sum), (value_ref, value_sum))):
+        part = dot_nn(shard_ref[...], weight_rows(weight_ref, ids_ref, tile, depth))
+        across[...] = (sum_ref[...] + part).T
         for owner in range(owners):
             first = owner * pad + index * group
             packed[first : first + group] = across[owner * group : (owner + 1) * group]
     for owner in range(owners):
         kv_ref[owner] = packed[owner * pad : owner * pad + 2 * group].astype(BF16)
-
-
-def key_value_part(shards, ids, w_key, w_value, owners):
-    count, rows, depth = shards.shape
-    channels = w_key.shape[1]
+    part = dot_nn(shard_ref[...], weight_rows(query_ref, ids_ref, tile, depth))
+    query_out[...] = (query_sum[...] + part).astype(BF16)
+
+
+def far_part(shard, weights, sums, ids, owners):
+    rows, depth = shard.shape
+    channels = weights[0].shape[1]
     group = channels // owners
     return pl.pallas_call(
-        functools.partial(key_value_kernel, group),
-        in_specs=in_vmem(3) + in_smem(1),
-        out_specs=in_vmem(1)[0],
-        out_shape=jax.ShapeDtypeStruct((owners, 2 * group, rows), BF16),
+        functools.partial(far_kernel, group),
+        in_specs=in_vmem(7) + in_smem(1),
+        out_specs=tuple(in_vmem(2)),
+        out_shape=(
+            jax.ShapeDtypeStruct((owners, 2 * group, rows), BF16),
+            jax.ShapeDtypeStruct((rows, channels), BF16),
+        ),
         scratch_shapes=[
-            pltpu.VMEM((rows, channels), F32),
             pltpu.VMEM((channels, rows), F32),
             pltpu.VMEM((owners * padded(2 * group), rows), F32),
         ],
         compiler_params=params(24),
-        cost_estimate=call_cost(4 * count * rows * depth * channels, 12_000_000),
-    )(shards, w_key, w_value, ids)
-
-
-def query_kernel(after_ref, shards_ref, weight_ref, ids_ref, query_ref, total):
-    projected(shards_ref, ids_ref, weight_ref, total)
-    query_ref[...] = total[...].astype(BF16)
-
-
-def query_part(after, shards, ids, w_query):
-    count, rows, depth = shards.shape
-    channels = w_query.shape[1]
+        cost_estimate=call_cost(6 * rows * depth * channels, 12_000_000),
+    )(shard, *weights, *sums, ids)
+
+
+def grad_near_kernel(after_ref, first_ref, second_ref, third_ref, weight_ref, ids_ref, sum_ref):
+    depth = first_ref.shape[1]
+
+    def part(tile, shard_ref):
+        first = pl.multiple_of(ids_ref[tile] * depth, LANE)
+        return dot_nt(shard_ref[...], weight_ref[:, pl.ds(first, depth)])
+
+    sum_ref[...] = part(0, first_ref) + part(1, second_ref) + part(2, third_ref)
+
+
+def grad_near_part(after, shards, w_out, ids):
+    rows, depth = shards[0].shape
+    channels = w_out.shape[0]
     return pl.pallas_call(
-        query_kernel,
-        in_specs=anywhere(1) + in_vmem(2) + in_smem(1),
+        grad_near_kernel,
+        in_specs=anywhere(1) + in_vmem(4) + in_smem(1),
         out_specs=in_vmem(1)[0],
-        out_shape=jax.ShapeDtypeStruct((rows, channels), BF16),
-        scratch_shapes=[pltpu.VMEM((rows, channels), F32)],
-        compiler_params=params(14),
-        cost_estimate=call_cost(2 * count * rows * depth * channels, 6_000_000),
-    )(after, shards, w_query, ids)
-
-
-def gated_grad_kernel(
-    group, kv_ref, shards_ref, weight_ref, query_ref, ids_ref, gated_ref, grouped_ref, total, across,
+        out_shape=jax.ShapeDtypeStruct((rows, channels), F32),
+        compiler_params=params(16),
+        cost_estimate=call_cost(6 * rows * depth * channels, 6_000_000),
+    )(after, *shards, w_out, ids)
+
+
+def grad_far_kernel(
+    group, kv_ref, shard_ref, weight_ref, sum_ref, query_ref, ids_ref, gated_ref, grouped_ref,
+    across,
 ):
-    count, _, depth = shards_ref.shape
-    total[...] = jnp.zeros_like(total)
-
-    def add(tile):
-        first = pl.multiple_of(ids_ref[tile] * depth, LANE)
-        total[...] += dot_nt(shards_ref[tile], weight_ref[:, pl.ds(first, depth)])
-
-    tiles_of(count, add)
-    gated = total[...].astype(BF16)
+    depth = shard_ref.shape[1]
+    first = pl.multiple_of(ids_ref[ids_ref.shape[0] - 1] * depth, LANE)
+    total = sum_ref[...] + dot_nt(shard_ref[...], weight_ref[:, pl.ds(first, depth)])
+    gated = total.astype(BF16)
     gated_ref[...] = gated
     across[...] = (gated.astype(F32) * query_ref[...].astype(F32)).T
     for owner in range(grouped_ref.shape[0]):
@@ -390,143 +420,163 @@
         grouped_ref[owner, 2 * group :] = across[owner * group : (owner + 1) * group].astype(BF16)
 
 
-def gated_grad_part(kv, shards, ids, w_out, query):
-    count, rows, depth = shards.shape
+def grad_far_part(kv, shard, w_out, total, query, ids):
+    rows, depth = shard.shape
     channels = w_out.shape[0]
     owners = kv.shape[0]
     group = channels // owners
     return pl.pallas_call(
-        functools.partial(gated_grad_kernel, group),
-        in_specs=in_vmem(4) + in_smem(1),
+        functools.partial(grad_far_kernel, group),
+        in_specs=in_vmem(5) + in_smem(1),
         out_specs=tuple(in_vmem(2)),
         out_shape=(
             jax.ShapeDtypeStruct((rows, channels), BF16),
             jax.ShapeDtypeStruct((owners, 3 * group, rows), BF16),
         ),
-        scratch_shapes=[pltpu.VMEM((rows, channels), F32), pltpu.VMEM((channels, rows), F32)],
-        compiler_params=params(18),
-        cost_estimate=call_cost(2 * count * rows * depth * channels, 9_000_000),
-    )(kv, shards, w_out, query, ids)
+        scratch_shapes=[pltpu.VMEM((channels, rows), F32)],
+        compiler_params=params(16),
+        cost_estimate=call_cost(2 * rows * depth * channels, 6_000_000),
+    )(kv, shard, w_out, total, query, ids)
 
 
 def unpack_kernel(
     group, returned_ref, query_ref, gated_ref, forward_ref, query_grad_ref, key_ref, value_ref,
-    response_rows, value_rows, key_rows,
+    filter_ref, init_ref, response_rows, value_rows, key_rows, small_rows,
 ):
-    for owner in range(returned_ref.shape[0]):
+    owners, lines, width = returned_ref.shape
+    extra = lines - 3 * group
+    for owner in range(owners):
         piece = returned_ref[owner].astype(F32)
         at = slice(owner * group, (owner + 1) * group)
         response_rows[at] = piece[:group]
         value_rows[at] = piece[group : 2 * group]
         key_rows[at] = piece[2 * group : 3 * group]
+        for part in range(width // LANE):
+            count = min(extra, group - extra * part)
+            first = owner * group + extra * part
+            small_rows[first : first + count] = piece[
+                3 * group : 3 * group + count, LANE * part : LANE * (part + 1)
+            ]
     response = response_rows[...].T
     forward_ref[...] = (query_ref[...].astype(F32) * response).astype(BF16)
     query_grad_ref[...] = (gated_ref[...].astype(F32) * response).astype(BF16)
     value_ref[...] = value_rows[...].T.astype(BF16)
     key_ref[...] = key_rows[...].T.astype(BF16)
-
-
-def unpack_part(returned, query, gated):
+    small = small_rows[...].T
+    taps = filter_ref.shape[0]
+    filter_ref[...] = small[:taps]
+    init_ref[...] = small[taps:]
+
+
+def unpack_part(returned, query, gated, taps):
     rows, channels = query.shape
+    short = jax.ShapeDtypeStruct((rows, channels), BF16)
     return pl.pallas_call(
         functools.partial(unpack_kernel, channels // returned.shape[0]),
         in_specs=in_vmem(3),
-        out_specs=tuple(in_vmem(4)),
-        out_shape=(jax.ShapeDtypeStruct((rows, channels), BF16),) * 4,
-        scratch_shapes=[pltpu.VMEM((channels, rows), F32)] * 3,
-        compiler_params=params(12),
+        out_specs=tuple(in_vmem(6)),
+        out_shape=(
+            short, short, short, short,
+            jax.ShapeDtypeStruct((taps, channels), F32),
+            jax.ShapeDtypeStruct((LANE - taps, channels), F32),
+        ),
+        scratch_shapes=[pltpu.VMEM((channels, rows), F32)] * 3
+        + [pltpu.VMEM((channels, LANE), F32)],
+        compiler_params=params(14),
         cost_estimate=call_cost(4 * rows * channels, 5_000_000),
     )(returned, query, gated)
 
 
-def turn_kernel(after_ref, first_ref, second_ref, first_out, second_out, first, second, sems):
-    count = first.shape[0]
-
-    def copy_out(index, tile):
-        held, target = ((first, first_out), (second, second_out))[index]
-        return pltpu.make_async_copy(held.at[tile], target.at[tile], sems.at[index, tile])
-
-    def turn(tile):
-        first[tile] = first_ref[tile].T
-        copy_out(0, tile).start()
-        second[tile] = second_ref[tile].T
-        copy_out(1, tile).start()
-
-    def finish(tile):
-        copy_out(0, tile).wait()
-        copy_out(1, tile).wait()
-
-    tiles_of(count, turn)
-    tiles_of(count, finish)
+def turn_kernel(after_ref, *refs):
+    count = (len(refs) - 5) // 2
+    shards, (first_out, second_out, first, second, sems) = refs[:-5], refs[-5:]
+    held = ((first, first_out), (second, second_out))
+    sent = []
+    for index, ref in enumerate(shards):
+        which, tile = index // count, index % count
+        source, target = held[which]
+        source[tile] = ref[...].T
+        sent.append(
+            pltpu.make_async_copy(source.at[tile], target.at[tile], sems.at[which, tile])
+        )
+        sent[-1].start()
+    for copy in sent:
+        copy.wait()
 
 
 def turn_part(after, first, second):
-    count, rows, depth = first.shape
+    rows, depth = first[0].shape
+    count = len(first)
     out = jax.ShapeDtypeStruct((count, depth, rows), BF16)
     return pl.pallas_call(
         turn_kernel,
-        in_specs=anywhere(1) + in_vmem(2),
-        out_specs=tuple(anywhere(2)),
+        in_specs=anywhere(1) + in_vmem(2 * count),
+        out_specs=tuple(in_hbm(2)),
         out_shape=(out, out),
         scratch_shapes=[pltpu.VMEM(out.shape, BF16)] * 2 + [pltpu.SemaphoreType.DMA((2, count))],
         compiler_params=params(16),
         cost_estimate=call_cost(2 * count * depth * rows, 8_000_000),
-    )(after, first, second)
-
-
-def weight_kernel(rows, unread, *refs):
-    (
-        wide_ref, narrow_ref, ids_ref, core_ref, keep_out, send_out, keep, send, keep_sems,
-        send_sems,
-    ) = refs[unread:]
-    tiles, held = keep.shape[:2]
-
-    def copies(tile):
+    )(after, *first, *second)
+
+
+def weight_kernel(rows, count, after_ref, wide_ref, *refs):
+    narrows, (ids_ref, core_ref), refs = refs[:count], refs[count : count + 2], refs[count + 2 :]
+    outs, (keep, send, sems) = refs[: 2 * count], refs[2 * count :]
+    tiles, held = keep.shape[1:3]
+
+    def copies(tile, index):
         at = pl.ds(ids_ref[tile] * held, held)
         return (
-            pltpu.make_async_copy(send.at[tile], send_out.at[at], send_sems.at[tile]),
-            pltpu.make_async_copy(keep.at[tile], keep_out.at[at], keep_sems.at[tile]),
+            pltpu.make_async_copy(
+                keep.at[index, tile], outs[2 * index].at[at], sems.at[0, index, tile]
+            ),
+            pltpu.make_async_copy(
+                send.at[index, tile], outs[2 * index + 1].at[at], sems.at[1, index, tile]
+            ),
         )
 
     def multiply(tile):
-        result = dot_nn(wide_ref[tile], narrow_ref[...]).astype(BF16)
-        for core in range(2):
-
-            @pl.when(core_ref[0] == core)
-            def _():
-                for chip in range(held):
-                    at = (2 * chip + core) * rows
-                    other = (2 * chip + 1 - core) * rows
-                    keep[tile, chip] = result[at : at + rows]
-                    send[tile, chip] = result[other : other + rows]
-
-        for copy in copies(tile):
-            copy.start()
+        for index in range(count):
+            result = dot_nn(wide_ref[tile], narrows[index][...]).astype(BF16)
+            for core in range(2):
+
+                @pl.when(core_ref[0] == core)
+                def _():
+                    for chip in range(held):
+                        at = (2 * chip + core) * rows
+                        other = (2 * chip + 1 - core) * rows
+                        keep[index, tile, chip] = result[at : at + rows]
+                        send[index, tile, chip] = result[other : other + rows]
+
+            for copy in copies(tile, index):
+                copy.start()
 
     def finish(tile):
-        for copy in copies(tile):
-            copy.wait()
+        for index in range(count):
+            for copy in copies(tile, index):
+                copy.wait()
 
     tiles_of(tiles, multiply)
     tiles_of(tiles, finish)
 
 
-def weight_partial(after, wide, ids, narrow, core, chips):
+def weight_partial(after, wide, ids, narrows, core, chips):
     tiles, height, depth = wide.shape
-    width = narrow.shape[1]
+    width = narrows[0].shape[1]
     total = tiles * height
     rows = total // (2 * chips)
-    halves = pltpu.VMEM((tiles, chips // tiles, rows, width), BF16)
-    return pl.pallas_call(
-        functools.partial(weight_kernel, rows, len(after)),
-        in_specs=anywhere(len(after)) + in_vmem(2) + in_smem(2),
-        out_specs=tuple(anywhere(2)),
-        out_shape=(jax.ShapeDtypeStruct((chips, rows, width), BF16),) * 2,
-        scratch_shapes=[halves, halves]
-        + [pltpu.SemaphoreType.DMA((tiles,)), pltpu.SemaphoreType.DMA((tiles,))],
-        compiler_params=params(16),
-        cost_estimate=call_cost(2 * total * depth * width, 6_000_000),
-    )(*after, wide, narrow, ids, core)
+    count = len(narrows)
+    halves = pltpu.VMEM((count, tiles, chips // tiles, rows, width), BF16)
+    flat = pl.pallas_call(
+        functools.partial(weight_kernel, rows, count),
+        in_specs=anywhere(1) + in_vmem(1 + count) + in_smem(2),
+        out_specs=tuple(in_hbm(2 * count)),
+        out_shape=(jax.ShapeDtypeStruct((chips, rows, width), BF16),) * (2 * count),
+        scratch_shapes=[halves, halves, pltpu.SemaphoreType.DMA((2, count, tiles))],
+        compiler_params=params(12 + 6 * count),
+        cost_estimate=call_cost(2 * count * total * depth * width, 6_000_000 * count),
+    )(after, wide, *narrows, ids, core)
+    return [flat[2 * index : 2 * index + 2] for index in range(count)]
 
 
 def mixed_kernel(after_ref, gated_ref, weight_ref, out_ref, result, sems):
@@ -549,7 +599,7 @@
     return pl.pallas_call(
         mixed_kernel,
         in_specs=anywhere(1) + in_vmem(2),
-        out_specs=anywhere(1)[0],
+        out_specs=in_hbm(1)[0],
         out_shape=jax.ShapeDtypeStruct((count, rows, width), BF16),
         scratch_shapes=[
             pltpu.VMEM((count, rows, width), BF16), pltpu.SemaphoreType.DMA((count,)),
@@ -585,7 +635,7 @@
     return pl.pallas_call(
         functools.partial(input_kernel, len(after)),
         in_specs=anywhere(len(after)) + in_vmem(len(backs) + len(weights)),
-        out_specs=anywhere(1)[0],
+        out_specs=in_hbm(1)[0],
         out_shape=jax.ShapeDtypeStruct((count, rows, width), BF16),
         scratch_shapes=[
             pltpu.VMEM((count, rows, width), BF16), pltpu.SemaphoreType.DMA((count,)),
@@ -631,38 +681,26 @@
     return travelling
 
 
-class SeqSum:
-    def __init__(self, halves, first, places, up):
-        keep, send = halves
-        _, rows, width = keep.shape
-        grid = (SIDE, SIDE, rows, width)
-        axis = "xy".index(first)
-        self.first, self.second = first, "yx"[axis]
-        self.places, self.up = places, up
-        self.keep = picked(keep.reshape(grid), axis)
-        self.came = picked(moved(send, "core", 1).reshape(grid), axis)
-        self.start = self.block((places[first] - up) % SIDE)
-        self.held = None
-
-    def block(self, index):
-        return added(self.keep(index), self.came(index))
-
-    def ring(self, travelling, steps):
-        return ring_sum(
-            travelling, self.block, self.places[self.first], self.up, self.first, steps
-        )
-
-    def step(self):
-        if self.held is None:
-            self.held = self.ring(self.start, (2,))
-        return self.held
-
-    def total(self):
-        half = self.ring(self.step(), range(3, SIDE + 1))
-        place = self.places[self.second]
-        block = picked(half)
-        start = block((place - self.up) % SIDE)
-        return ring_sum(start, block, place, self.up, self.second, range(2, SIDE + 1)).astype(F32)
+def summed_over_seq(halves, first, places, up):
+    keep, came = halves
+    _, rows, width = keep.shape
+    grid = (SIDE, SIDE, rows, width)
+    axis = "xy".index(first)
+    second = "yx"[axis]
+    keep = picked(keep.reshape(grid), axis)
+    came = picked(came.reshape(grid), axis)
+
+    def block(index):
+        return added(keep(index), came(index))
+
+    place = places[first]
+    half = ring_sum(block((place - up) % SIDE), block, place, up, first, range(2, SIDE + 1))
+    place, mine = places[second], picked(half)
+    total = mine(place).astype(F32)
+    for step in (1, -1, 2):
+        steps = (2, -2) if step == 2 else step
+        total += moved(mine((place + step) % SIDE), second, steps).astype(F32)
+    return total
 
 
 def per_device(
@@ -695,7 +733,7 @@
     def all_shards(mine, sides):
         below, above = sides
         far = moved(jnp.where(core == 0, below, above), "z", (1, -1))
-        return jnp.stack([mine, below, above, far])
+        return mine, below, above, far
 
     shards = all_shards(tokens, token_sides)
     grad_shards = all_shards(cotangent, grad_sides)
@@ -716,49 +754,37 @@
     def exchanged(value):
         return lax.all_to_all(value, "seq", 0, 0, tiled=True)
 
-    kv = key_value_part(shards, ids, w_key, w_value, seq_count)
-    query = query_part(kv, shards, ids, w_query)
-    gated_grad, packed = gated_grad_part(kv, grad_shards, ids, w_out, query)
+    weights = (w_key, w_value, w_query)
+    sums = near_part(shards[:3], weights, ids)
+    grad_sum = grad_near_part(sums[2], grad_shards[:3], w_out, ids)
+    kv, query = far_part(shards[3], weights, sums, ids, seq_count)
+    gated_grad, packed = grad_far_part(kv, grad_shards[3], w_out, grad_sum, query, ids)
     results = sequence_part(exchanged(packed), rows, cols, taps, skip)
     shards_turned, grad_turned = turn_part(results, shards, grad_shards)
     returned = exchanged(results)
-    gated, back_query, back_key, back_value = unpack_part(returned, query, gated_grad)
+    gated, back_query, back_key, back_value, grad_filter, grad_init = unpack_part(
+        returned, query, gated_grad, tap_count
+    )
     chips = SIDE * SIDE
     up = 1 - 2 * core
 
-    def weight(after, wide, narrow):
-        return weight_partial(after, wide, ids, narrow, core_word, chips)
-
-    out_halves = weight((gated,), grad_turned, gated)
-    out_sum = SeqSum(out_halves, "x", places, up)
-    query_halves = weight((out_halves[1],), shards_turned, back_query)
-    query_sum = SeqSum(query_halves, "y", places, up)
+    (out_halves,) = weight_partial(gated, grad_turned, ids, (gated,), core_word, chips)
+    query_halves, key_halves, value_halves = weight_partial(
+        out_halves[1], shards_turned, ids, (back_query, back_key, back_value), core_word, chips
+    )
     partial_mixed = mixed_part(query_halves[1], gated, w_out, SIDE)
     mixed = lax.psum_scatter(partial_mixed, "tp", scatter_dimension=0, tiled=True)[0]
-    key_halves = weight((partial_mixed,), shards_turned, back_key)
-    key_sum = SeqSum(key_halves, "x", places, up)
-    value_halves = weight((key_halves[1], out_sum.start), shards_turned, back_value)
-    value_sum = SeqSum(value_halves, "y", places, up)
-    out_first, query_first = out_sum.step(), query_sum.step()
-    out_first, value_sum.start = lax.optimization_barrier((out_first, value_sum.start))
-    out_sum.held = out_first
+    swapped = [
+        (keep, moved(send, "core", 1))
+        for keep, send in (out_halves, query_halves, key_halves, value_halves)
+    ]
     partial_input = input_part(
-        (value_halves[1], out_first, query_first, key_sum.start, value_sum.start),
-        (back_query, back_key, back_value),
-        (w_query, w_key, w_value),
-        SIDE,
-    )
-    returned, query_sum.held, partial_input = lax.optimization_barrier(
-        (returned, query_first, partial_input)
+        (partial_mixed, swapped[0][1], swapped[1][1], swapped[2][1]), (back_query, back_key, back_value), (w_query, w_key, w_value), SIDE
     )
     grad_input = lax.psum_scatter(partial_input, "tp", scatter_dimension=0, tiled=True)[0]
-    small = returned[:, 3 * group :].reshape(seq_count, -1, row_count // LANE, LANE)
-    small = small.transpose(0, 2, 1, 3).reshape(seq_count, -1, LANE)[:, :group]
-    small = small.reshape(channels, LANE).T.astype(F32)
-    grad_filter, grad_init = small[:tap_count], small[tap_count:]
-
     grad_out, grad_query, grad_key, grad_value = (
-        each.total() for each in (out_sum, query_sum, key_sum, value_sum)
+        summed_over_seq(halves, first, places, up)
+        for halves, first in zip(swapped, "xyxy")
     )
     grad_out = grad_out.T
     return (mixed, grad_input, grad_query, grad_key, grad_value, grad_out, grad_filter, grad_init)

time: 303 us -> 267 us (0.88)
  waiting for transfers between devices: 117 us -> 58 us
  starting transfers between devices: 39.6 us -> 52.8 us
  local copies, waits for them, and re-layouts: 34.5 us -> 47 us
    ppermute x34, waiting for transfers between devices: 83.8 us -> 31.1 us  [moved(): return lax.ppermute(value, ('seq', 'tp'), pairs)]
    unnamed x90 -> x132, local copies, waits for them, and re-layouts: 27.7 us -> 42.3 us
    ppermute x34, starting transfers between devices: 27.2 us -> 40.4 us  [moved(): return lax.ppermute(value, ('seq', 'tp'), pairs)]
    all_to_all x2, waiting for transfers between devices: 33.5 us -> 26.9 us  [exchanged(): return lax.all_to_all(value, 'seq', 0, 0, tiled=True)]
    pallas_call x8 -> x7, Pallas kernels: 36.9 us -> 34 us  [the longest x2 19.9 us: weight_partial(): pl.pallas_call(functools.partial(weight_kernel, rows, count), in_specs=an...]
    convert_element_type x24 -> x16, other arithmetic: 21.7 us -> 23 us  [added(): return (left.astype(F32) + right.astype(F32)).astype(BF16)]
  transfers between devices with their start and end apart: 38 -> 38, of which waited for: 23 -> 17; matrix products, arithmetic and copies ran while one was open for 13% -> 12% of each run, Pallas kernels for 8% -> 8%
where the time goes in v1:
time: 267 us; the launch traced here: 265 us
  Pallas kernels  66.7 us (25%)
  waiting for transfers between devices  58 us (22%)
  starting transfers between devices  52.8 us (20%)
  local copies, waits for them, and re-layouts  47 us (18%)
  other arithmetic  26.1 us (10%)
  between operations  14.6 us (5%)
    unnamed x132, local copies, waits for them, and re-layouts  42.3 us
    ppermute x34, starting transfers between devices, moved(): return lax.ppermute(value, ('seq', 'tp'), pairs)  40.4 us
    ppermute x34, waiting for transfers between devices, moved(): return lax.ppermute(value, ('seq', 'tp'), pairs)  31.1 us
    all_to_all x2, waiting for transfers between devices, exchanged(): return lax.all_to_all(value, 'seq', 0, 0, tiled=True)  26.9 us
    convert_element_type x16, other arithmetic, added(): return (left.astype(F32) + right.astype(F32)).astype(BF16)  23 us
    pallas_call x2, Pallas kernels, weight_partial(): pl.pallas_call(functools.partial(weight_kernel, rows, count), in_specs=an...  19.9 us
    pallas_call x1, Pallas kernels, sequence_part(): pl.pallas_call(functools.partial(sequence_kernel, group), out_shape=jax.S...  18.4 us
    all_to_all x2, starting transfers between devices, exchanged(): return lax.all_to_all(value, 'seq', 0, 0, tiled=True)  12.3 us
  transfers between devices with their start and end apart: 38, of which 17 were waited for; matrix products, arithmetic and copies ran while one was open for 12% of the time, Pallas kernels for 8%

profile of v1, /device:TPU:0, one launch (start us, length us, event | category | flops | bytes accessed | tf_op | source)
XLA Modules:
  0.0 265.2 jit_solution(3406819883301347678)
XLA Ops:
  7.2 2.1 collective-permute-start
  9.2 2.2 collective-permute-start.1
  11.5 3.2 %collective-permute-start.4 = (bf16[384,640]{1,0:T(8,128)(2,1)}, bf16[384,640]{1,0:T(8,128)(2,1)S(1)}, u32[]{:S(2)}, u32[]{:S(2)}) collective-permute-start(bf16[384,640]{1,0:T(8,128)(2,1)} %refs_4_.3), channel_id=1, source_target_pairs={{0,3},{1,0},{2,1},{3,2},{4,7},{5,4},{6,5},{7,6},{8,11},{9,8},{10,9... | collective-permute-start | bytes 1474568 | tf_op jit(solution)/shard_map/ppermute | solution.py:667
  14.7 8.9 %collective-permute-done.refs_1_ = bf16[384,640]{1,0:T(8,128)(2,1)S(1)} collective-permute-done((bf16[384,640]{1,0:T(8,128)(2,1)}, bf16[384,640]{1,0:T(8,128)(2,1)S(1)}, u32[]{:S(2)}, u32[]{:S(2)}) %collective-permute-start) | collective-permute-done | bytes 491552 | tf_op jit(solution)/shard_map/ppermute | solution.py:667
  23.7 2.0 collective-permute-start.2
  25.7 7.7 %collective-permute-done.3.second_ref.refs_5_ = bf16[384,640]{1,0:T(8,128)(2,1)S(1)} collective-permute-done((bf16[384,640]{1,0:T(8,128)(2,1)}, bf16[384,640]{1,0:T(8,128)(2,1)S(1)}, u32[]{:S(2)}, u32[]{:S(2)}) %collective-permute-start.3) | collective-permute-done | bytes 491552 | tf_op jit(solution)/shard_map/ppermute | solution.py:667
  34.2 2.0 collective-permute-start.5
  36.3 1.9 copy-done
  38.2 1.9 copy-done.2
  40.1 1.9 copy-done.5
  44.1 4.6 %shard_map.179 = (f32[384,640]{1,0:T(8,128)S(1)}, f32[384,640]{1,0:T(8,128)S(1)}, f32[384,640]{1,0:T(8,128)S(1)}) custom-call(bf16[384,640]{1,0:T(8,128)(2,1)S(1)} %copy-done.29, bf16[384,640]{1,0:T(8,128)(2,1)S(1)} %copy-done.16, bf16[384,640]{1,0:T(8,128)(2,1)S(1)} %copy-done.19, bf16[2560,640]{1,0:T(8,128)(2,1)S(1)} %copy-done, ...), custom_call_target="tpu_custom_call" | custom-call | flops 2831155200 | bytes 12000000 | tf_op jit(solution)/shard_map/pallas_call | solution.py:332
  48.8 2.0 shard_map.181.sum_ref
  51.7 2.1 shard_map.180
  53.9 1.4 shard_map.182
  57.2 7.6 %all-to-all-start = ((bf16[32,60,384]{2,1,0:T(8,128)(2,1)}), bf16[32,60,384]{2,1,0:T(8,128)(2,1)}, u32[]{:S(2)}, u32[]{:S(2)}) async-start(bf16[32,60,384]{2,1,0:T(8,128)(2,1)} %copy-done.46), calls=%async_computation | async-start | bytes 3145728 | tf_op jit(solution)/shard_map/all_to_all | solution.py:755
  67.2 1.6 copy.45.cols_ref
  69.7 18.0 %all-to-all-done.in_ref = bf16[32,60,384]{2,1,0:T(8,128)(2,1)} async-done(((bf16[32,60,384]{2,1,0:T(8,128)(2,1)}), bf16[32,60,384]{2,1,0:T(8,128)(2,1)}, u32[]{:S(2)}, u32[]{:S(2)}) %all-to-all-start) | async-done | bytes 1474592 | tf_op jit(solution)/shard_map/all_to_all | solution.py:755
  87.8 1.3 copy-done.47
  89.1 18.4 %shard_map.183.after_ref = bf16[32,67,384]{2,1,0:T(8,128)(2,1)S(1)} custom-call(bf16[32,60,384]{2,1,0:T(8,128)(2,1)} %all-to-all-done.in_ref, f32[2,20,64]{2,1,0:T(8,128)S(1)} %get-tuple-element.67.rows_ref, f32[2,20,64,1]{3,2,1,0:T(8,128)S(1)} %copy-done.47, f32[2,20,128]{2,1,0:T(8,128)S(1)} %pad_maximum_fusion.2.taps_ref, f32[20]{0:T(128)S(1)} %dynamic_slice.166.skip_ref), custom_call_target="tpu_custom_call" | custom-call | flops 22000001024 | bytes 5000000 | tf_op jit(solution)/shard_map/pallas_call | solution.py:282
  107.5 1.2 copy-done.13
  108.7 4.7 %all-to-all-start.1 = ((bf16[32,67,384]{2,1,0:T(8,128)(2,1)}), bf16[32,67,384]{2,1,0:T(8,128)(2,1)}, u32[]{:S(2)}, u32[]{:S(2)}) async-start(bf16[32,67,384]{2,1,0:T(8,128)(2,1)} %copy-done.13), calls=%async_computation.1 | async-start | bytes 3538944 | tf_op jit(solution)/shard_map/all_to_all | solution.py:755
  113.5 1.5 copy-done.14
  123.2 4.0 %shard_map.185 = (bf16[4,640,384]{2,1,0:T(8,128)(2,1)S(1)}, bf16[4,640,384]{2,1,0:T(8,128)(2,1)S(1)}) custom-call(bf16[32,67,384]{2,1,0:T(8,128)(2,1)S(1)} %copy-done.14, bf16[384,640]{1,0:T(8,128)(2,1)S(1)} %copy-done.30, bf16[384,640]{1,0:T(8,128)(2,1)S(1)} %copy-done.17, bf16[384,640]{1,0:T(8,128)(2,1)S(1)} %copy-done.20, ...), custom_call_target="tpu_custom_call" | custom-call | flops 1966080 | bytes 8000000 | tf_op jit(solution)/shard_map/pallas_call | solution.py:511
  127.3 1.3 copy-done.56
  128.6 1.3 copy-done.58
  129.9 8.8 %all-to-all-done.1.returned_ref = bf16[32,67,384]{2,1,0:T(8,128)(2,1)} async-done(((bf16[32,67,384]{2,1,0:T(8,128)(2,1)}), bf16[32,67,384]{2,1,0:T(8,128)(2,1)}, u32[]{:S(2)}, u32[]{:S(2)}) %all-to-all-start.1) | async-done | bytes 1646624 | tf_op jit(solution)/shard_map/all_to_all | solution.py:755
  140.8 3.2 %shard_map.184 = (bf16[384,640]{1,0:T(8,128)(2,1)S(1)}, bf16[384,640]{1,0:T(8,128)(2,1)S(1)}, bf16[384,640]{1,0:T(8,128)(2,1)S(1)}, bf16[384,640]{1,0:T(8,128)(2...) custom-call(bf16[32,67,384]{2,1,0:T(8,128)(2,1)} %all-to-all-done.1.returned_ref, bf16[384,640]{1,0:T(8,128)(2,1)S(1)} %copy-done.28, ...), custom_call_target="tpu_custom_call" | custom-call | flops 983040 | bytes 5000000 | tf_op jit(solution)/shard_map/pallas_call | solution.py:474
  144.0 5.2 %shard_map.186 = (bf16[16,80,640]{2,1,0:T(8,128)(2,1)S(1)}, bf16[16,80,640]{2,1,0:T(8,128)(2,1)S(1)}) custom-call(bf16[384,640]{1,0:T(8,128)(2,1)S(1)} %get-tuple-element.38.after_ref.refs_0_.gated_ref, bf16[4,640,384]{2,1,0:T(8,128)(2,1)S(1)} %copy-done.59, bf16[384,640]{1,0:T(8,128)(2,1)S(1)} %get-tuple-element.38.after_ref.refs_0_.gated_ref, ...), custom_call_target="tpu_custom_call" | custom-call | flops 1258291200 | bytes 6000000 | tf_op jit(solution)/shard_map/pallas_call | solution.py:570
  150.3 14.7 %shard_map.187 = (bf16[16,80,640]{2,1,0:T(8,128)(2,1)S(1)}, bf16[16,80,640]{2,1,0:T(8,128)(2,1)S(1)}, bf16[16,80,640]{2,1,0:T(8,128)(2,1)S(1)}, bf16[16,80,640]{...) custom-call(bf16[16,80,640]{2,1,0:T(8,128)(2,1)S(1)} %get-tuple-element.40.after_ref, ...), custom_call_target="tpu_custom_call" | custom-call | flops 3774873600 | bytes 18000000 | tf_op jit(solution)/shard_map/pallas_call | solution.py:570
  165.1 1.2 copy-done.38
  167.5 1.2 copy-done.42
  168.7 1.2 copy-done.60
  169.9 1.2 copy-done.61
  171.1 3.8 %shard_map.188.refs_0_ = bf16[4,384,640]{2,1,0:T(8,128)(2,1)S(1)} custom-call(bf16[16,80,640]{2,1,0:T(8,128)(2,1)S(1)} %get-tuple-element.45.after_ref, bf16[384,640]{1,0:T(8,128)(2,1)S(1)} %get-tuple-element.38.after_ref.refs_0_.gated_ref, bf16[640,2560]{1,0:T(8,128)(2,1)S(1)} %copy-done.9), custom_call_target="tpu_custom_call" | custom-call | flops 1258291200 | bytes 6000000 | tf_op jit(solution)/shard_map/pallas_call | solution.py:599
  174.8 1.3 copy-done.10
  176.1 1.2 copy-done.37
  178.5 2.8 %collective-permute-done.6.refs_1_ = bf16[16,80,640]{2,1,0:T(8,128)(2,1)} collective-permute-done((bf16[16,80,640]{2,1,0:T(8,128)(2,1)}, bf16[16,80,640]{2,1,0:T(8,128)(2,1)}, u32[]{:S(2)}, u32[]{:S(2)}) %collective-permute-start.6) | collective-permute-done | bytes 1638432 | tf_op jit(solution)/shard_map/ppermute | solution.py:667
  181.3 2.1 fusion.24
  183.7 2.1 fusion.20
  186.0 2.0 fusion.16
  188.8 2.0 fusion.12
  191.5 2.0 copy-done.7
  193.4 1.6 copy-done.11
  195.0 7.3 %shard_map.189 = bf16[4,384,640]{2,1,0:T(8,128)(2,1)S(1)} custom-call(bf16[4,384,640]{2,1,0:T(8,128)(2,1)S(1)} %copy-done.11, bf16[16,80,640]{2,1,0:T(8,128)(2,1)} %collective-permute-done.6.refs_1_, bf16[16,80,640]{2,1,0:T(8,128)(2,1)} %collective-permute-done.7.refs_2_, bf16[16,80,640]{2,1,0:T(8,128)(2,1)} %collective-permute-done.8.refs_3_, ...), custom_call_target="tpu_custom_call" | custom-call | flops 3774873600 | bytes 14000000 | tf_op jit(solution)/shard_map/pallas_call | solution.py:635
  202.3 1.3 copy-done.12
  203.6 1.5 fusion.2
  205.2 1.7 collective-permute-start.29
  206.9 1.4 fusion.5
  208.3 1.4 collective-permute-start.23
  209.8 1.3 fusion.8
  211.1 2.1 collective-permute-start.16
  213.1 1.3 fusion.11
  214.4 2.5 collective-permute-start.10
  222.3 1.4 collective-permute-done.10
  224.8 1.3 collective-permute-start.11
  226.1 1.2 collective-permute-done.30
  228.7 3.2 %collective-permute-start.32 = (bf16[80,640]{1,0:T(8,128)(2,1)S(1)}, bf16[80,640]{1,0:T(8,128)(2,1)S(1)}, u32[]{:S(2)}, u32[]{:S(2)}) collective-permute-start(bf16[80,640]{1,0:T(8,128)(2,1)S(1)} %get-tuple-element.56), channel_id=1, source_target_pairs={{0,24},{1,25},{2,26},{3,27},{4,28},{5,29},{6,30},{7,31},{8,0},{9,1... | collective-permute-start | bytes 307208 | tf_op jit(solution)/shard_map/ppermute | solution.py:667
  234.9 1.2 collective-permute-done.11
  236.1 2.3 collective-permute-start.26
  239.8 3.1 %collective-permute-start.19 = (bf16[80,640]{1,0:T(8,128)(2,1)S(1)}, bf16[80,640]{1,0:T(8,128)(2,1)S(1)}, u32[]{:S(2)}, u32[]{:S(2)}) collective-permute-start(bf16[80,640]{1,0:T(8,128)(2,1)S(1)} %get-tuple-element.62), channel_id=1, source_target_pairs={{0,24},{1,25},{2,26},{3,27},{4,28},{5,29},{6,30},{7,31},{8,0},{9,1... | collective-permute-start | bytes 307208 | tf_op jit(solution)/shard_map/ppermute | solution.py:667
  242.9 1.6 collective-permute-start.20
  246.3 1.8 collective-permute-start.12
  249.1 1.7 collective-permute-start.13
  253.7 3.9 %collective-permute-done.14 = bf16[80,640]{1,0:T(8,128)(2,1)S(1)} collective-permute-done((bf16[80,640]{1,0:T(8,128)(2,1)S(1)}, bf16[80,640]{1,0:T(8,128)(2,1)S(1)}, u32[]{:S(2)}, u32[]{:S(2)}) %collective-permute-start.14) | collective-permute-done | bytes 102432 | tf_op jit(solution)/shard_map/ppermute | solution.py:667
  (194 shorter events, 43.7 us)
Async XLA Ops:
  7.2 29.0 %copy-start.63 = (s32[4]{0:T(128)S(1)}, s32[4]{0:T(128)}, u32[]{:S(2)}) copy-start(s32[4]{0:T(128)} %constant.259.clone) | copy-start | bytes 52
  7.2 16.5 %collective-permute-start = (bf16[384,640]{1,0:T(8,128)(2,1)}, bf16[384,640]{1,0:T(8,128)(2,1)S(1)}, u32[]{:S(2)}, u32[]{:S(2)}) collective-permute-start(bf16[384,640]{1,0:T(8,128)(2,1)} %refs_0_.3), channel_id=1, source_target_pairs={{0,1},{1,2},{2,3},{3,0},{4,5},{5,6},{6,7},{7,4},{8,9},{9,10},{10,1... | collective-permute-start | bytes 1474568 | tf_op jit(solution)/shard_map/ppermute | solution.py:667
  9.2 14.4 %collective-permute-start.1 = (bf16[384,640]{1,0:T(8,128)(2,1)}, bf16[384,640]{1,0:T(8,128)(2,1)S(1)}, u32[]{:S(2)}, u32[]{:S(2)}) collective-permute-start(bf16[384,640]{1,0:T(8,128)(2,1)} %refs_0_.3), channel_id=1, source_target_pairs={{0,3},{1,0},{2,1},{3,2},{4,7},{5,4},{6,5},{7,6},{8,11},{9,8},{10,9... | collective-permute-start | bytes 1474568 | tf_op jit(solution)/shard_map/ppermute | solution.py:667
  11.5 21.9 %collective-permute-start.3 = (bf16[384,640]{1,0:T(8,128)(2,1)}, bf16[384,640]{1,0:T(8,128)(2,1)S(1)}, u32[]{:S(2)}, u32[]{:S(2)}) collective-permute-start(bf16[384,640]{1,0:T(8,128)(2,1)} %refs_4_.3), channel_id=1, source_target_pairs={{0,1},{1,2},{2,3},{3,0},{4,5},{5,6},{6,7},{7,4},{8,9},{9,10},{10,1... | collective-permute-start | bytes 1474568 | tf_op jit(solution)/shard_map/ppermute | solution.py:667
  11.5 22.7 %collective-permute-start.4 = (bf16[384,640]{1,0:T(8,128)(2,1)}, bf16[384,640]{1,0:T(8,128)(2,1)S(1)}, u32[]{:S(2)}, u32[]{:S(2)}) collective-permute-start(bf16[384,640]{1,0:T(8,128)(2,1)} %refs_4_.3), channel_id=1, source_target_pairs={{0,3},{1,0},{2,1},{3,2},{4,7},{5,4},{6,5},{7,6},{8,11},{9,8},{10,9... | collective-permute-start | bytes 1474568 | tf_op jit(solution)/shard_map/ppermute | solution.py:667
  14.7 21.5 %copy-start.29 = (bf16[384,640]{1,0:T(8,128)(2,1)S(1)}, bf16[384,640]{1,0:T(8,128)(2,1)}, u32[]{:S(2)}) copy-start(bf16[384,640]{1,0:T(8,128)(2,1)} %refs_0_.3) | copy-start | bytes 1474564
  23.6 12.6 %copy-start.15 = (bf16[384,640]{1,0:T(8,128)(2,1)}, bf16[384,640]{1,0:T(8,128)(2,1)S(1)}, u32[]{:S(2)}) copy-start(bf16[384,640]{1,0:T(8,128)(2,1)S(1)} %collective-permute-done.refs_1_) | copy-start | bytes 1474564
  23.6 12.6 %copy-start.18 = (bf16[384,640]{1,0:T(8,128)(2,1)}, bf16[384,640]{1,0:T(8,128)(2,1)S(1)}, u32[]{:S(2)}) copy-start(bf16[384,640]{1,0:T(8,128)(2,1)S(1)} %collective-permute-done.1.refs_2_) | copy-start | bytes 1474564
  23.7 27.1 %collective-permute-start.2 = (bf16[384,640]{1,0:T(8,128)(2,1)S(1)}, bf16[384,640]{1,0:T(8,128)(2,1)S(1)}, u32[]{:S(2)}, u32[]{:S(2)}) collective-permute-start(bf16[384,640]{1,0:T(8,128)(2,1)S(1)} %broadcast_select_fusion.1), channel_id=1, source_target_pairs={{0,1},{1,2},{2,3},{3,0},{4,7},{5,4},{6,5},{7,6},{8,9},{9,10},{10,1... | collective-permute-start | bytes 1474568 | tf_op jit(solution)/shard_map/ppermute | solution.py:667
  34.2 19.7 %collective-permute-start.5 = (bf16[384,640]{1,0:T(8,128)(2,1)S(1)}, bf16[384,640]{1,0:T(8,128)(2,1)S(1)}, u32[]{:S(2)}, u32[]{:S(2)}) collective-permute-start(bf16[384,640]{1,0:T(8,128)(2,1)S(1)} %broadcast_select_fusion), channel_id=1, source_target_pairs={{0,1},{1,2},{2,3},{3,0},{4,7},{5,4},{6,5},{7,6},{8,9},{9,10},{10,1... | collective-permute-start | bytes 1474568 | tf_op jit(solution)/shard_map/ppermute | solution.py:667
  44.1 4.6 %copy-start.8 = (bf16[640,2560]{1,0:T(8,128)(2,1)S(1)}, bf16[640,2560]{1,0:T(8,128)(2,1)}, u32[]{:S(2)}) copy-start(bf16[640,2560]{1,0:T(8,128)(2,1)} %weight_ref.5) | copy-start | bytes 9830404
  44.1 4.7 %copy-start.22 = (bf16[384,640]{1,0:T(8,128)(2,1)S(1)}, bf16[384,640]{1,0:T(8,128)(2,1)}, u32[]{:S(2)}) copy-start(bf16[384,640]{1,0:T(8,128)(2,1)} %copy-done.21) | copy-start | bytes 1474564
  44.1 4.7 %copy-start.25 = (bf16[384,640]{1,0:T(8,128)(2,1)S(1)}, bf16[384,640]{1,0:T(8,128)(2,1)}, u32[]{:S(2)}) copy-start(bf16[384,640]{1,0:T(8,128)(2,1)} %copy-done.24) | copy-start | bytes 1474564
  44.1 4.7 %copy-start.35 = (bf16[384,640]{1,0:T(8,128)(2,1)S(1)}, bf16[384,640]{1,0:T(8,128)(2,1)}, u32[]{:S(2)}) copy-start(bf16[384,640]{1,0:T(8,128)(2,1)} %refs_4_.3) | copy-start | bytes 1474564
  44.1 6.8 %copy-start.6 = (bf16[2560,640]{1,0:T(8,128)(2,1)S(1)}, bf16[2560,640]{1,0:T(8,128)(2,1)}, u32[]{:S(2)}) copy-start(bf16[2560,640]{1,0:T(8,128)(2,1)} %refs_7_.1) | copy-start | bytes 9830404
  48.8 2.9 %copy-start.3 = (bf16[2560,640]{1,0:T(8,128)(2,1)S(1)}, bf16[2560,640]{1,0:T(8,128)(2,1)}, u32[]{:S(2)}) copy-start(bf16[2560,640]{1,0:T(8,128)(2,1)} %refs_9_.1) | copy-start | bytes 9830404
  50.9 3.0 %copy-start.31 = (bf16[384,640]{1,0:T(8,128)(2,1)}, bf16[384,640]{1,0:T(8,128)(2,1)S(1)}, u32[]{:S(2)}) copy-start(bf16[384,640]{1,0:T(8,128)(2,1)S(1)} %collective-permute-done.2.shard_ref.refs_3_) | copy-start | bytes 1474564
  57.2 30.6 %all-to-all-start = ((bf16[32,60,384]{2,1,0:T(8,128)(2,1)}), bf16[32,60,384]{2,1,0:T(8,128)(2,1)}, u32[]{:S(2)}, u32[]{:S(2)}) async-start(bf16[32,60,384]{2,1,0:T(8,128)(2,1)} %copy-done.46), calls=%async_computation | async-start | bytes 3145728 | tf_op jit(solution)/shard_map/all_to_all | solution.py:755
  108.7 30.0 %all-to-all-start.1 = ((bf16[32,67,384]{2,1,0:T(8,128)(2,1)}), bf16[32,67,384]{2,1,0:T(8,128)(2,1)}, u32[]{:S(2)}, u32[]{:S(2)}) async-start(bf16[32,67,384]{2,1,0:T(8,128)(2,1)} %copy-done.13), calls=%async_computation.1 | async-start | bytes 3538944 | tf_op jit(solution)/shard_map/all_to_all | solution.py:755
  113.5 144.9 %reduce-scatter.3.cloned.1.call-start = ((), (), s32[]{:S(2)}) async-start(), calls=%async_computation.4 | async-start | bytes 2457600 | tf_op jit(solution)/shard_map/reduce_scatter | solution.py:776
  140.8 3.2 %copy-start.59 = (bf16[4,640,384]{2,1,0:T(8,128)(2,1)S(1)}, bf16[4,640,384]{2,1,0:T(8,128)(2,1)}, u32[]{:S(2)}) copy-start(bf16[4,640,384]{2,1,0:T(8,128)(2,1)} %copy-done.58) | copy-start | bytes 5898244
  144.0 6.4 %copy-start.48 = (bf16[384,640]{1,0:T(8,128)(2,1)}, bf16[384,640]{1,0:T(8,128)(2,1)S(1)}, u32[]{:S(2)}) copy-start(bf16[384,640]{1,0:T(8,128)(2,1)S(1)} %get-tuple-element.42.refs_0_.refs_4_) | copy-start | bytes 1474564
  144.0 6.4 %copy-start.50 = (bf16[384,640]{1,0:T(8,128)(2,1)}, bf16[384,640]{1,0:T(8,128)(2,1)S(1)}, u32[]{:S(2)}) copy-start(bf16[384,640]{1,0:T(8,128)(2,1)S(1)} %get-tuple-element.43.refs_1_.refs_5_) | copy-start | bytes 1474564
  144.0 6.4 %copy-start.52 = (bf16[384,640]{1,0:T(8,128)(2,1)}, bf16[384,640]{1,0:T(8,128)(2,1)S(1)}, u32[]{:S(2)}) copy-start(bf16[384,640]{1,0:T(8,128)(2,1)S(1)} %get-tuple-element.44.refs_2_.refs_6_) | copy-start | bytes 1474564
  144.0 6.4 %copy-start.57 = (bf16[4,640,384]{2,1,0:T(8,128)(2,1)S(1)}, bf16[4,640,384]{2,1,0:T(8,128)(2,1)}, u32[]{:S(2)}) copy-start(bf16[4,640,384]{2,1,0:T(8,128)(2,1)} %copy-done.56) | copy-start | bytes 5898244
  150.3 14.8 %copy-start.62 = (bf16[16,80,640]{2,1,0:T(8,128)(2,1)}, bf16[16,80,640]{2,1,0:T(8,128)(2,1)S(1)}, u32[]{:S(2)}) copy-start(bf16[16,80,640]{2,1,0:T(8,128)(2,1)S(1)} %get-tuple-element.40.after_ref) | copy-start | bytes 4915204
  150.3 20.7 %copy-start.9 = (bf16[640,2560]{1,0:T(8,128)(2,1)S(1)}, bf16[640,2560]{1,0:T(8,128)(2,1)}, u32[]{:S(2)}) copy-start(bf16[640,2560]{1,0:T(8,128)(2,1)} %weight_ref.5) | copy-start | bytes 9830404
  177.4 81.0 %reduce-scatter.5.cloned.1.call-start = ((), (), s32[]{:S(2)}) async-start(), calls=%async_computation.5 | async-start | bytes 2457600 | tf_op jit(solution)/shard_map/reduce_scatter | solution.py:784
  177.4 3.9 %collective-permute-start.6 = (bf16[16,80,640]{2,1,0:T(8,128)(2,1)}, bf16[16,80,640]{2,1,0:T(8,128)(2,1)}, u32[]{:S(2)}, u32[]{:S(2)}) collective-permute-start(bf16[16,80,640]{2,1,0:T(8,128)(2,1)} %copy-done.62), channel_id=1, source_target_pairs={{0,4},{1,5},{2,6},{3,7},{4,0},{5,1},{6,2},{7,3},{8,12},{9,13},{10,... | collective-permute-start | bytes 4915208 | tf_op jit(solution)/shard_map/ppermute | solution.py:667
  177.5 6.2 %collective-permute-start.21 = (bf16[16,80,640]{2,1,0:T(8,128)(2,1)}, bf16[16,80,640]{2,1,0:T(8,128)(2,1)}, u32[]{:S(2)}, u32[]{:S(2)}) collective-permute-start(bf16[16,80,640]{2,1,0:T(8,128)(2,1)} %copy-done.61), channel_id=1, source_target_pairs={{0,4},{1,5},{2,6},{3,7},{4,0},{5,1},{6,2},{7,3},{8,12},{9,13},{10,... | collective-permute-start | bytes 4915208 | tf_op jit(solution)/shard_map/ppermute | solution.py:667
  178.0 8.0 %collective-permute-start.8 = (bf16[16,80,640]{2,1,0:T(8,128)(2,1)}, bf16[16,80,640]{2,1,0:T(8,128)(2,1)}, u32[]{:S(2)}, u32[]{:S(2)}) collective-permute-start(bf16[16,80,640]{2,1,0:T(8,128)(2,1)} %copy-done.60), channel_id=1, source_target_pairs={{0,4},{1,5},{2,6},{3,7},{4,0},{5,1},{6,2},{7,3},{8,12},{9,13},{10,... | collective-permute-start | bytes 4915208 | tf_op jit(solution)/shard_map/ppermute | solution.py:667
  178.1 10.7 %collective-permute-start.7 = (bf16[16,80,640]{2,1,0:T(8,128)(2,1)}, bf16[16,80,640]{2,1,0:T(8,128)(2,1)}, u32[]{:S(2)}, u32[]{:S(2)}) collective-permute-start(bf16[16,80,640]{2,1,0:T(8,128)(2,1)} %copy-done.37), channel_id=1, source_target_pairs={{0,4},{1,5},{2,6},{3,7},{4,0},{5,1},{6,2},{7,3},{8,12},{9,13},{10,... | collective-permute-start | bytes 4915208 | tf_op jit(solution)/shard_map/ppermute | solution.py:667
  181.3 10.1 %copy-start.49 = (bf16[384,640]{1,0:T(8,128)(2,1)S(1)}, bf16[384,640]{1,0:T(8,128)(2,1)}, u32[]{:S(2)}) copy-start(bf16[384,640]{1,0:T(8,128)(2,1)} %copy-done.48) | copy-start | bytes 1474564
  181.3 10.1 %copy-start.51 = (bf16[384,640]{1,0:T(8,128)(2,1)S(1)}, bf16[384,640]{1,0:T(8,128)(2,1)}, u32[]{:S(2)}) copy-start(bf16[384,640]{1,0:T(8,128)(2,1)} %copy-done.50) | copy-start | bytes 1474564
  181.3 10.1 %copy-start.53 = (bf16[384,640]{1,0:T(8,128)(2,1)S(1)}, bf16[384,640]{1,0:T(8,128)(2,1)}, u32[]{:S(2)}) copy-start(bf16[384,640]{1,0:T(8,128)(2,1)} %copy-done.52) | copy-start | bytes 1474564
  183.4 20.2 %collective-permute-start.28 = (bf16[4,80,640]{2,1,0:T(8,128)(2,1)}, bf16[4,80,640]{2,1,0:T(8,128)(2,1)}, u32[]{:S(2)}, u32[]{:S(2)}) collective-permute-start(bf16[4,80,640]{2,1,0:T(8,128)(2,1)} %fusion.24), channel_id=1, source_target_pairs={{0,32},{1,33},{2,34},{3,35},{4,100},{5,101},{6,102},{7,103},{8,40}... | collective-permute-start | bytes 1228808 | tf_op jit(solution)/shard_map/ppermute | solution.py:667
  183.7 7.8 %copy-start.4 = (bf16[2560,640]{1,0:T(8,128)(2,1)S(1)}, bf16[2560,640]{1,0:T(8,128)(2,1)}, u32[]{:S(2)}) copy-start(bf16[2560,640]{1,0:T(8,128)(2,1)} %refs_9_.1) | copy-start | bytes 9830404
  185.8 21.1 %collective-permute-start.22 = (bf16[4,80,640]{2,1,0:T(8,128)(2,1)}, bf16[4,80,640]{2,1,0:T(8,128)(2,1)}, u32[]{:S(2)}, u32[]{:S(2)}) collective-permute-start(bf16[4,80,640]{2,1,0:T(8,128)(2,1)} %fusion.20), channel_id=1, source_target_pairs={{0,8},{1,9},{2,10},{3,11},{4,28},{5,29},{6,30},{7,31},{8,16},{9,17... | collective-permute-start | bytes 1228808 | tf_op jit(solution)/shard_map/ppermute | solution.py:667
  188.0 21.8 %collective-permute-start.15 = (bf16[4,80,640]{2,1,0:T(8,128)(2,1)}, bf16[4,80,640]{2,1,0:T(8,128)(2,1)}, u32[]{:S(2)}, u32[]{:S(2)}) collective-permute-start(bf16[4,80,640]{2,1,0:T(8,128)(2,1)} %fusion.16), channel_id=1, source_target_pairs={{0,32},{1,33},{2,34},{3,35},{4,100},{5,101},{6,102},{7,103},{8,40}... | collective-permute-start | bytes 1228808 | tf_op jit(solution)/shard_map/ppermute | solution.py:667
  190.8 22.3 %collective-permute-start.9 = (bf16[4,80,640]{2,1,0:T(8,128)(2,1)}, bf16[4,80,640]{2,1,0:T(8,128)(2,1)}, u32[]{:S(2)}, u32[]{:S(2)}) collective-permute-start(bf16[4,80,640]{2,1,0:T(8,128)(2,1)} %fusion.12), channel_id=1, source_target_pairs={{0,8},{1,9},{2,10},{3,11},{4,28},{5,29},{6,30},{7,31},{8,16},{9,17... | collective-permute-start | bytes 1228808 | tf_op jit(solution)/shard_map/ppermute | solution.py:667
  203.6 6.1 %copy-start.41 = (bf16[16,80,640]{2,1,0:T(8,128)(2,1)S(1)}, bf16[16,80,640]{2,1,0:T(8,128)(2,1)}, u32[]{:S(2)}) copy-start(bf16[16,80,640]{2,1,0:T(8,128)(2,1)} %copy-done.40) | copy-start | bytes 4915204
  205.2 8.0 %copy-start.39 = (bf16[16,80,640]{2,1,0:T(8,128)(2,1)S(1)}, bf16[16,80,640]{2,1,0:T(8,128)(2,1)}, u32[]{:S(2)}) copy-start(bf16[16,80,640]{2,1,0:T(8,128)(2,1)} %copy-done.38) | copy-start | bytes 4915204
  205.2 11.7 %collective-permute-start.29 = (bf16[4,80,640]{2,1,0:T(8,128)(2,1)S(1)}, bf16[4,80,640]{2,1,0:T(8,128)(2,1)S(1)}, u32[]{:S(2)}, u32[]{:S(2)}) collective-permute-start(bf16[4,80,640]{2,1,0:T(8,128)(2,1)S(1)} %fusion.2), channel_id=1, source_target_pairs={{0,32},{1,33},{2,34},{3,35},{4,100},{5,101},{6,102},{7,103},{8,40}... | collective-permute-start | bytes 1228808 | tf_op jit(solution)/shard_map/ppermute | solution.py:667
  208.3 8.6 %copy-start.45 = (bf16[16,80,640]{2,1,0:T(8,128)(2,1)S(1)}, bf16[16,80,640]{2,1,0:T(8,128)(2,1)}, u32[]{:S(2)}) copy-start(bf16[16,80,640]{2,1,0:T(8,128)(2,1)} %copy-done.44) | copy-start | bytes 4915204
  208.3 10.2 %collective-permute-start.23 = (bf16[4,80,640]{2,1,0:T(8,128)(2,1)S(1)}, bf16[4,80,640]{2,1,0:T(8,128)(2,1)S(1)}, u32[]{:S(2)}, u32[]{:S(2)}) collective-permute-start(bf16[4,80,640]{2,1,0:T(8,128)(2,1)S(1)} %fusion.5), channel_id=1, source_target_pairs={{0,8},{1,9},{2,10},{3,11},{4,28},{5,29},{6,30},{7,31},{8,16},{9,17... | collective-permute-start | bytes 1228808 | tf_op jit(solution)/shard_map/ppermute | solution.py:667
  211.0 7.5 %copy-start.43 = (bf16[16,80,640]{2,1,0:T(8,128)(2,1)S(1)}, bf16[16,80,640]{2,1,0:T(8,128)(2,1)}, u32[]{:S(2)}) copy-start(bf16[16,80,640]{2,1,0:T(8,128)(2,1)} %copy-done.42) | copy-start | bytes 4915204
  211.1 9.2 %collective-permute-start.16 = (bf16[4,80,640]{2,1,0:T(8,128)(2,1)S(1)}, bf16[4,80,640]{2,1,0:T(8,128)(2,1)S(1)}, u32[]{:S(2)}, u32[]{:S(2)}) collective-permute-start(bf16[4,80,640]{2,1,0:T(8,128)(2,1)S(1)} %fusion.8), channel_id=1, source_target_pairs={{0,32},{1,33},{2,34},{3,35},{4,100},{5,101},{6,102},{7,103},{8,40}... | collective-permute-start | bytes 1228808 | tf_op jit(solution)/shard_map/ppermute | solution.py:667
  214.4 9.2 %collective-permute-start.10 = (bf16[4,80,640]{2,1,0:T(8,128)(2,1)S(1)}, bf16[4,80,640]{2,1,0:T(8,128)(2,1)S(1)}, u32[]{:S(2)}, u32[]{:S(2)}) collective-permute-start(bf16[4,80,640]{2,1,0:T(8,128)(2,1)S(1)} %fusion.11), channel_id=1, source_target_pairs={{0,8},{1,9},{2,10},{3,11},{4,28},{5,29},{6,30},{7,31},{8,16},{9,17... | collective-permute-start | bytes 1228808 | tf_op jit(solution)/shard_map/ppermute | solution.py:667
  218.1 9.2 %collective-permute-start.30 = (bf16[4,80,640]{2,1,0:T(8,128)(2,1)S(1)}, bf16[4,80,640]{2,1,0:T(8,128)(2,1)S(1)}, u32[]{:S(2)}, u32[]{:S(2)}) collective-permute-start(bf16[4,80,640]{2,1,0:T(8,128)(2,1)S(1)} %fusion.1), channel_id=1, source_target_pairs={{0,32},{1,33},{2,34},{3,35},{4,100},{5,101},{6,102},{7,103},{8,40}... | collective-permute-start | bytes 1228808 | tf_op jit(solution)/shard_map/ppermute | solution.py:667
  219.7 12.1 %collective-permute-start.24 = (bf16[4,80,640]{2,1,0:T(8,128)(2,1)S(1)}, bf16[4,80,640]{2,1,0:T(8,128)(2,1)S(1)}, u32[]{:S(2)}, u32[]{:S(2)}) collective-permute-start(bf16[4,80,640]{2,1,0:T(8,128)(2,1)S(1)} %fusion.4), channel_id=1, source_target_pairs={{0,8},{1,9},{2,10},{3,11},{4,28},{5,29},{6,30},{7,31},{8,16},{9,17... | collective-permute-start | bytes 1228808 | tf_op jit(solution)/shard_map/ppermute | solution.py:667
  221.5 11.6 %collective-permute-start.17 = (bf16[4,80,640]{2,1,0:T(8,128)(2,1)S(1)}, bf16[4,80,640]{2,1,0:T(8,128)(2,1)S(1)}, u32[]{:S(2)}, u32[]{:S(2)}) collective-permute-start(bf16[4,80,640]{2,1,0:T(8,128)(2,1)S(1)} %fusion.7), channel_id=1, source_target_pairs={{0,32},{1,33},{2,34},{3,35},{4,100},{5,101},{6,102},{7,103},{8,40}... | collective-permute-start | bytes 1228808 | tf_op jit(solution)/shard_map/ppermute | solution.py:667
  224.8 11.3 %collective-permute-start.11 = (bf16[4,80,640]{2,1,0:T(8,128)(2,1)S(1)}, bf16[4,80,640]{2,1,0:T(8,128)(2,1)S(1)}, u32[]{:S(2)}, u32[]{:S(2)}) collective-permute-start(bf16[4,80,640]{2,1,0:T(8,128)(2,1)S(1)} %fusion.10), channel_id=1, source_target_pairs={{0,8},{1,9},{2,10},{3,11},{4,28},{5,29},{6,30},{7,31},{8,16},{9,17... | collective-permute-start | bytes 1228808 | tf_op jit(solution)/shard_map/ppermute | solution.py:667
  228.5 11.1 %collective-permute-start.31 = (bf16[80,640]{1,0:T(8,128)(2,1)S(1)}, bf16[80,640]{1,0:T(8,128)(2,1)S(1)}, u32[]{:S(2)}, u32[]{:S(2)}) collective-permute-start(bf16[80,640]{1,0:T(8,128)(2,1)S(1)} %get-tuple-element.54), channel_id=1, source_target_pairs={{0,8},{1,9},{2,10},{3,11},{4,12},{5,13},{6,14},{7,15},{8,16},{9,17... | collective-permute-start | bytes 307208 | tf_op jit(solution)/shard_map/ppermute | solution.py:667
  228.7 11.1 %collective-permute-start.32 = (bf16[80,640]{1,0:T(8,128)(2,1)S(1)}, bf16[80,640]{1,0:T(8,128)(2,1)S(1)}, u32[]{:S(2)}, u32[]{:S(2)}) collective-permute-start(bf16[80,640]{1,0:T(8,128)(2,1)S(1)} %get-tuple-element.56), channel_id=1, source_target_pairs={{0,24},{1,25},{2,26},{3,27},{4,28},{5,29},{6,30},{7,31},{8,0},{9,1... | collective-permute-start | bytes 307208 | tf_op jit(solution)/shard_map/ppermute | solution.py:667
  231.8 11.1 %collective-permute-start.33 = (bf16[80,640]{1,0:T(8,128)(2,1)S(1)}, bf16[80,640]{1,0:T(8,128)(2,1)S(1)}, u32[]{:S(2)}, u32[]{:S(2)}) collective-permute-start(bf16[80,640]{1,0:T(8,128)(2,1)S(1)} %get-tuple-element.55), channel_id=1, source_target_pairs={{0,16},{1,17},{2,18},{3,19},{4,20},{5,21},{6,22},{7,23},{8,24},{9,... | collective-permute-start | bytes 307208 | tf_op jit(solution)/shard_map/ppermute | solution.py:667
  233.1 18.4 %collective-permute-start.25 = (bf16[80,640]{1,0:T(8,128)(2,1)S(1)}, bf16[80,640]{1,0:T(8,128)(2,1)S(1)}, u32[]{:S(2)}, u32[]{:S(2)}) collective-permute-start(bf16[80,640]{1,0:T(8,128)(2,1)S(1)} %get-tuple-element.57), channel_id=1, source_target_pairs={{0,32},{1,33},{2,34},{3,35},{4,36},{5,37},{6,38},{7,39},{8,40},{9,... | collective-permute-start | bytes 307208 | tf_op jit(solution)/shard_map/ppermute | solution.py:667
  236.1 15.7 %collective-permute-start.26 = (bf16[80,640]{1,0:T(8,128)(2,1)S(1)}, bf16[80,640]{1,0:T(8,128)(2,1)S(1)}, u32[]{:S(2)}, u32[]{:S(2)}) collective-permute-start(bf16[80,640]{1,0:T(8,128)(2,1)S(1)} %get-tuple-element.59), channel_id=1, source_target_pairs={{0,96},{1,97},{2,98},{3,99},{4,100},{5,101},{6,102},{7,103},{8,104... | collective-permute-start | bytes 307208 | tf_op jit(solution)/shard_map/ppermute | solution.py:667
  239.6 5.9 %collective-permute-start.18 = (bf16[80,640]{1,0:T(8,128)(2,1)S(1)}, bf16[80,640]{1,0:T(8,128)(2,1)S(1)}, u32[]{:S(2)}, u32[]{:S(2)}) collective-permute-start(bf16[80,640]{1,0:T(8,128)(2,1)S(1)} %get-tuple-element.60), channel_id=1, source_target_pairs={{0,8},{1,9},{2,10},{3,11},{4,12},{5,13},{6,14},{7,15},{8,16},{9,17... | collective-permute-start | bytes 307208 | tf_op jit(solution)/shard_map/ppermute | solution.py:667
  239.8 6.5 %collective-permute-start.19 = (bf16[80,640]{1,0:T(8,128)(2,1)S(1)}, bf16[80,640]{1,0:T(8,128)(2,1)S(1)}, u32[]{:S(2)}, u32[]{:S(2)}) collective-permute-start(bf16[80,640]{1,0:T(8,128)(2,1)S(1)} %get-tuple-element.62), channel_id=1, source_target_pairs={{0,24},{1,25},{2,26},{3,27},{4,28},{5,29},{6,30},{7,31},{8,0},{9,1... | collective-permute-start | bytes 307208 | tf_op jit(solution)/shard_map/ppermute | solution.py:667
  242.9 6.2 %collective-permute-start.20 = (bf16[80,640]{1,0:T(8,128)(2,1)S(1)}, bf16[80,640]{1,0:T(8,128)(2,1)S(1)}, u32[]{:S(2)}, u32[]{:S(2)}) collective-permute-start(bf16[80,640]{1,0:T(8,128)(2,1)S(1)} %get-tuple-element.61), channel_id=1, source_target_pairs={{0,16},{1,17},{2,18},{3,19},{4,20},{5,21},{6,22},{7,23},{8,24},{9,... | collective-permute-start | bytes 307208 | tf_op jit(solution)/shard_map/ppermute | solution.py:667
  245.5 6.3 %collective-permute-start.27 = (bf16[80,640]{1,0:T(8,128)(2,1)S(1)}, bf16[80,640]{1,0:T(8,128)(2,1)S(1)}, u32[]{:S(2)}, u32[]{:S(2)}) collective-permute-start(bf16[80,640]{1,0:T(8,128)(2,1)S(1)} %get-tuple-element.58), channel_id=1, source_target_pairs={{0,64},{1,65},{2,66},{3,67},{4,68},{5,69},{6,70},{7,71},{8,72},{9,... | collective-permute-start | bytes 307208 | tf_op jit(solution)/shard_map/ppermute | solution.py:667
  246.3 6.5 %collective-permute-start.12 = (bf16[80,640]{1,0:T(8,128)(2,1)S(1)}, bf16[80,640]{1,0:T(8,128)(2,1)S(1)}, u32[]{:S(2)}, u32[]{:S(2)}) collective-permute-start(bf16[80,640]{1,0:T(8,128)(2,1)S(1)} %get-tuple-element.63), channel_id=1, source_target_pairs={{0,32},{1,33},{2,34},{3,35},{4,36},{5,37},{6,38},{7,39},{8,40},{9,... | collective-permute-start | bytes 307208 | tf_op jit(solution)/shard_map/ppermute | solution.py:667
  249.1 4.7 %collective-permute-start.13 = (bf16[80,640]{1,0:T(8,128)(2,1)S(1)}, bf16[80,640]{1,0:T(8,128)(2,1)S(1)}, u32[]{:S(2)}, u32[]{:S(2)}) collective-permute-start(bf16[80,640]{1,0:T(8,128)(2,1)S(1)} %get-tuple-element.65), channel_id=1, source_target_pairs={{0,96},{1,97},{2,98},{3,99},{4,100},{5,101},{6,102},{7,103},{8,104... | collective-permute-start | bytes 307208 | tf_op jit(solution)/shard_map/ppermute | solution.py:667
  251.5 6.2 %collective-permute-start.14 = (bf16[80,640]{1,0:T(8,128)(2,1)S(1)}, bf16[80,640]{1,0:T(8,128)(2,1)S(1)}, u32[]{:S(2)}, u32[]{:S(2)}) collective-permute-start(bf16[80,640]{1,0:T(8,128)(2,1)S(1)} %get-tuple-element.64), channel_id=1, source_target_pairs={{0,64},{1,65},{2,66},{3,67},{4,68},{5,69},{6,70},{7,71},{8,72},{9,... | collective-permute-start | bytes 307208 | tf_op jit(solution)/shard_map/ppermute | solution.py:667
  (38 other events, 51.0 us)
Sparse Core Ops, SparseCore 0:
  177.5 26.0 reduce-scatter.2
  206.6 28.5 reduce-scatter.4

commit v2 on v1

--- a/solution.py
+++ b/solution.py
@@ -61,6 +61,9 @@
 
 def anywhere(count):
     return [pl.BlockSpec(memory_space=pl.ANY)] * count
+
+
+TICK = jax.ShapeDtypeStruct((8, LANE), F32)
 
 
 def padded(rows):
@@ -238,7 +241,8 @@
 
 
 def sequence_kernel(
-    group, in_ref, rows_ref, cols_ref, taps_ref, skip_ref, out_ref, in_rows, out_rows, small_rows,
+    group, after_ref, in_ref, rows_ref, cols_ref, taps_ref, skip_ref, out_ref, in_rows, out_rows,
+    small_rows,
 ):
     sources, _, width = in_ref.shape
     parts = width // LANE
@@ -273,7 +277,7 @@
     lax.fori_loop(0, sources, pack, 0)
 
 
-def sequence_part(value, rows, cols, taps, skip):
+def sequence_part(after, value, rows, cols, taps, skip):
     sources, triple, width = value.shape
     group = triple // 3
     parts = width // LANE
@@ -282,7 +286,7 @@
     return pl.pallas_call(
         functools.partial(sequence_kernel, group),
         out_shape=jax.ShapeDtypeStruct((sources, triple + extra, width), BF16),
-        in_specs=in_vmem(4) + in_smem(1),
+        in_specs=anywhere(1) + in_vmem(4) + in_smem(1),
         out_specs=in_vmem(1)[0],
         scratch_shapes=[
             pltpu.VMEM((lines * padded(triple), LANE), F32),
@@ -291,7 +295,7 @@
         ],
         compiler_params=params(24),
         cost_estimate=call_cost(22_000_000_000, 5_000_000),
-    )(value, rows, cols, taps, skip)
+    )(after, value, rows, cols, taps, skip)
 
 
 def tiles_of(count, body):
@@ -488,8 +492,9 @@
 
 
 def turn_kernel(after_ref, *refs):
-    count = (len(refs) - 5) // 2
-    shards, (first_out, second_out, first, second, sems) = refs[:-5], refs[-5:]
+    count = (len(refs) - 6) // 2
+    shards, (first_out, second_out, tick_ref, first, second, sems) = refs[:-6], refs[-6:]
+    tick_ref[...] = jnp.zeros_like(tick_ref)
     held = ((first, first_out), (second, second_out))
     sent = []
     for index, ref in enumerate(shards):
@@ -511,138 +516,117 @@
     return pl.pallas_call(
         turn_kernel,
         in_specs=anywhere(1) + in_vmem(2 * count),
-        out_specs=tuple(in_hbm(2)),
-        out_shape=(out, out),
+        out_specs=tuple(in_hbm(2) + in_vmem(1)),
+        out_shape=(out, out, TICK),
         scratch_shapes=[pltpu.VMEM(out.shape, BF16)] * 2 + [pltpu.SemaphoreType.DMA((2, count))],
         compiler_params=params(16),
         cost_estimate=call_cost(2 * count * depth * rows, 8_000_000),
     )(after, *first, *second)
 
 
-def weight_kernel(rows, count, after_ref, wide_ref, *refs):
-    narrows, (ids_ref, core_ref), refs = refs[:count], refs[count : count + 2], refs[count + 2 :]
-    outs, (keep, send, sems) = refs[: 2 * count], refs[2 * count :]
-    tiles, held = keep.shape[1:3]
-
-    def copies(tile, index):
-        at = pl.ds(ids_ref[tile] * held, held)
-        return (
-            pltpu.make_async_copy(
-                keep.at[index, tile], outs[2 * index].at[at], sems.at[0, index, tile]
-            ),
-            pltpu.make_async_copy(
-                send.at[index, tile], outs[2 * index + 1].at[at], sems.at[1, index, tile]
-            ),
-        )
+def hold_kernel(after_ref, *refs):
+    count = (len(refs) - 1) // 2
+    sources, targets, sems = refs[:count], refs[count:-1], refs[-1]
+    copies = [
+        pltpu.make_async_copy(source, target, sems.at[index])
+        for index, (source, target) in enumerate(zip(sources, targets))
+    ]
+    for copy in copies:
+        copy.start()
+    for copy in copies:
+        copy.wait()
+
+
+def held_in_vmem(after, values):
+    count = len(values)
+    return pl.pallas_call(
+        hold_kernel,
+        in_specs=anywhere(1) + in_hbm(count),
+        out_specs=tuple(in_vmem(count)),
+        out_shape=tuple(jax.ShapeDtypeStruct(value.shape, value.dtype) for value in values),
+        scratch_shapes=[pltpu.SemaphoreType.DMA((count,))],
+        compiler_params=params(16),
+        cost_estimate=call_cost(0, 26_000_000),
+    )(after, *values)
+
+
+def weight_kernel(
+    rows, after_ref, wide_ref, narrow_ref, ids_ref, core_ref, keep_ref, send_ref, tick_ref
+):
+    tick_ref[...] = jnp.zeros_like(tick_ref)
+    tiles = wide_ref.shape[0]
+    held = keep_ref.shape[0] // tiles
 
     def multiply(tile):
-        for index in range(count):
-            result = dot_nn(wide_ref[tile], narrows[index][...]).astype(BF16)
-            for core in range(2):
-
-                @pl.when(core_ref[0] == core)
-                def _():
-                    for chip in range(held):
-                        at = (2 * chip + core) * rows
-                        other = (2 * chip + 1 - core) * rows
-                        keep[index, tile, chip] = result[at : at + rows]
-                        send[index, tile, chip] = result[other : other + rows]
-
-            for copy in copies(tile, index):
-                copy.start()
-
-    def finish(tile):
-        for index in range(count):
-            for copy in copies(tile, index):
-                copy.wait()
+        result = dot_nn(wide_ref[tile], narrow_ref[...]).astype(BF16)
+        first = ids_ref[tile] * held
+        for core in range(2):
+
+            @pl.when(core_ref[0] == core)
+            def _():
+                for chip in range(held):
+                    at = (2 * chip + core) * rows
+                    other = (2 * chip + 1 - core) * rows
+                    keep_ref[first + chip] = result[at : at + rows]
+                    send_ref[first + chip] = result[other : other + rows]
 
     tiles_of(tiles, multiply)
-    tiles_of(tiles, finish)
-
-
-def weight_partial(after, wide, ids, narrows, core, chips):
+
+
+def weight_partial(after, wide, ids, narrow, core, chips):
     tiles, height, depth = wide.shape
-    width = narrows[0].shape[1]
+    width = narrow.shape[1]
     total = tiles * height
     rows = total // (2 * chips)
-    count = len(narrows)
-    halves = pltpu.VMEM((count, tiles, chips // tiles, rows, width), BF16)
-    flat = pl.pallas_call(
-        functools.partial(weight_kernel, rows, count),
-        in_specs=anywhere(1) + in_vmem(1 + count) + in_smem(2),
-        out_specs=tuple(in_hbm(2 * count)),
-        out_shape=(jax.ShapeDtypeStruct((chips, rows, width), BF16),) * (2 * count),
-        scratch_shapes=[halves, halves, pltpu.SemaphoreType.DMA((2, count, tiles))],
-        compiler_params=params(12 + 6 * count),
-        cost_estimate=call_cost(2 * count * total * depth * width, 6_000_000 * count),
-    )(after, wide, *narrows, ids, core)
-    return [flat[2 * index : 2 * index + 2] for index in range(count)]
-
-
-def mixed_kernel(after_ref, gated_ref, weight_ref, out_ref, result, sems):
-    count, _, width = out_ref.shape
+    return pl.pallas_call(
+        functools.partial(weight_kernel, rows),
+        in_specs=anywhere(1) + in_vmem(2) + in_smem(2),
+        out_specs=tuple(in_vmem(3)),
+        out_shape=(jax.ShapeDtypeStruct((chips, rows, width), BF16),) * 2 + (TICK,),
+        compiler_params=params(14),
+        cost_estimate=call_cost(2 * total * depth * width, 6_000_000),
+    )(after, wide, narrow, ids, core)
+
+
+def outward_kernel(unread, *refs):
+    (
+        query_ref, key_ref, value_ref, gated_ref, query_weight, key_weight, value_weight,
+        out_weight, out_ref, result, sems,
+    ) = refs[unread:]
+    count, height, width = out_ref.shape
+    rows = height // 2
 
     def copy_out(tile):
         return pltpu.make_async_copy(result.at[tile], out_ref.at[tile], sems.at[tile])
 
     def multiply(tile):
-        result[tile] = dot_nn(gated_ref[...], weight_ref[:, columns_of(tile, width)]).astype(BF16)
+        result[tile, :rows] = dot_nn(
+            gated_ref[...], out_weight[:, columns_of(tile, width)]
+        ).astype(BF16)
+        at = rows_of(tile, width)
+        total = dot_nt(query_ref[...], query_weight[at, :])
+        total += dot_nt(key_ref[...], key_weight[at, :])
+        total += dot_nt(value_ref[...], value_weight[at, :])
+        result[tile, rows:] = total.astype(BF16)
         copy_out(tile).start()
 
     tiles_of(count, multiply)
     tiles_of(count, lambda tile: copy_out(tile).wait())
 
 
-def mixed_part(after, gated, w_out, count):
+def outward_part(after, backs, gated, weights, count):
     rows, depth = gated.shape
-    width = w_out.shape[1] // count
-    return pl.pallas_call(
-        mixed_kernel,
-        in_specs=anywhere(1) + in_vmem(2),
+    width = weights[0].shape[0] // count
+    shape = (count, 2 * rows, width)
+    return pl.pallas_call(
+        functools.partial(outward_kernel, len(after)),
+        in_specs=anywhere(len(after)) + in_vmem(8),
         out_specs=in_hbm(1)[0],
-        out_shape=jax.ShapeDtypeStruct((count, rows, width), BF16),
-        scratch_shapes=[
-            pltpu.VMEM((count, rows, width), BF16), pltpu.SemaphoreType.DMA((count,)),
-        ],
-        compiler_params=params(14),
-        cost_estimate=call_cost(2 * rows * depth * width * count, 6_000_000),
-    )(after, gated, w_out)
-
-
-def input_kernel(unread, *refs):
-    *pairs, out_ref, result, sems = refs[unread:]
-    half = len(pairs) // 2
-    count, _, width = out_ref.shape
-
-    def copy_out(tile):
-        return pltpu.make_async_copy(result.at[tile], out_ref.at[tile], sems.at[tile])
-
-    def multiply(tile):
-        at = rows_of(tile, width)
-        total = dot_nt(pairs[0][...], pairs[half][at, :])
-        for index in range(1, half):
-            total += dot_nt(pairs[index][...], pairs[half + index][at, :])
-        result[tile] = total.astype(BF16)
-        copy_out(tile).start()
-
-    tiles_of(count, multiply)
-    tiles_of(count, lambda tile: copy_out(tile).wait())
-
-
-def input_part(after, backs, weights, count):
-    rows, depth = backs[0].shape
-    width = weights[0].shape[0] // count
-    return pl.pallas_call(
-        functools.partial(input_kernel, len(after)),
-        in_specs=anywhere(len(after)) + in_vmem(len(backs) + len(weights)),
-        out_specs=in_hbm(1)[0],
-        out_shape=jax.ShapeDtypeStruct((count, rows, width), BF16),
-        scratch_shapes=[
-            pltpu.VMEM((count, rows, width), BF16), pltpu.SemaphoreType.DMA((count,)),
-        ],
-        compiler_params=params(22),
-        cost_estimate=call_cost(6 * rows * depth * width * count, 14_000_000),
-    )(*after, *backs, *weights)
+        out_shape=jax.ShapeDtypeStruct(shape, BF16),
+        scratch_shapes=[pltpu.VMEM(shape, BF16), pltpu.SemaphoreType.DMA((count,))],
+        compiler_params=params(24),
+        cost_estimate=call_cost(8 * rows * depth * width * count, 20_000_000),
+    )(*after, *backs, gated, *weights)
 
 
 def moved(value, axis, steps):
@@ -681,26 +665,36 @@
     return travelling
 
 
-def summed_over_seq(halves, first, places, up):
-    keep, came = halves
-    _, rows, width = keep.shape
-    grid = (SIDE, SIDE, rows, width)
-    axis = "xy".index(first)
-    second = "yx"[axis]
-    keep = picked(keep.reshape(grid), axis)
-    came = picked(came.reshape(grid), axis)
-
-    def block(index):
-        return added(keep(index), came(index))
-
-    place = places[first]
-    half = ring_sum(block((place - up) % SIDE), block, place, up, first, range(2, SIDE + 1))
-    place, mine = places[second], picked(half)
-    total = mine(place).astype(F32)
+class FirstAxis:
+    def __init__(self, halves, first, places, up):
+        keep, came = halves
+        _, rows, width = keep.shape
+        grid = (SIDE, SIDE, rows, width)
+        axis = "xy".index(first)
+        self.keep, self.came = picked(keep.reshape(grid), axis), picked(came.reshape(grid), axis)
+        self.first, self.place, self.up = first, places[first], up
+        self.start = self.block((self.place - up) % SIDE)
+
+    def block(self, index):
+        return added(self.keep(index), self.came(index))
+
+    def total(self):
+        return ring_sum(
+            self.start, self.block, self.place, self.up, self.first, range(2, SIDE + 1)
+        )
+
+
+def second_axis_sums(halves, second, places):
+    place = places[second]
+
+    def mine(step):
+        return jnp.stack([picked(half)((place + step) % SIDE) for half in halves])
+
+    total = mine(0).astype(F32)
     for step in (1, -1, 2):
         steps = (2, -2) if step == 2 else step
-        total += moved(mine((place + step) % SIDE), second, steps).astype(F32)
-    return total
+        total += moved(mine(step), second, steps).astype(F32)
+    return [total[index] for index in range(len(halves))]
 
 
 def per_device(
@@ -730,13 +724,16 @@
     token_sides = moved(tokens, "z", 1), moved(tokens, "z", -1)
     grad_sides = moved(cotangent, "z", 1), moved(cotangent, "z", -1)
 
-    def all_shards(mine, sides):
+    def passed(sides):
         below, above = sides
-        far = moved(jnp.where(core == 0, below, above), "z", (1, -1))
-        return mine, below, above, far
-
-    shards = all_shards(tokens, token_sides)
-    grad_shards = all_shards(cotangent, grad_sides)
+        return jnp.where(core == 0, below, above)
+
+    held = held_in_vmem(skip_gain, (w_key, w_value, w_query, w_out))
+    tokens_on, _ = lax.optimization_barrier((passed(token_sides), held[0]))
+    grad_sides, tokens_on = lax.optimization_barrier((grad_sides, tokens_on))
+    grads_on = passed(grad_sides)
+    shards = (tokens, *token_sides, moved(tokens_on, "z", (1, -1)))
+    grad_shards = (cotangent, *grad_sides, moved(grads_on, "z", (1, -1)))
     ids = (chip_z + jnp.array([0, SIDE - 1, 1, 2], jnp.int32)) % SIDE
 
     def own(value):
@@ -754,13 +751,13 @@
     def exchanged(value):
         return lax.all_to_all(value, "seq", 0, 0, tiled=True)
 
-    weights = (w_key, w_value, w_query)
+    weights = held[:3]
     sums = near_part(shards[:3], weights, ids)
-    grad_sum = grad_near_part(sums[2], grad_shards[:3], w_out, ids)
+    grad_sum = grad_near_part(sums[2], grad_shards[:3], held[3], ids)
     kv, query = far_part(shards[3], weights, sums, ids, seq_count)
-    gated_grad, packed = grad_far_part(kv, grad_shards[3], w_out, grad_sum, query, ids)
-    results = sequence_part(exchanged(packed), rows, cols, taps, skip)
-    shards_turned, grad_turned = turn_part(results, shards, grad_shards)
+    gated_grad, packed = grad_far_part(kv, grad_shards[3], held[3], grad_sum, query, ids)
+    shards_turned, grad_turned, turned = turn_part(packed, shards, grad_shards)
+    results = sequence_part(turned, exchanged(packed), rows, cols, taps, skip)
     returned = exchanged(results)
     gated, back_query, back_key, back_value, grad_filter, grad_init = unpack_part(
         returned, query, gated_grad, tap_count
@@ -768,24 +765,27 @@
     chips = SIDE * SIDE
     up = 1 - 2 * core
 
-    (out_halves,) = weight_partial(gated, grad_turned, ids, (gated,), core_word, chips)
-    query_halves, key_halves, value_halves = weight_partial(
-        out_halves[1], shards_turned, ids, (back_query, back_key, back_value), core_word, chips
+    after = gated
+    swapped = []
+    for wide, narrow in (
+        (grad_turned, gated), (shards_turned, back_query), (shards_turned, back_key),
+        (shards_turned, back_value),
+    ):
+        keep, send, after = weight_partial(after, wide, ids, narrow, core_word, chips)
+        swapped.append((keep, moved(send, "core", 1)))
+    sums = [FirstAxis(pair, first, places, up) for pair, first in zip(swapped, "xyxy")]
+    outward = outward_part(
+        tuple(each.start for each in sums),
+        (back_query, back_key, back_value),
+        gated,
+        (w_query, w_key, w_value, w_out),
+        SIDE,
     )
-    partial_mixed = mixed_part(query_halves[1], gated, w_out, SIDE)
-    mixed = lax.psum_scatter(partial_mixed, "tp", scatter_dimension=0, tiled=True)[0]
-    swapped = [
-        (keep, moved(send, "core", 1))
-        for keep, send in (out_halves, query_halves, key_halves, value_halves)
-    ]
-    partial_input = input_part(
-        (partial_mixed, swapped[0][1], swapped[1][1], swapped[2][1]), (back_query, back_key, back_value), (w_query, w_key, w_value), SIDE
-    )
-    grad_input = lax.psum_scatter(partial_input, "tp", scatter_dimension=0, tiled=True)[0]
-    grad_out, grad_query, grad_key, grad_value = (
-        summed_over_seq(halves, first, places, up)
-        for halves, first in zip(swapped, "xyxy")
-    )
+    outward = lax.psum_scatter(outward, "tp", scatter_dimension=0, tiled=True)[0]
+    mixed, grad_input = outward[:row_count], outward[row_count:]
+    halves = [each.total() for each in sums]
+    grad_out, grad_key = second_axis_sums(halves[0::2], "y", places)
+    grad_query, grad_value = second_axis_sums(halves[1::2], "x", places)
     grad_out = grad_out.T
     return (mixed, grad_input, grad_query, grad_key, grad_value, grad_out, grad_filter, grad_init)
 

time: 267 us -> 249 us (0.933)
  blocking collectives: 0 us -> 27.7 us
  starting transfers between devices: 52.8 us -> 34.7 us
  waiting for transfers between devices: 58 us -> 45.4 us
  local copies, waits for them, and re-layouts: 47 us -> 39.9 us
  other arithmetic: 26.1 us -> 21.2 us
    all_to_all x0 -> x1, blocking collectives: none -> 27.7 us  [exchanged(): return lax.all_to_all(value, 'seq', 0, 0, tiled=True)]
    all_to_all x2 -> x1, waiting for transfers between devices: 26.9 us -> 6.06 us  [exchanged(): return lax.all_to_all(value, 'seq', 0, 0, tiled=True)]
    ppermute x34 -> x28, starting transfers between devices: 40.4 us -> 27.1 us  [moved(): return lax.ppermute(value, ('seq', 'tp'), pairs)]
    unnamed x132 -> x98, local copies, waits for them, and re-layouts: 42.3 us -> 30.8 us
    ppermute x34 -> x28, waiting for transfers between devices: 31.1 us -> 39.3 us  [moved(): return lax.ppermute(value, ('seq', 'tp'), pairs)]
    all_to_all x2 -> x1, starting transfers between devices: 12.3 us -> 7.43 us  [exchanged(): return lax.all_to_all(value, 'seq', 0, 0, tiled=True)]
    convert_element_type x16, other arithmetic: 23 us -> 19.9 us  [added(): return (left.astype(F32) + right.astype(F32)).astype(BF16)]
    pallas_call x4 -> x6, Pallas kernels: 30.9 us -> 28.8 us  [the longest x4 18.2 us: weight_partial(): pl.pallas_call(functools.partial(weight_kernel, rows), in_specs=anywhere(...]
  transfers between devices with their start and end apart: 38 -> 30, of which waited for: 17 -> 14; matrix products, arithmetic and copies ran while one was open for 12% -> 12% of each run, Pallas kernels for 8% -> 11%
where the time goes in v2:
time: 249 us; the launch traced here: 248 us
  Pallas kernels  64.2 us (26%)
  waiting for transfers between devices  45.4 us (18%)
  local copies, waits for them, and re-layouts  39.9 us (16%)
  starting transfers between devices  34.7 us (14%)
  blocking collectives  27.7 us (11%)
  other arithmetic  21.2 us (9%)
  between operations  14.6 us (6%)
    ppermute x28, waiting for transfers between devices, moved(): return lax.ppermute(value, ('seq', 'tp'), pairs)  39.3 us
    unnamed x98, local copies, waits for them, and re-layouts  30.8 us
    all_to_all x1, blocking collectives, exchanged(): return lax.all_to_all(value, 'seq', 0, 0, tiled=True)  27.7 us
    ppermute x28, starting transfers between devices, moved(): return lax.ppermute(value, ('seq', 'tp'), pairs)  27.1 us
    convert_element_type x16, other arithmetic, added(): return (left.astype(F32) + right.astype(F32)).astype(BF16)  19.9 us
    pallas_call x1, Pallas kernels, sequence_part(): pl.pallas_call(functools.partial(sequence_kernel, group), out_shape=jax.S...  18.4 us
    pallas_call x4, Pallas kernels, weight_partial(): pl.pallas_call(functools.partial(weight_kernel, rows), in_specs=anywhere(...  18.2 us
    pallas_call x1, Pallas kernels, outward_part(): pl.pallas_call(functools.partial(outward_kernel, len(after)), in_specs=an...  9.09 us
  transfers between devices with their start and end apart: 30, of which 14 were waited for; matrix products, arithmetic and copies ran while one was open for 12% of the time, Pallas kernels for 11%

profile of v2, /device:TPU:0, one launch (start us, length us, event | category | flops | bytes accessed | tf_op | source)
XLA Modules:
  0.0 247.7 jit_solution(3171337343817406934)
XLA Ops:
  7.2 2.1 collective-permute-start.2
  9.2 2.2 collective-permute-start.3
  11.4 3.2 %collective-permute-start.1 = (bf16[384,640]{1,0:T(8,128)(2,1)}, bf16[384,640]{1,0:T(8,128)(2,1)S(1)}, u32[]{:S(2)}, u32[]{:S(2)}) collective-permute-start(bf16[384,640]{1,0:T(8,128)(2,1)} %refs_4_.1), channel_id=1, source_target_pairs={{0,3},{1,0},{2,1},{3,2},{4,7},{5,4},{6,5},{7,6},{8,11},{9,8},{10,9... | collective-permute-start | bytes 1474568 | tf_op jit(solution)/shard_map/ppermute | solution.py:651
  14.7 1.9 copy-done.1
  16.6 1.9 copy-done.3
  18.5 1.9 copy-done.5
  20.5 1.9 copy-done.7
  23.1 1.6 shard_map.179
  24.8 8.6 %collective-permute-done.second_ref.refs_5_ = bf16[384,640]{1,0:T(8,128)(2,1)S(1)} collective-permute-done((bf16[384,640]{1,0:T(8,128)(2,1)}, bf16[384,640]{1,0:T(8,128)(2,1)S(1)}, u32[]{:S(2)}, u32[]{:S(2)}) %collective-permute-start) | collective-permute-done | bytes 491552 | tf_op jit(solution)/shard_map/ppermute | solution.py:651
  33.3 1.3 collective-permute-start.4
  34.6 1.7 collective-permute-start.5
  36.4 4.6 %shard_map.180 = (f32[384,640]{1,0:T(8,128)S(1)}, f32[384,640]{1,0:T(8,128)S(1)}, f32[384,640]{1,0:T(8,128)S(1)}) custom-call(bf16[384,640]{1,0:T(8,128)(2,1)S(1)} %copy-done.9, bf16[384,640]{1,0:T(8,128)(2,1)S(1)} %collective-permute-done.2.refs_1_, bf16[384,640]{1,0:T(8,128)(2,1)S(1)} %collective-permute-done.3.refs_2_, ...), custom_call_target="tpu_custom_call" | custom-call | flops 2831155200 | bytes 12000000 | tf_op jit(solution)/shard_map/pallas_call | solution.py:336
  41.0 2.0 shard_map.182.sum_ref
  43.4 2.1 shard_map.181
  45.5 3.1 %collective-permute-done.5.shard_ref.refs_7_ = bf16[384,640]{1,0:T(8,128)(2,1)S(1)} collective-permute-done((bf16[384,640]{1,0:T(8,128)(2,1)S(1)}, bf16[384,640]{1,0:T(8,128)(2,1)S(1)}, u32[]{:S(2)}, u32[]{:S(2)}) %collective-permute-start.5) | collective-permute-done | bytes 491552 | tf_op jit(solution)/shard_map/ppermute | solution.py:651
  48.6 2.6 %shard_map.183 = (bf16[384,640]{1,0:T(8,128)(2,1)S(1)}, bf16[32,60,384]{2,1,0:T(8,128)(2,1)}) custom-call(bf16[32,40,384]{2,1,0:T(8,128)(2,1)S(1)} %get-tuple-element.51.kv_ref, bf16[384,640]{1,0:T(8,128)(2,1)S(1)} %collective-permute-done.5.shard_ref.refs_7_, bf16[640,2560]{1,0:T(8,128)(2,1)S(1)} %get-tuple-element.54.weight_ref, ...), custom_call_target="tpu_custom_call" | custom-call | flops 314572800 | bytes 6000000 | tf_op jit(solution)/shard_map/pallas_call | solution.py:432
  52.0 7.4 %all-to-all-start = ((bf16[32,60,384]{2,1,0:T(8,128)(2,1)}), bf16[32,60,384]{2,1,0:T(8,128)(2,1)}, u32[]{:S(2)}, u32[]{:S(2)}) async-start(bf16[32,60,384]{2,1,0:T(8,128)(2,1)} %get-tuple-element.56.after_ref), calls=%async_computation | async-start | bytes 3145728 | tf_op jit(solution)/shard_map/all_to_all | solution.py:752
  61.5 1.6 constant_dynamic-slice_fusion.16
  63.1 1.4 copy.50
  65.9 1.6 copy.29.cols_ref
  69.9 4.0 %shard_map.184 = (bf16[4,640,384]{2,1,0:T(8,128)(2,1)S(1)}, bf16[4,640,384]{2,1,0:T(8,128)(2,1)S(1)}, f32[8,128]{1,0:T(8,128)S(1)}) custom-call(bf16[32,60,384]{2,1,0:T(8,128)(2,1)} %get-tuple-element.56.after_ref, bf16[384,640]{1,0:T(8,128)(2,1)S(1)} %copy-done.9, bf16[384,640]{1,0:T(8,128)(2,1)S(1)} %collective-permute-done.2.refs_1_, ...), custom_call_target="tpu_custom_call" | custom-call | flops 1966080 | bytes 8000000 | tf_op jit(solution)/shard_map/pallas_call | solution.py:516
  73.9 1.3 copy-done.42
  75.2 1.3 copy-done.44
  76.5 6.1 %all-to-all-done.in_ref = bf16[32,60,384]{2,1,0:T(8,128)(2,1)} async-done(((bf16[32,60,384]{2,1,0:T(8,128)(2,1)}), bf16[32,60,384]{2,1,0:T(8,128)(2,1)}, u32[]{:S(2)}, u32[]{:S(2)}) %all-to-all-start) | async-done | bytes 1474592 | tf_op jit(solution)/shard_map/all_to_all | solution.py:752
  82.6 1.3 copy-done.30
  83.9 18.4 %shard_map.185 = bf16[32,67,384]{2,1,0:T(8,128)(2,1)S(1)} custom-call(f32[8,128]{1,0:T(8,128)S(1)} %get-tuple-element.57.after_ref, bf16[32,60,384]{2,1,0:T(8,128)(2,1)} %all-to-all-done.in_ref, f32[2,20,64]{2,1,0:T(8,128)S(1)} %get-tuple-element.101.rows_ref, f32[2,20,64,1]{3,2,1,0:T(8,128)S(1)} %copy-done.30, ...), custom_call_target="tpu_custom_call" | custom-call | flops 22000001024 | bytes 5000000 | tf_op jit(solution)/shard_map/pallas_call | solution.py:286
  102.3 27.7 %all_to_all.10.returned_ref = bf16[32,67,384]{2,1,0:T(8,128)(2,1)S(1)} all-to-all(bf16[32,67,384]{2,1,0:T(8,128)(2,1)S(1)} %shard_map.185), channel_id=1, replica_groups=mesh['seq'=32,'tp'=4] {'seq'}, dimensions={0} | all-to-all | bytes 3293184 | tf_op jit(solution)/shard_map/all_to_all | solution.py:752
  130.1 1.5 shard_map.186
  131.6 4.5 %shard_map.187 = (bf16[16,80,640]{2,1,0:T(8,128)(2,1)S(1)}, bf16[16,80,640]{2,1,0:T(8,128)(2,1)}, f32[8,128]{1,0:T(8,128)S(1)}) custom-call(bf16[384,640]{1,0:T(8,128)(2,1)S(1)} %get-tuple-element.59.after_ref.narrow_ref.refs_7_, bf16[4,640,384]{2,1,0:T(8,128)(2,1)S(1)} %copy-done.45, bf16[384,640]{1,0:T(8,128)(2,1)S(1)} %get-tuple-element.59.after_ref.narrow_ref.refs_7_, ...), custom_call_target="tpu_custom_call" | custom-call | flops 1258291200 | bytes 6000000 | tf_op jit(solution)/shard_map/pallas_call | solution.py:581
  136.1 1.2 copy-done.22
  138.0 4.6 %shard_map.188 = (bf16[16,80,640]{2,1,0:T(8,128)(2,1)S(1)}, bf16[16,80,640]{2,1,0:T(8,128)(2,1)}, f32[8,128]{1,0:T(8,128)S(1)}) custom-call(f32[8,128]{1,0:T(8,128)S(1)} %get-tuple-element.63.after_ref, bf16[4,640,384]{2,1,0:T(8,128)(2,1)S(1)} %copy-done.43, bf16[384,640]{1,0:T(8,128)(2,1)S(1)} %get-tuple-element.65.narrow_ref.refs_4_, ...), custom_call_target="tpu_custom_call" | custom-call | flops 1258291200 | bytes 6000000 | tf_op jit(solution)/shard_map/pallas_call | solution.py:581
  142.6 1.3 copy-done.26
  143.8 4.5 %shard_map.189 = (bf16[16,80,640]{2,1,0:T(8,128)(2,1)S(1)}, bf16[16,80,640]{2,1,0:T(8,128)(2,1)}, f32[8,128]{1,0:T(8,128)S(1)}) custom-call(f32[8,128]{1,0:T(8,128)S(1)} %get-tuple-element.68.after_ref, bf16[4,640,384]{2,1,0:T(8,128)(2,1)S(1)} %copy-done.43, bf16[384,640]{1,0:T(8,128)(2,1)S(1)} %get-tuple-element.69.narrow_ref.refs_5_, ...), custom_call_target="tpu_custom_call" | custom-call | flops 1258291200 | bytes 6000000 | tf_op jit(solution)/shard_map/pallas_call | solution.py:581
  148.4 1.2 copy-done.24
  150.0 4.6 %shard_map.190 = (bf16[16,80,640]{2,1,0:T(8,128)(2,1)S(1)}, bf16[16,80,640]{2,1,0:T(8,128)(2,1)}, f32[8,128]{1,0:T(8,128)}) custom-call(f32[8,128]{1,0:T(8,128)S(1)} %get-tuple-element.72.after_ref, bf16[4,640,384]{2,1,0:T(8,128)(2,1)S(1)} %copy-done.43, bf16[384,640]{1,0:T(8,128)(2,1)S(1)} %get-tuple-element.73.narrow_ref.refs_6_, ...), custom_call_target="tpu_custom_call" | custom-call | flops 1258291200 | bytes 6000000 | tf_op jit(solution)/shard_map/pallas_call | solution.py:581
  154.6 1.2 copy-done.28
  155.8 1.3 fusion.12.refs_0_
  157.2 1.4 fusion.14.refs_2_
  158.6 1.4 fusion.13.refs_1_
  160.0 1.4 fusion.15.refs_3_
  161.5 1.9 copy-done.6
  163.4 1.9 copy-done.8
  166.3 9.1 %shard_map.191 = bf16[4,768,640]{2,1,0:T(8,128)(2,1)S(1)} custom-call(bf16[4,80,640]{2,1,0:T(8,128)(2,1)S(1)} %fusion.12.refs_0_, bf16[4,80,640]{2,1,0:T(8,128)(2,1)S(1)} %fusion.13.refs_1_, bf16[4,80,640]{2,1,0:T(8,128)(2,1)S(1)} %fusion.14.refs_2_, bf16[4,80,640]{2,1,0:T(8,128)(2,1)S(1)} %fusion.15.refs_3_, bf16[384,640]{1,0:T(8,128)(2,1)S(1)} %copy-done.34, ...), custom_call_target="tpu_custom_call" | custom-call | flops 5033164800 | bytes 20000000 | tf_op jit(solution)/shard_map/pallas_call | solution.py:621
  175.5 1.9 copy-done
  181.6 6.7 %collective-permute-done.13 = bf16[4,80,640]{2,1,0:T(8,128)(2,1)} collective-permute-done((bf16[4,80,640]{2,1,0:T(8,128)(2,1)S(1)}, bf16[4,80,640]{2,1,0:T(8,128)(2,1)}, u32[]{:S(2)}, u32[]{:S(2)}) %collective-permute-start.13) | collective-permute-done | bytes 409632 | tf_op jit(solution)/shard_map/ppermute | solution.py:651
  188.4 1.4 fusion.8
  189.9 2.9 %collective-permute-done.10 = bf16[4,80,640]{2,1,0:T(8,128)(2,1)} collective-permute-done((bf16[4,80,640]{2,1,0:T(8,128)(2,1)S(1)}, bf16[4,80,640]{2,1,0:T(8,128)(2,1)}, u32[]{:S(2)}, u32[]{:S(2)}) %collective-permute-start.10) | collective-permute-done | bytes 409632 | tf_op jit(solution)/shard_map/ppermute | solution.py:651
  192.8 1.3 fusion.11
  194.2 1.3 fusion.2
  195.6 1.2 fusion.5
  196.8 1.4 collective-permute-start.20
  199.0 1.2 fusion.7
  200.3 3.1 %collective-permute-done.11 = bf16[4,80,640]{2,1,0:T(8,128)(2,1)S(1)} collective-permute-done((bf16[4,80,640]{2,1,0:T(8,128)(2,1)S(1)}, bf16[4,80,640]{2,1,0:T(8,128)(2,1)S(1)}, u32[]{:S(2)}, u32[]{:S(2)}) %collective-permute-start.11) | collective-permute-done | bytes 409632 | tf_op jit(solution)/shard_map/ppermute | solution.py:651
  203.4 1.2 fusion.10
  206.0 3.0 %collective-permute-done.20 = bf16[4,80,640]{2,1,0:T(8,128)(2,1)S(1)} collective-permute-done((bf16[4,80,640]{2,1,0:T(8,128)(2,1)S(1)}, bf16[4,80,640]{2,1,0:T(8,128)(2,1)S(1)}, u32[]{:S(2)}, u32[]{:S(2)}) %collective-permute-start.20) | collective-permute-done | bytes 409632 | tf_op jit(solution)/shard_map/ppermute | solution.py:651
  210.3 1.2 fusion.6
  211.5 2.3 collective-permute-done.12
  215.1 2.5 %collective-permute-start.18 = (bf16[2,80,640]{2,1,0:T(8,128)(2,1)S(1)}, bf16[2,80,640]{2,1,0:T(8,128)(2,1)S(1)}, u32[]{:S(2)}, u32[]{:S(2)}) collective-permute-start(bf16[2,80,640]{2,1,0:T(8,128)(2,1)S(1)} %pad_maximum_fusion.2), channel_id=1, source_target_pairs={{0,64},{1,65},{2,66},{3,67},{4,68},{5,69},{6,70},{7,71},{8,72},{9,... | collective-permute-start | bytes 614408 | tf_op jit(solution)/shard_map/ppermute | solution.py:651
  218.1 1.7 collective-permute-start.16
  221.0 3.2 %collective-permute-done.21 = bf16[4,80,640]{2,1,0:T(8,128)(2,1)S(1)} collective-permute-done((bf16[4,80,640]{2,1,0:T(8,128)(2,1)S(1)}, bf16[4,80,640]{2,1,0:T(8,128)(2,1)S(1)}, u32[]{:S(2)}, u32[]{:S(2)}) %collective-permute-start.21) | collective-permute-done | bytes 409632 | tf_op jit(solution)/shard_map/ppermute | solution.py:651
  225.5 3.3 %collective-permute-start.27 = (bf16[2,80,640]{2,1,0:T(8,128)(2,1)S(1)}, bf16[2,80,640]{2,1,0:T(8,128)(2,1)S(1)}, u32[]{:S(2)}, u32[]{:S(2)}) collective-permute-start(bf16[2,80,640]{2,1,0:T(8,128)(2,1)S(1)} %pad_maximum_fusion.5), channel_id=1, source_target_pairs={{0,16},{1,17},{2,18},{3,19},{4,20},{5,21},{6,22},{7,23},{8,24},{9,... | collective-permute-start | bytes 614408 | tf_op jit(solution)/shard_map/ppermute | solution.py:651
  228.8 1.9 collective-permute-start.26
  232.8 4.6 %collective-permute-done.26 = bf16[2,80,640]{2,1,0:T(8,128)(2,1)S(1)} collective-permute-done((bf16[2,80,640]{2,1,0:T(8,128)(2,1)S(1)}, bf16[2,80,640]{2,1,0:T(8,128)(2,1)S(1)}, u32[]{:S(2)}, u32[]{:S(2)}) %collective-permute-start.26) | collective-permute-done | bytes 204832 | tf_op jit(solution)/shard_map/ppermute | solution.py:651
  238.7 2.2 slice_bitcast_fusion
  (153 shorter events, 26.0 us)
Async XLA Ops:
  7.2 17.5 %collective-permute-start.2 = (bf16[384,640]{1,0:T(8,128)(2,1)}, bf16[384,640]{1,0:T(8,128)(2,1)S(1)}, u32[]{:S(2)}, u32[]{:S(2)}) collective-permute-start(bf16[384,640]{1,0:T(8,128)(2,1)} %refs_0_.5), channel_id=1, source_target_pairs={{0,1},{1,2},{2,3},{3,0},{4,5},{5,6},{6,7},{7,4},{8,9},{9,10},{10,1... | collective-permute-start | bytes 1474568 | tf_op jit(solution)/shard_map/ppermute | solution.py:651
  9.2 15.5 %collective-permute-start.3 = (bf16[384,640]{1,0:T(8,128)(2,1)}, bf16[384,640]{1,0:T(8,128)(2,1)S(1)}, u32[]{:S(2)}, u32[]{:S(2)}) collective-permute-start(bf16[384,640]{1,0:T(8,128)(2,1)} %refs_0_.5), channel_id=1, source_target_pairs={{0,3},{1,0},{2,1},{3,2},{4,7},{5,4},{6,5},{7,6},{8,11},{9,8},{10,9... | collective-permute-start | bytes 1474568 | tf_op jit(solution)/shard_map/ppermute | solution.py:651
  11.4 21.9 %collective-permute-start = (bf16[384,640]{1,0:T(8,128)(2,1)}, bf16[384,640]{1,0:T(8,128)(2,1)S(1)}, u32[]{:S(2)}, u32[]{:S(2)}) collective-permute-start(bf16[384,640]{1,0:T(8,128)(2,1)} %refs_4_.1), channel_id=1, source_target_pairs={{0,1},{1,2},{2,3},{3,0},{4,5},{5,6},{6,7},{7,4},{8,9},{9,10},{10,1... | collective-permute-start | bytes 1474568 | tf_op jit(solution)/shard_map/ppermute | solution.py:651
  11.4 21.9 %collective-permute-start.1 = (bf16[384,640]{1,0:T(8,128)(2,1)}, bf16[384,640]{1,0:T(8,128)(2,1)S(1)}, u32[]{:S(2)}, u32[]{:S(2)}) collective-permute-start(bf16[384,640]{1,0:T(8,128)(2,1)} %refs_4_.1), channel_id=1, source_target_pairs={{0,3},{1,0},{2,1},{3,2},{4,7},{5,4},{6,5},{7,6},{8,11},{9,8},{10,9... | collective-permute-start | bytes 1474568 | tf_op jit(solution)/shard_map/ppermute | solution.py:651
  14.7 1.9 copy-start.1
  16.6 1.9 copy-start.3
  18.5 1.9 copy-start.5
  20.5 1.9 copy-start.7
  24.6 11.7 %copy-start.46 = (s32[4]{0:T(128)S(1)}, s32[4]{0:T(128)}, u32[]{:S(2)}) copy-start(s32[4]{0:T(128)} %constant.271.clone) | copy-start | bytes 52
  24.7 11.7 %copy-start.9 = (bf16[384,640]{1,0:T(8,128)(2,1)S(1)}, bf16[384,640]{1,0:T(8,128)(2,1)}, u32[]{:S(2)}) copy-start(bf16[384,640]{1,0:T(8,128)(2,1)} %refs_0_.5) | copy-start | bytes 1474564
  33.3 10.0 %collective-permute-start.4 = (bf16[384,640]{1,0:T(8,128)(2,1)S(1)}, bf16[384,640]{1,0:T(8,128)(2,1)S(1)}, u32[]{:S(2)}, u32[]{:S(2)}) collective-permute-start(bf16[384,640]{1,0:T(8,128)(2,1)S(1)} %broadcast_select_fusion.1), channel_id=1, source_target_pairs={{0,1},{1,2},{2,3},{3,0},{4,7},{5,4},{6,5},{7,6},{8,9},{9,10},{10,1... | collective-permute-start | bytes 1474568 | tf_op jit(solution)/shard_map/ppermute | solution.py:651
  34.6 14.0 %collective-permute-start.5 = (bf16[384,640]{1,0:T(8,128)(2,1)S(1)}, bf16[384,640]{1,0:T(8,128)(2,1)S(1)}, u32[]{:S(2)}, u32[]{:S(2)}) collective-permute-start(bf16[384,640]{1,0:T(8,128)(2,1)S(1)} %broadcast_select_fusion), channel_id=1, source_target_pairs={{0,1},{1,2},{2,3},{3,0},{4,7},{5,4},{6,5},{7,6},{8,9},{9,10},{10,1... | collective-permute-start | bytes 1474568 | tf_op jit(solution)/shard_map/ppermute | solution.py:651
  36.4 4.6 %copy-start.12 = (bf16[384,640]{1,0:T(8,128)(2,1)S(1)}, bf16[384,640]{1,0:T(8,128)(2,1)}, u32[]{:S(2)}) copy-start(bf16[384,640]{1,0:T(8,128)(2,1)} %refs_4_.1) | copy-start | bytes 1474564
  48.6 2.6 %copy-start.10 = (bf16[384,640]{1,0:T(8,128)(2,1)}, bf16[384,640]{1,0:T(8,128)(2,1)S(1)}, u32[]{:S(2)}) copy-start(bf16[384,640]{1,0:T(8,128)(2,1)S(1)} %collective-permute-done.5.shard_ref.refs_7_) | copy-start | bytes 1474564
  52.0 30.6 %all-to-all-start = ((bf16[32,60,384]{2,1,0:T(8,128)(2,1)}), bf16[32,60,384]{2,1,0:T(8,128)(2,1)}, u32[]{:S(2)}, u32[]{:S(2)}) async-start(bf16[32,60,384]{2,1,0:T(8,128)(2,1)} %get-tuple-element.56.after_ref), calls=%async_computation | async-start | bytes 3145728 | tf_op jit(solution)/shard_map/all_to_all | solution.py:752
  59.5 179.2 %reduce-scatter.2.cloned.1.call-start = ((), (), s32[]{:S(2)}) async-start(), calls=%async_computation.3 | async-start | bytes 4915200 | tf_op jit(solution)/shard_map/reduce_scatter | solution.py:784
  73.9 1.3 copy-start.42
  102.3 27.8 %copy-start.40 = (bf16[384,640]{1,0:T(8,128)(2,1)S(1)}, bf16[384,640]{1,0:T(8,128)(2,1)}, u32[]{:S(2)}) copy-start(bf16[384,640]{1,0:T(8,128)(2,1)} %copy-done.39) | copy-start | bytes 1474564
  130.1 1.5 copy-start.45
  131.6 4.6 %copy-start.31 = (bf16[384,640]{1,0:T(8,128)(2,1)}, bf16[384,640]{1,0:T(8,128)(2,1)S(1)}, u32[]{:S(2)}) copy-start(bf16[384,640]{1,0:T(8,128)(2,1)S(1)} %get-tuple-element.59.after_ref.narrow_ref.refs_7_) | copy-start | bytes 1474564
  131.6 6.4 %copy-start.33 = (bf16[384,640]{1,0:T(8,128)(2,1)}, bf16[384,640]{1,0:T(8,128)(2,1)S(1)}, u32[]{:S(2)}) copy-start(bf16[384,640]{1,0:T(8,128)(2,1)S(1)} %get-tuple-element.65.narrow_ref.refs_4_) | copy-start | bytes 1474564
  131.6 12.2 %copy-start.35 = (bf16[384,640]{1,0:T(8,128)(2,1)}, bf16[384,640]{1,0:T(8,128)(2,1)S(1)}, u32[]{:S(2)}) copy-start(bf16[384,640]{1,0:T(8,128)(2,1)S(1)} %get-tuple-element.69.narrow_ref.refs_5_) | copy-start | bytes 1474564
  131.6 18.4 %copy-start.37 = (bf16[384,640]{1,0:T(8,128)(2,1)}, bf16[384,640]{1,0:T(8,128)(2,1)S(1)}, u32[]{:S(2)}) copy-start(bf16[384,640]{1,0:T(8,128)(2,1)S(1)} %get-tuple-element.73.narrow_ref.refs_6_) | copy-start | bytes 1474564
  131.6 6.4 %copy-start.43 = (bf16[4,640,384]{2,1,0:T(8,128)(2,1)S(1)}, bf16[4,640,384]{2,1,0:T(8,128)(2,1)}, u32[]{:S(2)}) copy-start(bf16[4,640,384]{2,1,0:T(8,128)(2,1)} %copy-done.42) | copy-start | bytes 5898244
  137.3 18.4 %collective-permute-start.6 = (bf16[16,80,640]{2,1,0:T(8,128)(2,1)}, bf16[16,80,640]{2,1,0:T(8,128)(2,1)}, u32[]{:S(2)}, u32[]{:S(2)}) collective-permute-start(bf16[16,80,640]{2,1,0:T(8,128)(2,1)} %get-tuple-element.62), channel_id=1, source_target_pairs={{0,4},{1,5},{2,6},{3,7},{4,0},{5,1},{6,2},{7,3},{8,12},{9,13},{10,... | collective-permute-start | bytes 4915208 | tf_op jit(solution)/shard_map/ppermute | solution.py:651
  149.5 7.6 %collective-permute-start.8 = (bf16[16,80,640]{2,1,0:T(8,128)(2,1)}, bf16[16,80,640]{2,1,0:T(8,128)(2,1)}, u32[]{:S(2)}, u32[]{:S(2)}) collective-permute-start(bf16[16,80,640]{2,1,0:T(8,128)(2,1)} %get-tuple-element.71), channel_id=1, source_target_pairs={{0,4},{1,5},{2,6},{3,7},{4,0},{5,1},{6,2},{7,3},{8,12},{9,13},{10,... | collective-permute-start | bytes 4915208 | tf_op jit(solution)/shard_map/ppermute | solution.py:651
  149.5 9.1 %collective-permute-start.7 = (bf16[16,80,640]{2,1,0:T(8,128)(2,1)}, bf16[16,80,640]{2,1,0:T(8,128)(2,1)}, u32[]{:S(2)}, u32[]{:S(2)}) collective-permute-start(bf16[16,80,640]{2,1,0:T(8,128)(2,1)} %get-tuple-element.67), channel_id=1, source_target_pairs={{0,4},{1,5},{2,6},{3,7},{4,0},{5,1},{6,2},{7,3},{8,12},{9,13},{10,... | collective-permute-start | bytes 4915208 | tf_op jit(solution)/shard_map/ppermute | solution.py:651
  150.0 11.4 %copy-start.4 = (bf16[2560,640]{1,0:T(8,128)(2,1)S(1)}, bf16[2560,640]{1,0:T(8,128)(2,1)}, u32[]{:S(2)}) copy-start(bf16[2560,640]{1,0:T(8,128)(2,1)} %refs_10_.1) | copy-start | bytes 9830404
  155.8 4.2 %collective-permute-start.9 = (bf16[16,80,640]{2,1,0:T(8,128)(2,1)}, bf16[16,80,640]{2,1,0:T(8,128)(2,1)}, u32[]{:S(2)}, u32[]{:S(2)}) collective-permute-start(bf16[16,80,640]{2,1,0:T(8,128)(2,1)} %get-tuple-element.75), channel_id=1, source_target_pairs={{0,4},{1,5},{2,6},{3,7},{4,0},{5,1},{6,2},{7,3},{8,12},{9,13},{10,... | collective-permute-start | bytes 4915208 | tf_op jit(solution)/shard_map/ppermute | solution.py:651
  155.8 5.7 %copy-start.32 = (bf16[384,640]{1,0:T(8,128)(2,1)S(1)}, bf16[384,640]{1,0:T(8,128)(2,1)}, u32[]{:S(2)}) copy-start(bf16[384,640]{1,0:T(8,128)(2,1)} %copy-done.31) | copy-start | bytes 1474564
  155.8 5.7 %copy-start.34 = (bf16[384,640]{1,0:T(8,128)(2,1)S(1)}, bf16[384,640]{1,0:T(8,128)(2,1)}, u32[]{:S(2)}) copy-start(bf16[384,640]{1,0:T(8,128)(2,1)} %copy-done.33) | copy-start | bytes 1474564
  155.8 5.7 %copy-start.36 = (bf16[384,640]{1,0:T(8,128)(2,1)S(1)}, bf16[384,640]{1,0:T(8,128)(2,1)}, u32[]{:S(2)}) copy-start(bf16[384,640]{1,0:T(8,128)(2,1)} %copy-done.35) | copy-start | bytes 1474564
  157.1 4.2 %copy-start.14 = (bf16[4,80,640]{2,1,0:T(8,128)(2,1)}, bf16[4,80,640]{2,1,0:T(8,128)(2,1)S(1)}, u32[]{:S(2)}) copy-start(bf16[4,80,640]{2,1,0:T(8,128)(2,1)S(1)} %fusion.12.refs_0_) | copy-start | bytes 1228804
  157.2 4.3 %copy-start.2 = (bf16[2560,640]{1,0:T(8,128)(2,1)S(1)}, bf16[2560,640]{1,0:T(8,128)(2,1)}, u32[]{:S(2)}) copy-start(bf16[2560,640]{1,0:T(8,128)(2,1)} %refs_9_.1) | copy-start | bytes 9830404
  158.6 2.8 %copy-start.16 = (bf16[4,80,640]{2,1,0:T(8,128)(2,1)}, bf16[4,80,640]{2,1,0:T(8,128)(2,1)S(1)}, u32[]{:S(2)}) copy-start(bf16[4,80,640]{2,1,0:T(8,128)(2,1)S(1)} %fusion.14.refs_2_) | copy-start | bytes 1228804
  160.0 1.4 copy-start.18
  161.5 1.9 copy-start.6
  163.4 1.9 copy-start.8
  175.4 1.9 copy-start
  178.1 1.6 copy-start.19
  178.1 2.7 %copy-start.17 = (bf16[4,80,640]{2,1,0:T(8,128)(2,1)S(1)}, bf16[4,80,640]{2,1,0:T(8,128)(2,1)}, u32[]{:S(2)}) copy-start(bf16[4,80,640]{2,1,0:T(8,128)(2,1)} %copy-done.16) | copy-start | bytes 1228804
  178.1 3.3 %copy-start.15 = (bf16[4,80,640]{2,1,0:T(8,128)(2,1)S(1)}, bf16[4,80,640]{2,1,0:T(8,128)(2,1)}, u32[]{:S(2)}) copy-start(bf16[4,80,640]{2,1,0:T(8,128)(2,1)} %copy-done.14) | copy-start | bytes 1228804
  179.1 13.7 %copy-start.27 = (bf16[16,80,640]{2,1,0:T(8,128)(2,1)S(1)}, bf16[16,80,640]{2,1,0:T(8,128)(2,1)}, u32[]{:S(2)}) copy-start(bf16[16,80,640]{2,1,0:T(8,128)(2,1)} %copy-done.26) | copy-start | bytes 4915204
  179.1 9.3 %collective-permute-start.13 = (bf16[4,80,640]{2,1,0:T(8,128)(2,1)S(1)}, bf16[4,80,640]{2,1,0:T(8,128)(2,1)}, u32[]{:S(2)}, u32[]{:S(2)}) collective-permute-start(bf16[4,80,640]{2,1,0:T(8,128)(2,1)S(1)} %copy-done.21), channel_id=1, source_target_pairs={{0,8},{1,9},{2,10},{3,11},{4,28},{5,29},{6,30},{7,31},{8,16},{9,17... | collective-permute-start | bytes 1228808 | tf_op jit(solution)/shard_map/ppermute | solution.py:651
  179.7 13.1 %collective-permute-start.10 = (bf16[4,80,640]{2,1,0:T(8,128)(2,1)S(1)}, bf16[4,80,640]{2,1,0:T(8,128)(2,1)}, u32[]{:S(2)}, u32[]{:S(2)}) collective-permute-start(bf16[4,80,640]{2,1,0:T(8,128)(2,1)S(1)} %copy-done.19), channel_id=1, source_target_pairs={{0,8},{1,9},{2,10},{3,11},{4,28},{5,29},{6,30},{7,31},{8,16},{9,17... | collective-permute-start | bytes 1228808 | tf_op jit(solution)/shard_map/ppermute | solution.py:651
  180.8 13.4 %copy-start.25 = (bf16[16,80,640]{2,1,0:T(8,128)(2,1)S(1)}, bf16[16,80,640]{2,1,0:T(8,128)(2,1)}, u32[]{:S(2)}) copy-start(bf16[16,80,640]{2,1,0:T(8,128)(2,1)} %copy-done.24) | copy-start | bytes 4915204
  180.8 13.4 %collective-permute-start.22 = (bf16[4,80,640]{2,1,0:T(8,128)(2,1)S(1)}, bf16[4,80,640]{2,1,0:T(8,128)(2,1)S(1)}, u32[]{:S(2)}, u32[]{:S(2)}) collective-permute-start(bf16[4,80,640]{2,1,0:T(8,128)(2,1)S(1)} %copy-done.17), channel_id=1, source_target_pairs={{0,32},{1,33},{2,34},{3,35},{4,100},{5,101},{6,102},{7,103},{8,40}... | collective-permute-start | bytes 1228808 | tf_op jit(solution)/shard_map/ppermute | solution.py:651
  181.4 14.2 %collective-permute-start.19 = (bf16[4,80,640]{2,1,0:T(8,128)(2,1)S(1)}, bf16[4,80,640]{2,1,0:T(8,128)(2,1)S(1)}, u32[]{:S(2)}, u32[]{:S(2)}) collective-permute-start(bf16[4,80,640]{2,1,0:T(8,128)(2,1)S(1)} %copy-done.15), channel_id=1, source_target_pairs={{0,32},{1,33},{2,34},{3,35},{4,100},{5,101},{6,102},{7,103},{8,40}... | collective-permute-start | bytes 1228808 | tf_op jit(solution)/shard_map/ppermute | solution.py:651
  189.8 5.9 %copy-start.23 = (bf16[16,80,640]{2,1,0:T(8,128)(2,1)S(1)}, bf16[16,80,640]{2,1,0:T(8,128)(2,1)}, u32[]{:S(2)}) copy-start(bf16[16,80,640]{2,1,0:T(8,128)(2,1)} %copy-done.22) | copy-start | bytes 4915204
  189.8 9.2 %collective-permute-start.14 = (bf16[4,80,640]{2,1,0:T(8,128)(2,1)S(1)}, bf16[4,80,640]{2,1,0:T(8,128)(2,1)S(1)}, u32[]{:S(2)}, u32[]{:S(2)}) collective-permute-start(bf16[4,80,640]{2,1,0:T(8,128)(2,1)S(1)} %fusion.8), channel_id=1, source_target_pairs={{0,8},{1,9},{2,10},{3,11},{4,28},{5,29},{6,30},{7,31},{8,16},{9,17... | collective-permute-start | bytes 1228808 | tf_op jit(solution)/shard_map/ppermute | solution.py:651
  194.1 5.0 %copy-start.29 = (bf16[16,80,640]{2,1,0:T(8,128)(2,1)S(1)}, bf16[16,80,640]{2,1,0:T(8,128)(2,1)}, u32[]{:S(2)}) copy-start(bf16[16,80,640]{2,1,0:T(8,128)(2,1)} %copy-done.28) | copy-start | bytes 4915204
  194.1 9.3 %collective-permute-start.11 = (bf16[4,80,640]{2,1,0:T(8,128)(2,1)S(1)}, bf16[4,80,640]{2,1,0:T(8,128)(2,1)S(1)}, u32[]{:S(2)}, u32[]{:S(2)}) collective-permute-start(bf16[4,80,640]{2,1,0:T(8,128)(2,1)S(1)} %fusion.11), channel_id=1, source_target_pairs={{0,8},{1,9},{2,10},{3,11},{4,28},{5,29},{6,30},{7,31},{8,16},{9,17... | collective-permute-start | bytes 1228808 | tf_op jit(solution)/shard_map/ppermute | solution.py:651
  195.4 9.2 %collective-permute-start.23 = (bf16[4,80,640]{2,1,0:T(8,128)(2,1)S(1)}, bf16[4,80,640]{2,1,0:T(8,128)(2,1)S(1)}, u32[]{:S(2)}, u32[]{:S(2)}) collective-permute-start(bf16[4,80,640]{2,1,0:T(8,128)(2,1)S(1)} %fusion.2), channel_id=1, source_target_pairs={{0,32},{1,33},{2,34},{3,35},{4,100},{5,101},{6,102},{7,103},{8,40}... | collective-permute-start | bytes 1228808 | tf_op jit(solution)/shard_map/ppermute | solution.py:651
  196.8 12.2 %collective-permute-start.20 = (bf16[4,80,640]{2,1,0:T(8,128)(2,1)S(1)}, bf16[4,80,640]{2,1,0:T(8,128)(2,1)S(1)}, u32[]{:S(2)}, u32[]{:S(2)}) collective-permute-start(bf16[4,80,640]{2,1,0:T(8,128)(2,1)S(1)} %fusion.5), channel_id=1, source_target_pairs={{0,32},{1,33},{2,34},{3,35},{4,100},{5,101},{6,102},{7,103},{8,40}... | collective-permute-start | bytes 1228808 | tf_op jit(solution)/shard_map/ppermute | solution.py:651
  200.2 10.1 %collective-permute-start.15 = (bf16[4,80,640]{2,1,0:T(8,128)(2,1)S(1)}, bf16[4,80,640]{2,1,0:T(8,128)(2,1)S(1)}, u32[]{:S(2)}, u32[]{:S(2)}) collective-permute-start(bf16[4,80,640]{2,1,0:T(8,128)(2,1)S(1)} %fusion.7), channel_id=1, source_target_pairs={{0,8},{1,9},{2,10},{3,11},{4,28},{5,29},{6,30},{7,31},{8,16},{9,17... | collective-permute-start | bytes 1228808 | tf_op jit(solution)/shard_map/ppermute | solution.py:651
  204.6 9.2 %collective-permute-start.12 = (bf16[4,80,640]{2,1,0:T(8,128)(2,1)S(1)}, bf16[4,80,640]{2,1,0:T(8,128)(2,1)S(1)}, u32[]{:S(2)}, u32[]{:S(2)}) collective-permute-start(bf16[4,80,640]{2,1,0:T(8,128)(2,1)S(1)} %fusion.10), channel_id=1, source_target_pairs={{0,8},{1,9},{2,10},{3,11},{4,28},{5,29},{6,30},{7,31},{8,16},{9,17... | collective-permute-start | bytes 1228808 | tf_op jit(solution)/shard_map/ppermute | solution.py:651
  205.8 14.0 %collective-permute-start.24 = (bf16[4,80,640]{2,1,0:T(8,128)(2,1)S(1)}, bf16[4,80,640]{2,1,0:T(8,128)(2,1)S(1)}, u32[]{:S(2)}, u32[]{:S(2)}) collective-permute-start(bf16[4,80,640]{2,1,0:T(8,128)(2,1)S(1)} %fusion.1), channel_id=1, source_target_pairs={{0,32},{1,33},{2,34},{3,35},{4,100},{5,101},{6,102},{7,103},{8,40}... | collective-permute-start | bytes 1228808 | tf_op jit(solution)/shard_map/ppermute | solution.py:651
  210.2 14.0 %collective-permute-start.21 = (bf16[4,80,640]{2,1,0:T(8,128)(2,1)S(1)}, bf16[4,80,640]{2,1,0:T(8,128)(2,1)S(1)}, u32[]{:S(2)}, u32[]{:S(2)}) collective-permute-start(bf16[4,80,640]{2,1,0:T(8,128)(2,1)S(1)} %fusion.4), channel_id=1, source_target_pairs={{0,32},{1,33},{2,34},{3,35},{4,100},{5,101},{6,102},{7,103},{8,40}... | collective-permute-start | bytes 1228808 | tf_op jit(solution)/shard_map/ppermute | solution.py:651
  215.1 15.7 %collective-permute-start.18 = (bf16[2,80,640]{2,1,0:T(8,128)(2,1)S(1)}, bf16[2,80,640]{2,1,0:T(8,128)(2,1)S(1)}, u32[]{:S(2)}, u32[]{:S(2)}) collective-permute-start(bf16[2,80,640]{2,1,0:T(8,128)(2,1)S(1)} %pad_maximum_fusion.2), channel_id=1, source_target_pairs={{0,64},{1,65},{2,66},{3,67},{4,68},{5,69},{6,70},{7,71},{8,72},{9,... | collective-permute-start | bytes 614408 | tf_op jit(solution)/shard_map/ppermute | solution.py:651
  217.6 14.0 %collective-permute-start.17 = (bf16[2,80,640]{2,1,0:T(8,128)(2,1)S(1)}, bf16[2,80,640]{2,1,0:T(8,128)(2,1)S(1)}, u32[]{:S(2)}, u32[]{:S(2)}) collective-permute-start(bf16[2,80,640]{2,1,0:T(8,128)(2,1)S(1)} %pad_maximum_fusion.1), channel_id=1, source_target_pairs={{0,96},{1,97},{2,98},{3,99},{4,100},{5,101},{6,102},{7,103},{8,104... | collective-permute-start | bytes 614408 | tf_op jit(solution)/shard_map/ppermute | solution.py:651
  218.1 13.6 %collective-permute-start.16 = (bf16[2,80,640]{2,1,0:T(8,128)(2,1)S(1)}, bf16[2,80,640]{2,1,0:T(8,128)(2,1)S(1)}, u32[]{:S(2)}, u32[]{:S(2)}) collective-permute-start(bf16[2,80,640]{2,1,0:T(8,128)(2,1)S(1)} %pad_maximum_fusion), channel_id=1, source_target_pairs={{0,32},{1,33},{2,34},{3,35},{4,36},{5,37},{6,38},{7,39},{8,40},{9,... | collective-permute-start | bytes 614408 | tf_op jit(solution)/shard_map/ppermute | solution.py:651
  225.5 7.3 %collective-permute-start.27 = (bf16[2,80,640]{2,1,0:T(8,128)(2,1)S(1)}, bf16[2,80,640]{2,1,0:T(8,128)(2,1)S(1)}, u32[]{:S(2)}, u32[]{:S(2)}) collective-permute-start(bf16[2,80,640]{2,1,0:T(8,128)(2,1)S(1)} %pad_maximum_fusion.5), channel_id=1, source_target_pairs={{0,16},{1,17},{2,18},{3,19},{4,20},{5,21},{6,22},{7,23},{8,24},{9,... | collective-permute-start | bytes 614408 | tf_op jit(solution)/shard_map/ppermute | solution.py:651
  228.8 8.6 %collective-permute-start.26 = (bf16[2,80,640]{2,1,0:T(8,128)(2,1)S(1)}, bf16[2,80,640]{2,1,0:T(8,128)(2,1)S(1)}, u32[]{:S(2)}, u32[]{:S(2)}) collective-permute-start(bf16[2,80,640]{2,1,0:T(8,128)(2,1)S(1)} %pad_maximum_fusion.4), channel_id=1, source_target_pairs={{0,24},{1,25},{2,26},{3,27},{4,28},{5,29},{6,30},{7,31},{8,0},{9,1... | collective-permute-start | bytes 614408 | tf_op jit(solution)/shard_map/ppermute | solution.py:651
  230.7 7.0 %collective-permute-start.25 = (bf16[2,80,640]{2,1,0:T(8,128)(2,1)S(1)}, bf16[2,80,640]{2,1,0:T(8,128)(2,1)S(1)}, u32[]{:S(2)}, u32[]{:S(2)}) collective-permute-start(bf16[2,80,640]{2,1,0:T(8,128)(2,1)S(1)} %pad_maximum_fusion.3), channel_id=1, source_target_pairs={{0,8},{1,9},{2,10},{3,11},{4,12},{5,13},{6,14},{7,15},{8,16},{9,17... | collective-permute-start | bytes 614408 | tf_op jit(solution)/shard_map/ppermute | solution.py:651
  (13 other events, 13.7 us)
Sparse Core Ops, SparseCore 0:
  178.3 41.6 reduce-scatter.1

commit v3 on v2

--- a/solution.py
+++ b/solution.py
@@ -684,17 +684,17 @@
         )
 
 
-def second_axis_sums(halves, second, places):
+def second_axis_sums(halves, second, places, ahead=()):
     place = places[second]
 
     def mine(step):
         return jnp.stack([picked(half)((place + step) % SIDE) for half in halves])
 
-    total = mine(0).astype(F32)
+    total, *ahead = lax.optimization_barrier((mine(0).astype(F32), *ahead))
     for step in (1, -1, 2):
         steps = (2, -2) if step == 2 else step
         total += moved(mine(step), second, steps).astype(F32)
-    return [total[index] for index in range(len(halves))]
+    return [total[index] for index in range(len(halves))] + ahead
 
 
 def per_device(
@@ -775,7 +775,7 @@
         swapped.append((keep, moved(send, "core", 1)))
     sums = [FirstAxis(pair, first, places, up) for pair, first in zip(swapped, "xyxy")]
     outward = outward_part(
-        tuple(each.start for each in sums),
+        (after,),
         (back_query, back_key, back_value),
         gated,
         (w_query, w_key, w_value, w_out),
@@ -785,7 +785,9 @@
     mixed, grad_input = outward[:row_count], outward[row_count:]
     halves = [each.total() for each in sums]
     grad_out, grad_key = second_axis_sums(halves[0::2], "y", places)
-    grad_query, grad_value = second_axis_sums(halves[1::2], "x", places)
+    grad_query, grad_value, mixed, grad_input = second_axis_sums(
+        halves[1::2], "x", places, (mixed, grad_input)
+    )
     grad_out = grad_out.T
     return (mixed, grad_input, grad_query, grad_key, grad_value, grad_out, grad_filter, grad_init)
 

time: 249 us -> 237 us (0.952)
  local copies, waits for them, and re-layouts: 39.9 us -> 32.1 us
  Pallas kernels: 64.2 us -> 59.5 us
    unnamed x98 -> x66, local copies, waits for them, and re-layouts: 30.8 us -> 23 us
    pallas_call x4, Pallas kernels: 18.2 us -> 13.4 us  [weight_partial(): pl.pallas_call(functools.partial(weight_kernel, rows), in_specs=anywhere(...]
  transfers between devices with their start and end apart: 30 -> 30, of which waited for: 14 -> 16; matrix products, arithmetic and copies ran while one was open for 12% -> 14% of each run, Pallas kernels for 11% -> 6%
where the time goes in v3:
time: 237 us; the launch traced here: 234 us
  Pallas kernels  59.5 us (25%)
  waiting for transfers between devices  43.9 us (19%)
  starting transfers between devices  33.9 us (14%)
  local copies, waits for them, and re-layouts  32.1 us (14%)
  blocking collectives  27.8 us (12%)
  other arithmetic  22.7 us (10%)
  between operations  14.5 us (6%)
    ppermute x28, waiting for transfers between devices, moved(): return lax.ppermute(value, ('seq', 'tp'), pairs)  37.9 us
    all_to_all x1, blocking collectives, exchanged(): return lax.all_to_all(value, 'seq', 0, 0, tiled=True)  27.8 us
    ppermute x28, starting transfers between devices, moved(): return lax.ppermute(value, ('seq', 'tp'), pairs)  26.3 us
    unnamed x66, local copies, waits for them, and re-layouts  23 us
    convert_element_type x16, other arithmetic, added(): return (left.astype(F32) + right.astype(F32)).astype(BF16)  19.6 us
    pallas_call x1, Pallas kernels, sequence_part(): pl.pallas_call(functools.partial(sequence_kernel, group), out_shape=jax.S...  18.4 us
    pallas_call x4, Pallas kernels, weight_partial(): pl.pallas_call(functools.partial(weight_kernel, rows), in_specs=anywhere(...  13.4 us
    pallas_call x1, Pallas kernels, outward_part(): pl.pallas_call(functools.partial(outward_kernel, len(after)), in_specs=an...  9.12 us
  transfers between devices with their start and end apart: 30, of which 16 were waited for; matrix products, arithmetic and copies ran while one was open for 14% of the time, Pallas kernels for 6%

profile of v3, /device:TPU:0, one launch (start us, length us, event | category | flops | bytes accessed | tf_op | source)
XLA Modules:
  0.0 234.4 jit_solution(2946532637763460697)
XLA Ops:
  7.2 2.1 collective-permute-start.2
  9.2 2.2 collective-permute-start.3
  11.4 3.2 %collective-permute-start.1 = (bf16[384,640]{1,0:T(8,128)(2,1)}, bf16[384,640]{1,0:T(8,128)(2,1)S(1)}, u32[]{:S(2)}, u32[]{:S(2)}) collective-permute-start(bf16[384,640]{1,0:T(8,128)(2,1)} %refs_4_.1), channel_id=1, source_target_pairs={{0,3},{1,0},{2,1},{3,2},{4,7},{5,4},{6,5},{7,6},{8,11},{9,8},{10,9... | collective-permute-start | bytes 1474568 | tf_op jit(solution)/shard_map/ppermute | solution.py:651
  14.7 1.9 copy-done.1
  16.6 1.9 copy-done.3
  18.5 1.9 copy-done.5
  20.5 1.9 copy-done.7
  23.1 1.6 shard_map.179
  24.8 8.6 %collective-permute-done.second_ref.refs_5_ = bf16[384,640]{1,0:T(8,128)(2,1)S(1)} collective-permute-done((bf16[384,640]{1,0:T(8,128)(2,1)}, bf16[384,640]{1,0:T(8,128)(2,1)S(1)}, u32[]{:S(2)}, u32[]{:S(2)}) %collective-permute-start) | collective-permute-done | bytes 491552 | tf_op jit(solution)/shard_map/ppermute | solution.py:651
  33.3 1.3 collective-permute-start.4
  34.6 1.7 collective-permute-start.5
  36.4 4.7 %shard_map.180 = (f32[384,640]{1,0:T(8,128)S(1)}, f32[384,640]{1,0:T(8,128)S(1)}, f32[384,640]{1,0:T(8,128)S(1)}) custom-call(bf16[384,640]{1,0:T(8,128)(2,1)S(1)} %copy-done.9, bf16[384,640]{1,0:T(8,128)(2,1)S(1)} %collective-permute-done.2.refs_1_, bf16[384,640]{1,0:T(8,128)(2,1)S(1)} %collective-permute-done.3.refs_2_, ...), custom_call_target="tpu_custom_call" | custom-call | flops 2831155200 | bytes 12000000 | tf_op jit(solution)/shard_map/pallas_call | solution.py:336
  41.0 2.0 shard_map.182.sum_ref
  43.4 2.2 shard_map.181
  45.6 3.1 %collective-permute-done.5.shard_ref.refs_7_ = bf16[384,640]{1,0:T(8,128)(2,1)S(1)} collective-permute-done((bf16[384,640]{1,0:T(8,128)(2,1)S(1)}, bf16[384,640]{1,0:T(8,128)(2,1)S(1)}, u32[]{:S(2)}, u32[]{:S(2)}) %collective-permute-start.5) | collective-permute-done | bytes 491552 | tf_op jit(solution)/shard_map/ppermute | solution.py:651
  48.6 2.5 %shard_map.183 = (bf16[384,640]{1,0:T(8,128)(2,1)S(1)}, bf16[32,60,384]{2,1,0:T(8,128)(2,1)}) custom-call(bf16[32,40,384]{2,1,0:T(8,128)(2,1)S(1)} %get-tuple-element.55.kv_ref, bf16[384,640]{1,0:T(8,128)(2,1)S(1)} %collective-permute-done.5.shard_ref.refs_7_, bf16[640,2560]{1,0:T(8,128)(2,1)S(1)} %get-tuple-element.58.weight_ref, ...), custom_call_target="tpu_custom_call" | custom-call | flops 314572800 | bytes 6000000 | tf_op jit(solution)/shard_map/pallas_call | solution.py:432
  51.9 7.4 %all-to-all-start = ((bf16[32,60,384]{2,1,0:T(8,128)(2,1)}), bf16[32,60,384]{2,1,0:T(8,128)(2,1)}, u32[]{:S(2)}, u32[]{:S(2)}) async-start(bf16[32,60,384]{2,1,0:T(8,128)(2,1)} %get-tuple-element.60.after_ref), calls=%async_computation | async-start | bytes 3145728 | tf_op jit(solution)/shard_map/all_to_all | solution.py:752
  61.4 1.6 constant_dynamic-slice_fusion.16
  63.0 1.4 copy.66
  65.8 1.6 copy.45.cols_ref
  69.8 4.0 %shard_map.184 = (bf16[4,640,384]{2,1,0:T(8,128)(2,1)S(1)}, bf16[4,640,384]{2,1,0:T(8,128)(2,1)S(1)}, f32[8,128]{1,0:T(8,128)S(1)}) custom-call(bf16[32,60,384]{2,1,0:T(8,128)(2,1)} %get-tuple-element.60.after_ref, bf16[384,640]{1,0:T(8,128)(2,1)S(1)} %copy-done.9, bf16[384,640]{1,0:T(8,128)(2,1)S(1)} %collective-permute-done.2.refs_1_, ...), custom_call_target="tpu_custom_call" | custom-call | flops 1966080 | bytes 8000000 | tf_op jit(solution)/shard_map/pallas_call | solution.py:516
  73.9 1.3 copy-done.22
  75.1 1.3 copy-done.24
  76.5 6.0 %all-to-all-done.in_ref = bf16[32,60,384]{2,1,0:T(8,128)(2,1)} async-done(((bf16[32,60,384]{2,1,0:T(8,128)(2,1)}), bf16[32,60,384]{2,1,0:T(8,128)(2,1)}, u32[]{:S(2)}, u32[]{:S(2)}) %all-to-all-start) | async-done | bytes 1474592 | tf_op jit(solution)/shard_map/all_to_all | solution.py:752
  82.5 1.3 copy-done.18
  83.8 18.4 %shard_map.185 = bf16[32,67,384]{2,1,0:T(8,128)(2,1)S(1)} custom-call(f32[8,128]{1,0:T(8,128)S(1)} %get-tuple-element.61.after_ref, bf16[32,60,384]{2,1,0:T(8,128)(2,1)} %all-to-all-done.in_ref, f32[2,20,64]{2,1,0:T(8,128)S(1)} %get-tuple-element.109.rows_ref, f32[2,20,64,1]{3,2,1,0:T(8,128)S(1)} %copy-done.18, ...), custom_call_target="tpu_custom_call" | custom-call | flops 22000001024 | bytes 5000000 | tf_op jit(solution)/shard_map/pallas_call | solution.py:286
  102.2 27.8 %all_to_all.10.returned_ref = bf16[32,67,384]{2,1,0:T(8,128)(2,1)S(1)} all-to-all(bf16[32,67,384]{2,1,0:T(8,128)(2,1)S(1)} %shard_map.185), channel_id=1, replica_groups=mesh['seq'=32,'tp'=4] {'seq'}, dimensions={0} | all-to-all | bytes 3293184 | tf_op jit(solution)/shard_map/all_to_all | solution.py:752
  130.0 1.5 shard_map.186
  131.5 3.4 %shard_map.187 = (bf16[16,80,640]{2,1,0:T(8,128)(2,1)S(1)}, bf16[16,80,640]{2,1,0:T(8,128)(2,1)S(1)}, f32[8,128]{1,0:T(8,128)S(1)}) custom-call(bf16[384,640]{1,0:T(8,128)(2,1)S(1)} %get-tuple-element.63.after_ref.narrow_ref.refs_4_, bf16[4,640,384]{2,1,0:T(8,128)(2,1)S(1)} %copy-done.25, ...), custom_call_target="tpu_custom_call" | custom-call | flops 1258291200 | bytes 6000000 | tf_op jit(solution)/shard_map/pallas_call | solution.py:581
  134.9 3.4 %shard_map.188 = (bf16[16,80,640]{2,1,0:T(8,128)(2,1)S(1)}, bf16[16,80,640]{2,1,0:T(8,128)(2,1)S(1)}, f32[8,128]{1,0:T(8,128)S(1)}) custom-call(f32[8,128]{1,0:T(8,128)S(1)} %get-tuple-element.65.after_ref, bf16[4,640,384]{2,1,0:T(8,128)(2,1)S(1)} %copy-done.23, bf16[384,640]{1,0:T(8,128)(2,1)S(1)} %get-tuple-element.67.narrow_ref.refs_1_, ...), custom_call_target="tpu_custom_call" | custom-call | flops 1258291200 | bytes 6000000 | tf_op jit(solution)/shard_map/pallas_call | solution.py:581
  139.5 3.4 %shard_map.189 = (bf16[16,80,640]{2,1,0:T(8,128)(2,1)S(1)}, bf16[16,80,640]{2,1,0:T(8,128)(2,1)S(1)}, f32[8,128]{1,0:T(8,128)S(1)}) custom-call(f32[8,128]{1,0:T(8,128)S(1)} %get-tuple-element.70.after_ref, bf16[4,640,384]{2,1,0:T(8,128)(2,1)S(1)} %copy-done.23, bf16[384,640]{1,0:T(8,128)(2,1)S(1)} %get-tuple-element.71.narrow_ref.refs_2_, ...), custom_call_target="tpu_custom_call" | custom-call | flops 1258291200 | bytes 6000000 | tf_op jit(solution)/shard_map/pallas_call | solution.py:581
  142.9 3.4 %shard_map.190 = (bf16[16,80,640]{2,1,0:T(8,128)(2,1)S(1)}, bf16[16,80,640]{2,1,0:T(8,128)(2,1)S(1)}, f32[8,128]{1,0:T(8,128)S(1)}) custom-call(f32[8,128]{1,0:T(8,128)S(1)} %get-tuple-element.72.after_ref, bf16[4,640,384]{2,1,0:T(8,128)(2,1)S(1)} %copy-done.23, bf16[384,640]{1,0:T(8,128)(2,1)S(1)} %get-tuple-element.73.narrow_ref.refs_3_, ...), custom_call_target="tpu_custom_call" | custom-call | flops 1258291200 | bytes 6000000 | tf_op jit(solution)/shard_map/pallas_call | solution.py:581
  146.3 1.3 copy-done.16
  147.5 1.2 copy-done.29
  148.7 9.1 %shard_map.191 = bf16[4,768,640]{2,1,0:T(8,128)(2,1)S(1)} custom-call(f32[8,128]{1,0:T(8,128)S(1)} %get-tuple-element.76.refs_0_, bf16[384,640]{1,0:T(8,128)(2,1)S(1)} %get-tuple-element.67.narrow_ref.refs_1_, bf16[384,640]{1,0:T(8,128)(2,1)S(1)} %get-tuple-element.71.narrow_ref.refs_2_, bf16[384,640]{1,0:T(8,128)(2,1)S(1)} %get-tuple-element.73.narrow_ref.refs_3_, ...), custom_call_target="tpu_custom_call" | custom-call | flops 5033164800 | bytes 20000000 | tf_op jit(solution)/shard_map/pallas_call | solution.py:621
  157.9 1.9 copy-done
  161.1 2.9 %collective-permute-done.10 = bf16[16,80,640]{2,1,0:T(8,128)(2,1)} collective-permute-done((bf16[16,80,640]{2,1,0:T(8,128)(2,1)}, bf16[16,80,640]{2,1,0:T(8,128)(2,1)}, u32[]{:S(2)}, u32[]{:S(2)}) %collective-permute-start.10) | collective-permute-done | bytes 1638432 | tf_op jit(solution)/shard_map/ppermute | solution.py:651
  164.0 2.0 fusion.16
  166.5 1.4 fusion.12
  167.8 1.2 collective-permute-start.7
  172.7 2.8 %collective-permute-done.11 = bf16[4,80,640]{2,1,0:T(8,128)(2,1)} collective-permute-done((bf16[4,80,640]{2,1,0:T(8,128)(2,1)}, bf16[4,80,640]{2,1,0:T(8,128)(2,1)}, u32[]{:S(2)}, u32[]{:S(2)}) %collective-permute-start.11) | collective-permute-done | bytes 409632 | tf_op jit(solution)/shard_map/ppermute | solution.py:651
  175.5 1.3 fusion.8
  176.9 2.9 %collective-permute-done.7 = bf16[4,80,640]{2,1,0:T(8,128)(2,1)S(1)} collective-permute-done((bf16[4,80,640]{2,1,0:T(8,128)(2,1)S(1)}, bf16[4,80,640]{2,1,0:T(8,128)(2,1)S(1)}, u32[]{:S(2)}, u32[]{:S(2)}) %collective-permute-start.7) | collective-permute-done | bytes 409632 | tf_op jit(solution)/shard_map/ppermute | solution.py:651
  179.7 1.2 fusion.11
  181.0 1.2 fusion.2
  182.4 1.6 collective-permute-done.18
  184.0 1.2 fusion.5
  186.0 1.2 fusion.7
  187.8 2.6 %collective-permute-done.8 = bf16[4,80,640]{2,1,0:T(8,128)(2,1)S(1)} collective-permute-done((bf16[4,80,640]{2,1,0:T(8,128)(2,1)S(1)}, bf16[4,80,640]{2,1,0:T(8,128)(2,1)S(1)}, u32[]{:S(2)}, u32[]{:S(2)}) %collective-permute-start.8) | collective-permute-done | bytes 409632 | tf_op jit(solution)/shard_map/ppermute | solution.py:651
  190.4 1.2 fusion.10
  191.7 1.2 fusion.1
  193.0 2.8 %collective-permute-done.19 = bf16[4,80,640]{2,1,0:T(8,128)(2,1)S(1)} collective-permute-done((bf16[4,80,640]{2,1,0:T(8,128)(2,1)S(1)}, bf16[4,80,640]{2,1,0:T(8,128)(2,1)S(1)}, u32[]{:S(2)}, u32[]{:S(2)}) %collective-permute-start.19) | collective-permute-done | bytes 409632 | tf_op jit(solution)/shard_map/ppermute | solution.py:651
  195.8 1.2 fusion.4
  197.1 1.2 fusion.6
  198.2 2.6 %collective-permute-done.9 = bf16[4,80,640]{2,1,0:T(8,128)(2,1)S(1)} collective-permute-done((bf16[4,80,640]{2,1,0:T(8,128)(2,1)S(1)}, bf16[4,80,640]{2,1,0:T(8,128)(2,1)S(1)}, u32[]{:S(2)}, u32[]{:S(2)}) %collective-permute-start.9) | collective-permute-done | bytes 409632 | tf_op jit(solution)/shard_map/ppermute | solution.py:651
  200.8 1.2 fusion.9
  202.1 2.2 collective-permute-start.16
  205.7 1.2 fusion
  206.9 1.3 collective-permute-done.20
  208.2 1.2 fusion.3
  209.5 2.0 collective-permute-start.27
  211.5 4.0 %collective-permute-start.26 = (bf16[2,80,640]{2,1,0:T(8,128)(2,1)S(1)}, bf16[2,80,640]{2,1,0:T(8,128)(2,1)S(1)}, u32[]{:S(2)}, u32[]{:S(2)}) collective-permute-start(bf16[2,80,640]{2,1,0:T(8,128)(2,1)S(1)} %pad_maximum_fusion.4), channel_id=1, source_target_pairs={{0,24},{1,25},{2,26},{3,27},{4,28},{5,29},{6,30},{7,31},{8,0},{9,1... | collective-permute-start | bytes 614408 | tf_op jit(solution)/shard_map/ppermute | solution.py:651
  217.4 4.8 %collective-permute-done.26 = bf16[2,80,640]{2,1,0:T(8,128)(2,1)S(1)} collective-permute-done((bf16[2,80,640]{2,1,0:T(8,128)(2,1)S(1)}, bf16[2,80,640]{2,1,0:T(8,128)(2,1)S(1)}, u32[]{:S(2)}, u32[]{:S(2)}) %collective-permute-start.26) | collective-permute-done | bytes 204832 | tf_op jit(solution)/shard_map/ppermute | solution.py:651
  223.5 2.2 slice_bitcast_fusion
  (123 shorter events, 23.4 us)
Async XLA Ops:
  7.2 17.5 %collective-permute-start.2 = (bf16[384,640]{1,0:T(8,128)(2,1)}, bf16[384,640]{1,0:T(8,128)(2,1)S(1)}, u32[]{:S(2)}, u32[]{:S(2)}) collective-permute-start(bf16[384,640]{1,0:T(8,128)(2,1)} %refs_0_.5), channel_id=1, source_target_pairs={{0,1},{1,2},{2,3},{3,0},{4,5},{5,6},{6,7},{7,4},{8,9},{9,10},{10,1... | collective-permute-start | bytes 1474568 | tf_op jit(solution)/shard_map/ppermute | solution.py:651
  9.2 15.5 %collective-permute-start.3 = (bf16[384,640]{1,0:T(8,128)(2,1)}, bf16[384,640]{1,0:T(8,128)(2,1)S(1)}, u32[]{:S(2)}, u32[]{:S(2)}) collective-permute-start(bf16[384,640]{1,0:T(8,128)(2,1)} %refs_0_.5), channel_id=1, source_target_pairs={{0,3},{1,0},{2,1},{3,2},{4,7},{5,4},{6,5},{7,6},{8,11},{9,8},{10,9... | collective-permute-start | bytes 1474568 | tf_op jit(solution)/shard_map/ppermute | solution.py:651
  11.4 21.9 %collective-permute-start = (bf16[384,640]{1,0:T(8,128)(2,1)}, bf16[384,640]{1,0:T(8,128)(2,1)S(1)}, u32[]{:S(2)}, u32[]{:S(2)}) collective-permute-start(bf16[384,640]{1,0:T(8,128)(2,1)} %refs_4_.1), channel_id=1, source_target_pairs={{0,1},{1,2},{2,3},{3,0},{4,5},{5,6},{6,7},{7,4},{8,9},{9,10},{10,1... | collective-permute-start | bytes 1474568 | tf_op jit(solution)/shard_map/ppermute | solution.py:651
  11.4 21.9 %collective-permute-start.1 = (bf16[384,640]{1,0:T(8,128)(2,1)}, bf16[384,640]{1,0:T(8,128)(2,1)S(1)}, u32[]{:S(2)}, u32[]{:S(2)}) collective-permute-start(bf16[384,640]{1,0:T(8,128)(2,1)} %refs_4_.1), channel_id=1, source_target_pairs={{0,3},{1,0},{2,1},{3,2},{4,7},{5,4},{6,5},{7,6},{8,11},{9,8},{10,9... | collective-permute-start | bytes 1474568 | tf_op jit(solution)/shard_map/ppermute | solution.py:651
  14.7 1.9 copy-start.1
  16.6 1.9 copy-start.3
  18.5 1.9 copy-start.5
  20.5 1.9 copy-start.7
  22.4 0.7 copy-start.21
  24.6 11.7 %copy-start.30 = (s32[4]{0:T(128)S(1)}, s32[4]{0:T(128)}, u32[]{:S(2)}) copy-start(s32[4]{0:T(128)} %constant.271.clone) | copy-start | bytes 52
  24.7 11.7 %copy-start.9 = (bf16[384,640]{1,0:T(8,128)(2,1)S(1)}, bf16[384,640]{1,0:T(8,128)(2,1)}, u32[]{:S(2)}) copy-start(bf16[384,640]{1,0:T(8,128)(2,1)} %refs_0_.5) | copy-start | bytes 1474564
  33.3 10.0 %collective-permute-start.4 = (bf16[384,640]{1,0:T(8,128)(2,1)S(1)}, bf16[384,640]{1,0:T(8,128)(2,1)S(1)}, u32[]{:S(2)}, u32[]{:S(2)}) collective-permute-start(bf16[384,640]{1,0:T(8,128)(2,1)S(1)} %broadcast_select_fusion.1), channel_id=1, source_target_pairs={{0,1},{1,2},{2,3},{3,0},{4,7},{5,4},{6,5},{7,6},{8,9},{9,10},{10,1... | collective-permute-start | bytes 1474568 | tf_op jit(solution)/shard_map/ppermute | solution.py:651
  34.6 14.0 %collective-permute-start.5 = (bf16[384,640]{1,0:T(8,128)(2,1)S(1)}, bf16[384,640]{1,0:T(8,128)(2,1)S(1)}, u32[]{:S(2)}, u32[]{:S(2)}) collective-permute-start(bf16[384,640]{1,0:T(8,128)(2,1)S(1)} %broadcast_select_fusion), channel_id=1, source_target_pairs={{0,1},{1,2},{2,3},{3,0},{4,7},{5,4},{6,5},{7,6},{8,9},{9,10},{10,1... | collective-permute-start | bytes 1474568 | tf_op jit(solution)/shard_map/ppermute | solution.py:651
  36.4 4.7 %copy-start.12 = (bf16[384,640]{1,0:T(8,128)(2,1)S(1)}, bf16[384,640]{1,0:T(8,128)(2,1)}, u32[]{:S(2)}) copy-start(bf16[384,640]{1,0:T(8,128)(2,1)} %refs_4_.1) | copy-start | bytes 1474564
  48.6 2.5 %copy-start.10 = (bf16[384,640]{1,0:T(8,128)(2,1)}, bf16[384,640]{1,0:T(8,128)(2,1)S(1)}, u32[]{:S(2)}) copy-start(bf16[384,640]{1,0:T(8,128)(2,1)S(1)} %collective-permute-done.5.shard_ref.refs_7_) | copy-start | bytes 1474564
  51.1 0.8 copy-start.19
  51.9 30.6 %all-to-all-start = ((bf16[32,60,384]{2,1,0:T(8,128)(2,1)}), bf16[32,60,384]{2,1,0:T(8,128)(2,1)}, u32[]{:S(2)}, u32[]{:S(2)}) async-start(bf16[32,60,384]{2,1,0:T(8,128)(2,1)} %get-tuple-element.60.after_ref), calls=%async_computation | async-start | bytes 3145728 | tf_op jit(solution)/shard_map/all_to_all | solution.py:752
  59.4 164.1 %reduce-scatter.2.cloned.1.call-start = ((), (), s32[]{:S(2)}) async-start(), calls=%async_computation.3 | async-start | bytes 4915200 | tf_op jit(solution)/shard_map/reduce_scatter | solution.py:784
  67.8 1.0 copy-start.11
  68.8 1.0 copy-start.13
  73.9 1.3 copy-start.22
  75.1 1.3 copy-start.24
  82.5 1.3 copy-start.18
  102.2 27.8 %copy-start.20 = (bf16[384,640]{1,0:T(8,128)(2,1)S(1)}, bf16[384,640]{1,0:T(8,128)(2,1)}, u32[]{:S(2)}) copy-start(bf16[384,640]{1,0:T(8,128)(2,1)} %copy-done.19) | copy-start | bytes 1474564
  130.0 1.5 copy-start.25
  131.5 3.4 %copy-start.23 = (bf16[4,640,384]{2,1,0:T(8,128)(2,1)S(1)}, bf16[4,640,384]{2,1,0:T(8,128)(2,1)}, u32[]{:S(2)}) copy-start(bf16[4,640,384]{2,1,0:T(8,128)(2,1)} %copy-done.22) | copy-start | bytes 5898244
  134.9 4.6 %copy-start.26 = (bf16[16,80,640]{2,1,0:T(8,128)(2,1)}, bf16[16,80,640]{2,1,0:T(8,128)(2,1)S(1)}, u32[]{:S(2)}) copy-start(bf16[16,80,640]{2,1,0:T(8,128)(2,1)S(1)} %get-tuple-element.81) | copy-start | bytes 4915204
  134.9 13.8 %copy-start.6 = (bf16[2560,640]{1,0:T(8,128)(2,1)S(1)}, bf16[2560,640]{1,0:T(8,128)(2,1)}, u32[]{:S(2)}) copy-start(bf16[2560,640]{1,0:T(8,128)(2,1)} %refs_5_.1) | copy-start | bytes 9830404
  134.9 13.8 %copy-start.8 = (bf16[640,2560]{1,0:T(8,128)(2,1)S(1)}, bf16[640,2560]{1,0:T(8,128)(2,1)}, u32[]{:S(2)}) copy-start(bf16[640,2560]{1,0:T(8,128)(2,1)} %refs_8_.1) | copy-start | bytes 9830404
  138.3 1.2 copy-start.28
  139.5 3.4 %copy-start.14 = (bf16[16,80,640]{2,1,0:T(8,128)(2,1)}, bf16[16,80,640]{2,1,0:T(8,128)(2,1)S(1)}, u32[]{:S(2)}) copy-start(bf16[16,80,640]{2,1,0:T(8,128)(2,1)S(1)} %get-tuple-element.68) | copy-start | bytes 4915204
  139.5 9.2 %copy-start.4 = (bf16[2560,640]{1,0:T(8,128)(2,1)S(1)}, bf16[2560,640]{1,0:T(8,128)(2,1)}, u32[]{:S(2)}) copy-start(bf16[2560,640]{1,0:T(8,128)(2,1)} %refs_7_.1) | copy-start | bytes 9830404
  142.8 3.4 %copy-start.27 = (bf16[16,80,640]{2,1,0:T(8,128)(2,1)}, bf16[16,80,640]{2,1,0:T(8,128)(2,1)S(1)}, u32[]{:S(2)}) copy-start(bf16[16,80,640]{2,1,0:T(8,128)(2,1)S(1)} %get-tuple-element.83) | copy-start | bytes 4915204
  142.9 5.9 %copy-start.2 = (bf16[2560,640]{1,0:T(8,128)(2,1)S(1)}, bf16[2560,640]{1,0:T(8,128)(2,1)}, u32[]{:S(2)}) copy-start(bf16[2560,640]{1,0:T(8,128)(2,1)} %refs_6_.1) | copy-start | bytes 9830404
  146.2 1.3 copy-start.16
  147.5 1.2 copy-start.29
  157.8 1.9 copy-start
  159.8 4.2 %collective-permute-start.10 = (bf16[16,80,640]{2,1,0:T(8,128)(2,1)}, bf16[16,80,640]{2,1,0:T(8,128)(2,1)}, u32[]{:S(2)}, u32[]{:S(2)}) collective-permute-start(bf16[16,80,640]{2,1,0:T(8,128)(2,1)} %copy-done.29), channel_id=1, source_target_pairs={{0,4},{1,5},{2,6},{3,7},{4,0},{5,1},{6,2},{7,3},{8,12},{9,13},{10,... | collective-permute-start | bytes 4915208 | tf_op jit(solution)/shard_map/ppermute | solution.py:651
  160.5 5.9 %collective-permute-start.6 = (bf16[16,80,640]{2,1,0:T(8,128)(2,1)}, bf16[16,80,640]{2,1,0:T(8,128)(2,1)}, u32[]{:S(2)}, u32[]{:S(2)}) collective-permute-start(bf16[16,80,640]{2,1,0:T(8,128)(2,1)} %copy-done.28), channel_id=1, source_target_pairs={{0,4},{1,5},{2,6},{3,7},{4,0},{5,1},{6,2},{7,3},{8,12},{9,13},{10,... | collective-permute-start | bytes 4915208 | tf_op jit(solution)/shard_map/ppermute | solution.py:651
  160.6 8.4 %collective-permute-start.21 = (bf16[16,80,640]{2,1,0:T(8,128)(2,1)}, bf16[16,80,640]{2,1,0:T(8,128)(2,1)}, u32[]{:S(2)}, u32[]{:S(2)}) collective-permute-start(bf16[16,80,640]{2,1,0:T(8,128)(2,1)} %copy-done.27), channel_id=1, source_target_pairs={{0,4},{1,5},{2,6},{3,7},{4,0},{5,1},{6,2},{7,3},{8,12},{9,13},{10,... | collective-permute-start | bytes 4915208 | tf_op jit(solution)/shard_map/ppermute | solution.py:651
  161.0 10.2 %collective-permute-start.17 = (bf16[16,80,640]{2,1,0:T(8,128)(2,1)}, bf16[16,80,640]{2,1,0:T(8,128)(2,1)}, u32[]{:S(2)}, u32[]{:S(2)}) collective-permute-start(bf16[16,80,640]{2,1,0:T(8,128)(2,1)} %copy-done.26), channel_id=1, source_target_pairs={{0,4},{1,5},{2,6},{3,7},{4,0},{5,1},{6,2},{7,3},{8,12},{9,13},{10,... | collective-permute-start | bytes 4915208 | tf_op jit(solution)/shard_map/ppermute | solution.py:651
  166.0 9.5 %collective-permute-start.11 = (bf16[4,80,640]{2,1,0:T(8,128)(2,1)}, bf16[4,80,640]{2,1,0:T(8,128)(2,1)}, u32[]{:S(2)}, u32[]{:S(2)}) collective-permute-start(bf16[4,80,640]{2,1,0:T(8,128)(2,1)} %fusion.16), channel_id=1, source_target_pairs={{0,8},{1,9},{2,10},{3,11},{4,28},{5,29},{6,30},{7,31},{8,16},{9,17... | collective-permute-start | bytes 1228808 | tf_op jit(solution)/shard_map/ppermute | solution.py:651
  166.5 9.0 %copy-start.17 = (bf16[16,80,640]{2,1,0:T(8,128)(2,1)S(1)}, bf16[16,80,640]{2,1,0:T(8,128)(2,1)}, u32[]{:S(2)}) copy-start(bf16[16,80,640]{2,1,0:T(8,128)(2,1)} %copy-done.16) | copy-start | bytes 4915204
  167.8 11.9 %collective-permute-start.7 = (bf16[4,80,640]{2,1,0:T(8,128)(2,1)S(1)}, bf16[4,80,640]{2,1,0:T(8,128)(2,1)S(1)}, u32[]{:S(2)}, u32[]{:S(2)}) collective-permute-start(bf16[4,80,640]{2,1,0:T(8,128)(2,1)S(1)} %fusion.12), channel_id=1, source_target_pairs={{0,8},{1,9},{2,10},{3,11},{4,28},{5,29},{6,30},{7,31},{8,16},{9,17... | collective-permute-start | bytes 1228808 | tf_op jit(solution)/shard_map/ppermute | solution.py:651
  170.1 9.6 %copy-start.15 = (bf16[16,80,640]{2,1,0:T(8,128)(2,1)S(1)}, bf16[16,80,640]{2,1,0:T(8,128)(2,1)}, u32[]{:S(2)}) copy-start(bf16[16,80,640]{2,1,0:T(8,128)(2,1)} %copy-done.14) | copy-start | bytes 4915204
  170.2 10.8 %collective-permute-start.22 = (bf16[4,80,640]{2,1,0:T(8,128)(2,1)S(1)}, bf16[4,80,640]{2,1,0:T(8,128)(2,1)S(1)}, u32[]{:S(2)}, u32[]{:S(2)}) collective-permute-start(bf16[4,80,640]{2,1,0:T(8,128)(2,1)S(1)} %fusion.24), channel_id=1, source_target_pairs={{0,32},{1,33},{2,34},{3,35},{4,100},{5,101},{6,102},{7,103},{8,40}... | collective-permute-start | bytes 1228808 | tf_op jit(solution)/shard_map/ppermute | solution.py:651
  172.4 11.6 %collective-permute-start.18 = (bf16[4,80,640]{2,1,0:T(8,128)(2,1)S(1)}, bf16[4,80,640]{2,1,0:T(8,128)(2,1)S(1)}, u32[]{:S(2)}, u32[]{:S(2)}) collective-permute-start(bf16[4,80,640]{2,1,0:T(8,128)(2,1)S(1)} %fusion.20), channel_id=1, source_target_pairs={{0,32},{1,33},{2,34},{3,35},{4,100},{5,101},{6,102},{7,103},{8,40}... | collective-permute-start | bytes 1228808 | tf_op jit(solution)/shard_map/ppermute | solution.py:651
  176.8 9.2 %collective-permute-start.12 = (bf16[4,80,640]{2,1,0:T(8,128)(2,1)S(1)}, bf16[4,80,640]{2,1,0:T(8,128)(2,1)S(1)}, u32[]{:S(2)}, u32[]{:S(2)}) collective-permute-start(bf16[4,80,640]{2,1,0:T(8,128)(2,1)S(1)} %fusion.8), channel_id=1, source_target_pairs={{0,8},{1,9},{2,10},{3,11},{4,28},{5,29},{6,30},{7,31},{8,16},{9,17... | collective-permute-start | bytes 1228808 | tf_op jit(solution)/shard_map/ppermute | solution.py:651
  180.9 9.5 %collective-permute-start.8 = (bf16[4,80,640]{2,1,0:T(8,128)(2,1)S(1)}, bf16[4,80,640]{2,1,0:T(8,128)(2,1)S(1)}, u32[]{:S(2)}, u32[]{:S(2)}) collective-permute-start(bf16[4,80,640]{2,1,0:T(8,128)(2,1)S(1)} %fusion.11), channel_id=1, source_target_pairs={{0,8},{1,9},{2,10},{3,11},{4,28},{5,29},{6,30},{7,31},{8,16},{9,17... | collective-permute-start | bytes 1228808 | tf_op jit(solution)/shard_map/ppermute | solution.py:651
  182.2 9.5 %collective-permute-start.23 = (bf16[4,80,640]{2,1,0:T(8,128)(2,1)S(1)}, bf16[4,80,640]{2,1,0:T(8,128)(2,1)S(1)}, u32[]{:S(2)}, u32[]{:S(2)}) collective-permute-start(bf16[4,80,640]{2,1,0:T(8,128)(2,1)S(1)} %fusion.2), channel_id=1, source_target_pairs={{0,32},{1,33},{2,34},{3,35},{4,100},{5,101},{6,102},{7,103},{8,40}... | collective-permute-start | bytes 1228808 | tf_op jit(solution)/shard_map/ppermute | solution.py:651
  185.1 10.7 %collective-permute-start.19 = (bf16[4,80,640]{2,1,0:T(8,128)(2,1)S(1)}, bf16[4,80,640]{2,1,0:T(8,128)(2,1)S(1)}, u32[]{:S(2)}, u32[]{:S(2)}) collective-permute-start(bf16[4,80,640]{2,1,0:T(8,128)(2,1)S(1)} %fusion.5), channel_id=1, source_target_pairs={{0,32},{1,33},{2,34},{3,35},{4,100},{5,101},{6,102},{7,103},{8,40}... | collective-permute-start | bytes 1228808 | tf_op jit(solution)/shard_map/ppermute | solution.py:651
  187.2 9.9 %collective-permute-start.13 = (bf16[4,80,640]{2,1,0:T(8,128)(2,1)S(1)}, bf16[4,80,640]{2,1,0:T(8,128)(2,1)S(1)}, u32[]{:S(2)}, u32[]{:S(2)}) collective-permute-start(bf16[4,80,640]{2,1,0:T(8,128)(2,1)S(1)} %fusion.7), channel_id=1, source_target_pairs={{0,8},{1,9},{2,10},{3,11},{4,28},{5,29},{6,30},{7,31},{8,16},{9,17... | collective-permute-start | bytes 1228808 | tf_op jit(solution)/shard_map/ppermute | solution.py:651
  191.6 9.2 %collective-permute-start.9 = (bf16[4,80,640]{2,1,0:T(8,128)(2,1)S(1)}, bf16[4,80,640]{2,1,0:T(8,128)(2,1)S(1)}, u32[]{:S(2)}, u32[]{:S(2)}) collective-permute-start(bf16[4,80,640]{2,1,0:T(8,128)(2,1)S(1)} %fusion.10), channel_id=1, source_target_pairs={{0,8},{1,9},{2,10},{3,11},{4,28},{5,29},{6,30},{7,31},{8,16},{9,17... | collective-permute-start | bytes 1228808 | tf_op jit(solution)/shard_map/ppermute | solution.py:651
  192.8 12.9 %collective-permute-start.24 = (bf16[4,80,640]{2,1,0:T(8,128)(2,1)S(1)}, bf16[4,80,640]{2,1,0:T(8,128)(2,1)S(1)}, u32[]{:S(2)}, u32[]{:S(2)}) collective-permute-start(bf16[4,80,640]{2,1,0:T(8,128)(2,1)S(1)} %fusion.1), channel_id=1, source_target_pairs={{0,32},{1,33},{2,34},{3,35},{4,100},{5,101},{6,102},{7,103},{8,40}... | collective-permute-start | bytes 1228808 | tf_op jit(solution)/shard_map/ppermute | solution.py:651
  197.0 11.3 %collective-permute-start.20 = (bf16[4,80,640]{2,1,0:T(8,128)(2,1)S(1)}, bf16[4,80,640]{2,1,0:T(8,128)(2,1)S(1)}, u32[]{:S(2)}, u32[]{:S(2)}) collective-permute-start(bf16[4,80,640]{2,1,0:T(8,128)(2,1)S(1)} %fusion.4), channel_id=1, source_target_pairs={{0,32},{1,33},{2,34},{3,35},{4,100},{5,101},{6,102},{7,103},{8,40}... | collective-permute-start | bytes 1228808 | tf_op jit(solution)/shard_map/ppermute | solution.py:651
  202.1 23.5 %collective-permute-start.16 = (bf16[2,80,640]{2,1,0:T(8,128)(2,1)S(1)}, bf16[2,80,640]{2,1,0:T(8,128)(2,1)}, u32[]{:S(2)}, u32[]{:S(2)}) collective-permute-start(bf16[2,80,640]{2,1,0:T(8,128)(2,1)S(1)} %pad_maximum_fusion.2), channel_id=1, source_target_pairs={{0,64},{1,65},{2,66},{3,67},{4,68},{5,69},{6,70},{7,71},{8,72},{9,... | collective-permute-start | bytes 614408 | tf_op jit(solution)/shard_map/ppermute | solution.py:651
  205.1 20.6 %collective-permute-start.15 = (bf16[2,80,640]{2,1,0:T(8,128)(2,1)}, bf16[2,80,640]{2,1,0:T(8,128)(2,1)}, u32[]{:S(2)}, u32[]{:S(2)}) collective-permute-start(bf16[2,80,640]{2,1,0:T(8,128)(2,1)} %pad_maximum_fusion.1), channel_id=1, source_target_pairs={{0,96},{1,97},{2,98},{3,99},{4,100},{5,101},{6,102},{7,103},{8,104... | collective-permute-start | bytes 614408 | tf_op jit(solution)/shard_map/ppermute | solution.py:651
  209.5 7.7 %collective-permute-start.27 = (bf16[2,80,640]{2,1,0:T(8,128)(2,1)S(1)}, bf16[2,80,640]{2,1,0:T(8,128)(2,1)S(1)}, u32[]{:S(2)}, u32[]{:S(2)}) collective-permute-start(bf16[2,80,640]{2,1,0:T(8,128)(2,1)S(1)} %pad_maximum_fusion.5), channel_id=1, source_target_pairs={{0,16},{1,17},{2,18},{3,19},{4,20},{5,21},{6,22},{7,23},{8,24},{9,... | collective-permute-start | bytes 614408 | tf_op jit(solution)/shard_map/ppermute | solution.py:651
  211.5 10.7 %collective-permute-start.26 = (bf16[2,80,640]{2,1,0:T(8,128)(2,1)S(1)}, bf16[2,80,640]{2,1,0:T(8,128)(2,1)S(1)}, u32[]{:S(2)}, u32[]{:S(2)}) collective-permute-start(bf16[2,80,640]{2,1,0:T(8,128)(2,1)S(1)} %pad_maximum_fusion.4), channel_id=1, source_target_pairs={{0,24},{1,25},{2,26},{3,27},{4,28},{5,29},{6,30},{7,31},{8,0},{9,1... | collective-permute-start | bytes 614408 | tf_op jit(solution)/shard_map/ppermute | solution.py:651
  215.6 7.0 %collective-permute-start.25 = (bf16[2,80,640]{2,1,0:T(8,128)(2,1)S(1)}, bf16[2,80,640]{2,1,0:T(8,128)(2,1)S(1)}, u32[]{:S(2)}, u32[]{:S(2)}) collective-permute-start(bf16[2,80,640]{2,1,0:T(8,128)(2,1)S(1)} %pad_maximum_fusion.3), channel_id=1, source_target_pairs={{0,8},{1,9},{2,10},{3,11},{4,12},{5,13},{6,14},{7,15},{8,16},{9,17... | collective-permute-start | bytes 614408 | tf_op jit(solution)/shard_map/ppermute | solution.py:651
  217.2 8.5 %collective-permute-start.14 = (bf16[2,80,640]{2,1,0:T(8,128)(2,1)S(1)}, bf16[2,80,640]{2,1,0:T(8,128)(2,1)S(1)}, u32[]{:S(2)}, u32[]{:S(2)}) collective-permute-start(bf16[2,80,640]{2,1,0:T(8,128)(2,1)S(1)} %pad_maximum_fusion), channel_id=1, source_target_pairs={{0,32},{1,33},{2,34},{3,35},{4,36},{5,37},{6,38},{7,39},{8,40},{9,... | collective-permute-start | bytes 614408 | tf_op jit(solution)/shard_map/ppermute | solution.py:651
Sparse Core Ops, SparseCore 0:
  159.9 41.8 reduce-scatter.1

commit v4 on v3

--- a/solution.py
+++ b/solution.py
@@ -730,9 +730,10 @@
 
     held = held_in_vmem(skip_gain, (w_key, w_value, w_query, w_out))
     tokens_on, _ = lax.optimization_barrier((passed(token_sides), held[0]))
-    grad_sides, tokens_on = lax.optimization_barrier((grad_sides, tokens_on))
+    tokens_far = moved(tokens_on, "z", (1, -1))
+    grad_sides, tokens_far = lax.optimization_barrier((grad_sides, tokens_far))
     grads_on = passed(grad_sides)
-    shards = (tokens, *token_sides, moved(tokens_on, "z", (1, -1)))
+    shards = (tokens, *token_sides, tokens_far)
     grad_shards = (cotangent, *grad_sides, moved(grads_on, "z", (1, -1)))
     ids = (chip_z + jnp.array([0, SIDE - 1, 1, 2], jnp.int32)) % SIDE
 
@@ -784,10 +785,10 @@
     outward = lax.psum_scatter(outward, "tp", scatter_dimension=0, tiled=True)[0]
     mixed, grad_input = outward[:row_count], outward[row_count:]
     halves = [each.total() for each in sums]
-    grad_out, grad_key = second_axis_sums(halves[0::2], "y", places)
-    grad_query, grad_value, mixed, grad_input = second_axis_sums(
-        halves[1::2], "x", places, (mixed, grad_input)
+    grad_out, grad_key, mixed, grad_input = second_axis_sums(
+        halves[0::2], "y", places, (mixed, grad_input)
     )
+    grad_query, grad_value = second_axis_sums(halves[1::2], "x", places)
     grad_out = grad_out.T
     return (mixed, grad_input, grad_query, grad_key, grad_value, grad_out, grad_filter, grad_init)
 

time: 237 us -> 245 us (1.034)
  starting transfers between devices: 33.9 us -> 26.8 us
  local copies, waits for them, and re-layouts: 32.1 us -> 38.2 us
  waiting for transfers between devices: 43.9 us -> 49.3 us
  Pallas kernels: 59.5 us -> 62.9 us
    ppermute x28, starting transfers between devices: 26.3 us -> 19.1 us  [moved(): return lax.ppermute(value, ('seq', 'tp'), pairs)]
    unnamed x66 -> x84, local copies, waits for them, and re-layouts: 23 us -> 29.5 us
    all_to_all x1, waiting for transfers between devices: 6.03 us -> 9.55 us  [exchanged(): return lax.all_to_all(value, 'seq', 0, 0, tiled=True)]
    select_n x2, other arithmetic: 0.11 us -> 2.96 us  [passed(): return jnp.where(core == 0, below, above)]
  transfers between devices with their start and end apart: 30 -> 30, of which waited for: 16 -> 20; matrix products, arithmetic and copies ran while one was open for 14% -> 13% of each run, Pallas kernels for 6% -> 7%
where the time goes in v4:
time: 245 us; the launch traced here: 243 us
  Pallas kernels  62.9 us (26%)
  waiting for transfers between devices  49.3 us (20%)
  local copies, waits for them, and re-layouts  38.2 us (16%)
  blocking collectives  27.8 us (11%)
  starting transfers between devices  26.8 us (11%)
  other arithmetic  23.5 us (10%)
  between operations  14.6 us (6%)
    ppermute x28, waiting for transfers between devices, moved(): return lax.ppermute(value, ('seq', 'tp'), pairs)  39.8 us
    unnamed x84, local copies, waits for them, and re-layouts  29.5 us
    all_to_all x1, blocking collectives, exchanged(): return lax.all_to_all(value, 'seq', 0, 0, tiled=True)  27.8 us
    convert_element_type x16, other arithmetic, added(): return (left.astype(F32) + right.astype(F32)).astype(BF16)  19.9 us
    ppermute x28, starting transfers between devices, moved(): return lax.ppermute(value, ('seq', 'tp'), pairs)  19.1 us
    pallas_call x1, Pallas kernels, sequence_part(): pl.pallas_call(functools.partial(sequence_kernel, group), out_shape=jax.S...  18.4 us
    pallas_call x4, Pallas kernels, weight_partial(): pl.pallas_call(functools.partial(weight_kernel, rows), in_specs=anywhere(...  13.4 us
    all_to_all x1, waiting for transfers between devices, exchanged(): return lax.all_to_all(value, 'seq', 0, 0, tiled=True)  9.55 us
  transfers between devices with their start and end apart: 30, of which 20 were waited for; matrix products, arithmetic and copies ran while one was open for 13% of the time, Pallas kernels for 7%

profile of v4, /device:TPU:0, one launch (start us, length us, event | category | flops | bytes accessed | tf_op | source)
XLA Modules:
  0.0 243.1 jit_solution(5159156276476708287)
XLA Ops:
  7.2 2.1 collective-permute-start.2
  9.2 2.2 collective-permute-start.3
  11.4 3.2 %collective-permute-start.1 = (bf16[384,640]{1,0:T(8,128)(2,1)}, bf16[384,640]{1,0:T(8,128)(2,1)}, u32[]{:S(2)}, u32[]{:S(2)}) collective-permute-start(bf16[384,640]{1,0:T(8,128)(2,1)} %refs_4_.1), channel_id=1, source_target_pairs={{0,3},{1,0},{2,1},{3,2},{4,7},{5,4},{6,5},{7,6},{8,11},{9,8},{10,9... | collective-permute-start | bytes 1474568 | tf_op jit(solution)/shard_map/ppermute | solution.py:651
  14.7 1.9 copy-done.7
  16.6 1.9 copy-done.9
  18.5 1.9 copy-done.11
  20.5 1.9 copy-done.13
  23.1 1.6 shard_map.179
  24.7 1.7 copy-done.1
  26.3 1.7 copy-done.3
  28.0 1.8 copy-done.5
  29.8 1.9 broadcast_select_fusion.1
  31.7 1.7 collective-permute-done.second_ref.refs_5_
  33.9 8.2 %collective-permute-done.4.shard_ref.refs_3_ = bf16[384,640]{1,0:T(8,128)(2,1)} collective-permute-done((bf16[384,640]{1,0:T(8,128)(2,1)}, bf16[384,640]{1,0:T(8,128)(2,1)}, u32[]{:S(2)}, u32[]{:S(2)}) %collective-permute-start.4) | collective-permute-done | bytes 491552 | tf_op jit(solution)/shard_map/ppermute | solution.py:651
  43.3 1.9 copy-done.2
  45.2 1.9 copy-done.4
  47.2 5.4 %shard_map.180 = (f32[384,640]{1,0:T(8,128)S(1)}, f32[384,640]{1,0:T(8,128)S(1)}, f32[384,640]{1,0:T(8,128)S(1)}) custom-call(bf16[384,640]{1,0:T(8,128)(2,1)S(1)} %copy-done.17, bf16[384,640]{1,0:T(8,128)(2,1)} %collective-permute-done.2.refs_1_, bf16[384,640]{1,0:T(8,128)(2,1)} %collective-permute-done.3.refs_2_, ...), custom_call_target="tpu_custom_call" | custom-call | flops 2831155200 | bytes 12000000 | tf_op jit(solution)/shard_map/pallas_call | solution.py:336
  52.6 2.7 %shard_map.182.sum_ref = f32[384,640]{1,0:T(8,128)S(1)} custom-call(f32[384,640]{1,0:T(8,128)S(1)} %get-tuple-element.54.query_sum.after_ref, bf16[384,640]{1,0:T(8,128)(2,1)S(1)} %copy-done.21, bf16[384,640]{1,0:T(8,128)(2,1)} %collective-permute-done.second_ref.refs_5_, bf16[384,640]{1,0:T(8,128)(2,1)} %collective-permute-done.1.third_ref.refs_6_, ...), custom_call_target="tpu_custom_call" | custom-call | flops 943718400 | bytes 6000000 | tf_op jit(solution)/shard_map/pallas_call | solution.py:402
  55.3 2.6 %shard_map.181 = (bf16[32,40,384]{2,1,0:T(8,128)(2,1)S(1)}, bf16[384,640]{1,0:T(8,128)(2,1)S(1)}) custom-call(bf16[384,640]{1,0:T(8,128)(2,1)} %collective-permute-done.4.shard_ref.refs_3_, bf16[2560,640]{1,0:T(8,128)(2,1)S(1)} %get-tuple-element.47.refs_3_.key_ref, bf16[2560,640]{1,0:T(8,128)(2,1)S(1)} %copy-done.2, bf16[2560,640]{1,0:T(8,128)(2,1)S(1)} %copy-done.4, ...), custom_call_target="tpu_custom_call" | custom-call | flops 943718400 | bytes 12000000 | tf_op jit(solution)/shard_map/pallas_call | solution.py:372
  57.9 2.5 %shard_map.183 = (bf16[384,640]{1,0:T(8,128)(2,1)S(1)}, bf16[32,60,384]{2,1,0:T(8,128)(2,1)}) custom-call(bf16[32,40,384]{2,1,0:T(8,128)(2,1)S(1)} %get-tuple-element.55.kv_ref, bf16[384,640]{1,0:T(8,128)(2,1)S(1)} %collective-permute-done.5.shard_ref.refs_7_, bf16[640,2560]{1,0:T(8,128)(2,1)S(1)} %copy-done.6, f32[384,640]{1,0:T(8,128)S(1)} %shard_map.182.sum_ref, ...), custom_call_target="tpu_custom_call" | custom-call | flops 314572800 | bytes 6000000 | tf_op jit(solution)/shard_map/pallas_call | solution.py:432
  60.5 7.4 %all-to-all-start = ((bf16[32,60,384]{2,1,0:T(8,128)(2,1)}), bf16[32,60,384]{2,1,0:T(8,128)(2,1)}, u32[]{:S(2)}, u32[]{:S(2)}) async-start(bf16[32,60,384]{2,1,0:T(8,128)(2,1)} %get-tuple-element.60.after_ref), calls=%async_computation | async-start | bytes 3145728 | tf_op jit(solution)/shard_map/all_to_all | solution.py:753
  71.3 1.6 copy.45.cols_ref
  73.3 5.7 %shard_map.184 = (bf16[4,640,384]{2,1,0:T(8,128)(2,1)S(1)}, bf16[4,640,384]{2,1,0:T(8,128)(2,1)S(1)}, f32[8,128]{1,0:T(8,128)S(1)}) custom-call(bf16[32,60,384]{2,1,0:T(8,128)(2,1)} %get-tuple-element.60.after_ref, bf16[384,640]{1,0:T(8,128)(2,1)S(1)} %copy-done.18, bf16[384,640]{1,0:T(8,128)(2,1)} %collective-permute-done.2.refs_1_, ...), custom_call_target="tpu_custom_call" | custom-call | flops 1966080 | bytes 8000000 | tf_op jit(solution)/shard_map/pallas_call | solution.py:516
  79.0 1.3 copy-done.31
  80.2 1.3 copy-done.33
  81.5 9.5 %all-to-all-done.in_ref = bf16[32,60,384]{2,1,0:T(8,128)(2,1)} async-done(((bf16[32,60,384]{2,1,0:T(8,128)(2,1)}), bf16[32,60,384]{2,1,0:T(8,128)(2,1)}, u32[]{:S(2)}, u32[]{:S(2)}) %all-to-all-start) | async-done | bytes 1474592 | tf_op jit(solution)/shard_map/all_to_all | solution.py:753
  91.1 1.3 copy-done.27
  92.4 18.4 %shard_map.185 = bf16[32,67,384]{2,1,0:T(8,128)(2,1)S(1)} custom-call(f32[8,128]{1,0:T(8,128)S(1)} %get-tuple-element.61.after_ref, bf16[32,60,384]{2,1,0:T(8,128)(2,1)} %all-to-all-done.in_ref, f32[2,20,64]{2,1,0:T(8,128)S(1)} %get-tuple-element.109.rows_ref, f32[2,20,64,1]{3,2,1,0:T(8,128)S(1)} %copy-done.27, ...), custom_call_target="tpu_custom_call" | custom-call | flops 22000001024 | bytes 5000000 | tf_op jit(solution)/shard_map/pallas_call | solution.py:286
  110.8 27.8 %all_to_all.10.returned_ref = bf16[32,67,384]{2,1,0:T(8,128)(2,1)S(1)} all-to-all(bf16[32,67,384]{2,1,0:T(8,128)(2,1)S(1)} %shard_map.185), channel_id=1, replica_groups=mesh['seq'=32,'tp'=4] {'seq'}, dimensions={0} | all-to-all | bytes 3293184 | tf_op jit(solution)/shard_map/all_to_all | solution.py:753
  138.6 1.5 shard_map.186
  140.1 3.4 %shard_map.187 = (bf16[16,80,640]{2,1,0:T(8,128)(2,1)S(1)}, bf16[16,80,640]{2,1,0:T(8,128)(2,1)S(1)}, f32[8,128]{1,0:T(8,128)S(1)}) custom-call(bf16[384,640]{1,0:T(8,128)(2,1)S(1)} %get-tuple-element.63.after_ref.narrow_ref.refs_4_, bf16[4,640,384]{2,1,0:T(8,128)(2,1)S(1)} %copy-done.34, ...), custom_call_target="tpu_custom_call" | custom-call | flops 1258291200 | bytes 6000000 | tf_op jit(solution)/shard_map/pallas_call | solution.py:581
  143.5 1.2 copy-done.36
  144.7 3.4 %shard_map.188 = (bf16[16,80,640]{2,1,0:T(8,128)(2,1)S(1)}, bf16[16,80,640]{2,1,0:T(8,128)(2,1)S(1)}, f32[8,128]{1,0:T(8,128)S(1)}) custom-call(f32[8,128]{1,0:T(8,128)S(1)} %get-tuple-element.67.after_ref, bf16[4,640,384]{2,1,0:T(8,128)(2,1)S(1)} %copy-done.32, bf16[384,640]{1,0:T(8,128)(2,1)S(1)} %get-tuple-element.69.narrow_ref.refs_1_, ...), custom_call_target="tpu_custom_call" | custom-call | flops 1258291200 | bytes 6000000 | tf_op jit(solution)/shard_map/pallas_call | solution.py:581
  148.1 1.2 copy-done.35
  149.3 3.4 %shard_map.189 = (bf16[16,80,640]{2,1,0:T(8,128)(2,1)S(1)}, bf16[16,80,640]{2,1,0:T(8,128)(2,1)S(1)}, f32[8,128]{1,0:T(8,128)S(1)}) custom-call(f32[8,128]{1,0:T(8,128)S(1)} %get-tuple-element.70.after_ref, bf16[4,640,384]{2,1,0:T(8,128)(2,1)S(1)} %copy-done.32, bf16[384,640]{1,0:T(8,128)(2,1)S(1)} %get-tuple-element.71.narrow_ref.refs_2_, ...), custom_call_target="tpu_custom_call" | custom-call | flops 1258291200 | bytes 6000000 | tf_op jit(solution)/shard_map/pallas_call | solution.py:581
  152.7 1.2 copy-done.38
  153.8 3.4 %shard_map.190 = (bf16[16,80,640]{2,1,0:T(8,128)(2,1)S(1)}, bf16[16,80,640]{2,1,0:T(8,128)(2,1)S(1)}, f32[8,128]{1,0:T(8,128)S(1)}) custom-call(f32[8,128]{1,0:T(8,128)S(1)} %get-tuple-element.74.after_ref, bf16[4,640,384]{2,1,0:T(8,128)(2,1)S(1)} %copy-done.32, bf16[384,640]{1,0:T(8,128)(2,1)S(1)} %get-tuple-element.75.narrow_ref.refs_3_, ...), custom_call_target="tpu_custom_call" | custom-call | flops 1258291200 | bytes 6000000 | tf_op jit(solution)/shard_map/pallas_call | solution.py:581
  157.2 1.2 copy-done.25
  158.4 1.2 copy-done.37
  159.6 9.1 %shard_map.191 = bf16[4,768,640]{2,1,0:T(8,128)(2,1)S(1)} custom-call(f32[8,128]{1,0:T(8,128)S(1)} %get-tuple-element.76.refs_0_, bf16[384,640]{1,0:T(8,128)(2,1)S(1)} %get-tuple-element.69.narrow_ref.refs_1_, bf16[384,640]{1,0:T(8,128)(2,1)S(1)} %get-tuple-element.71.narrow_ref.refs_2_, bf16[384,640]{1,0:T(8,128)(2,1)S(1)} %get-tuple-element.75.narrow_ref.refs_3_, ...), custom_call_target="tpu_custom_call" | custom-call | flops 5033164800 | bytes 20000000 | tf_op jit(solution)/shard_map/pallas_call | solution.py:621
  168.7 1.9 copy-done
  172.0 2.9 %collective-permute-done.10 = bf16[16,80,640]{2,1,0:T(8,128)(2,1)} collective-permute-done((bf16[16,80,640]{2,1,0:T(8,128)(2,1)}, bf16[16,80,640]{2,1,0:T(8,128)(2,1)}, u32[]{:S(2)}, u32[]{:S(2)}) %collective-permute-start.10) | collective-permute-done | bytes 1638432 | tf_op jit(solution)/shard_map/ppermute | solution.py:651
  174.8 1.9 fusion.16
  177.2 1.7 fusion.12
  179.5 1.2 fusion.24
  184.0 2.2 collective-permute-done.11
  186.2 1.3 fusion.8
  187.5 2.9 %collective-permute-done.7 = bf16[4,80,640]{2,1,0:T(8,128)(2,1)S(1)} collective-permute-done((bf16[4,80,640]{2,1,0:T(8,128)(2,1)S(1)}, bf16[4,80,640]{2,1,0:T(8,128)(2,1)S(1)}, u32[]{:S(2)}, u32[]{:S(2)}) %collective-permute-start.7) | collective-permute-done | bytes 409632 | tf_op jit(solution)/shard_map/ppermute | solution.py:651
  190.5 1.2 fusion.11
  191.7 1.2 fusion.2
  194.6 1.2 fusion.5
  197.9 4.2 %collective-permute-done.20 = bf16[4,80,640]{2,1,0:T(8,128)(2,1)S(1)} collective-permute-done((bf16[4,80,640]{2,1,0:T(8,128)(2,1)S(1)}, bf16[4,80,640]{2,1,0:T(8,128)(2,1)S(1)}, u32[]{:S(2)}, u32[]{:S(2)}) %collective-permute-start.20) | collective-permute-done | bytes 409632 | tf_op jit(solution)/shard_map/ppermute | solution.py:651
  203.4 3.1 %collective-permute-done.16 = bf16[4,80,640]{2,1,0:T(8,128)(2,1)S(1)} collective-permute-done((bf16[4,80,640]{2,1,0:T(8,128)(2,1)S(1)}, bf16[4,80,640]{2,1,0:T(8,128)(2,1)S(1)}, u32[]{:S(2)}, u32[]{:S(2)}) %collective-permute-start.16) | collective-permute-done | bytes 409632 | tf_op jit(solution)/shard_map/ppermute | solution.py:651
  206.5 1.2 fusion.4
  207.8 1.2 fusion.10
  209.2 3.3 %collective-permute-done.21 = bf16[4,80,640]{2,1,0:T(8,128)(2,1)S(1)} collective-permute-done((bf16[4,80,640]{2,1,0:T(8,128)(2,1)S(1)}, bf16[4,80,640]{2,1,0:T(8,128)(2,1)S(1)}, u32[]{:S(2)}, u32[]{:S(2)}) %collective-permute-start.21) | collective-permute-done | bytes 409632 | tf_op jit(solution)/shard_map/ppermute | solution.py:651
  213.8 3.2 %collective-permute-done.17 = bf16[4,80,640]{2,1,0:T(8,128)(2,1)S(1)} collective-permute-done((bf16[4,80,640]{2,1,0:T(8,128)(2,1)S(1)}, bf16[4,80,640]{2,1,0:T(8,128)(2,1)S(1)}, u32[]{:S(2)}, u32[]{:S(2)}) %collective-permute-start.17) | collective-permute-done | bytes 409632 | tf_op jit(solution)/shard_map/ppermute | solution.py:651
  218.2 1.9 collective-permute-start.24
  220.1 1.5 collective-permute-start.23
  223.8 1.2 fusion.9
  225.2 1.5 collective-permute-start.26
  229.6 2.2 slice_bitcast_fusion
  231.8 2.0 collective-permute-done.27
  233.8 1.6 collective-permute-done.25
  (141 shorter events, 25.9 us)
Async XLA Ops:
  7.2 22.7 %collective-permute-start.2 = (bf16[384,640]{1,0:T(8,128)(2,1)}, bf16[384,640]{1,0:T(8,128)(2,1)}, u32[]{:S(2)}, u32[]{:S(2)}) collective-permute-start(bf16[384,640]{1,0:T(8,128)(2,1)} %refs_0_.5), channel_id=1, source_target_pairs={{0,1},{1,2},{2,3},{3,0},{4,5},{5,6},{6,7},{7,4},{8,9},{9,10},{10,1... | collective-permute-start | bytes 1474568 | tf_op jit(solution)/shard_map/ppermute | solution.py:651
  9.2 20.6 %collective-permute-start.3 = (bf16[384,640]{1,0:T(8,128)(2,1)}, bf16[384,640]{1,0:T(8,128)(2,1)}, u32[]{:S(2)}, u32[]{:S(2)}) collective-permute-start(bf16[384,640]{1,0:T(8,128)(2,1)} %refs_0_.5), channel_id=1, source_target_pairs={{0,3},{1,0},{2,1},{3,2},{4,7},{5,4},{6,5},{7,6},{8,11},{9,8},{10,9... | collective-permute-start | bytes 1474568 | tf_op jit(solution)/shard_map/ppermute | solution.py:651
  11.4 22.0 %collective-permute-start = (bf16[384,640]{1,0:T(8,128)(2,1)}, bf16[384,640]{1,0:T(8,128)(2,1)}, u32[]{:S(2)}, u32[]{:S(2)}) collective-permute-start(bf16[384,640]{1,0:T(8,128)(2,1)} %refs_4_.1), channel_id=1, source_target_pairs={{0,1},{1,2},{2,3},{3,0},{4,5},{5,6},{6,7},{7,4},{8,9},{9,10},{10,1... | collective-permute-start | bytes 1474568 | tf_op jit(solution)/shard_map/ppermute | solution.py:651
  11.4 22.5 %collective-permute-start.1 = (bf16[384,640]{1,0:T(8,128)(2,1)}, bf16[384,640]{1,0:T(8,128)(2,1)}, u32[]{:S(2)}, u32[]{:S(2)}) collective-permute-start(bf16[384,640]{1,0:T(8,128)(2,1)} %refs_4_.1), channel_id=1, source_target_pairs={{0,3},{1,0},{2,1},{3,2},{4,7},{5,4},{6,5},{7,6},{8,11},{9,8},{10,9... | collective-permute-start | bytes 1474568 | tf_op jit(solution)/shard_map/ppermute | solution.py:651
  14.7 1.9 copy-start.7
  16.6 1.9 copy-start.9
  18.5 1.9 copy-start.11
  20.5 1.9 copy-start.13
  24.7 1.7 copy-start.1
  26.3 1.7 copy-start.3
  28.0 1.8 copy-start.5
  29.8 13.4 %copy-start.39 = (s32[4]{0:T(128)S(1)}, s32[4]{0:T(128)}, u32[]{:S(2)}) copy-start(s32[4]{0:T(128)} %constant.271.clone) | copy-start | bytes 52
  31.7 10.4 %collective-permute-start.4 = (bf16[384,640]{1,0:T(8,128)(2,1)}, bf16[384,640]{1,0:T(8,128)(2,1)}, u32[]{:S(2)}, u32[]{:S(2)}) collective-permute-start(bf16[384,640]{1,0:T(8,128)(2,1)} %broadcast_select_fusion.1), channel_id=1, source_target_pairs={{0,1},{1,2},{2,3},{3,0},{4,7},{5,4},{6,5},{7,6},{8,9},{9,10},{10,1... | collective-permute-start | bytes 1474568 | tf_op jit(solution)/shard_map/ppermute | solution.py:651
  31.7 11.6 %copy-start.17 = (bf16[384,640]{1,0:T(8,128)(2,1)S(1)}, bf16[384,640]{1,0:T(8,128)(2,1)}, u32[]{:S(2)}) copy-start(bf16[384,640]{1,0:T(8,128)(2,1)} %refs_0_.5) | copy-start | bytes 1474564
  43.2 14.8 %collective-permute-start.5 = (bf16[384,640]{1,0:T(8,128)(2,1)S(1)}, bf16[384,640]{1,0:T(8,128)(2,1)S(1)}, u32[]{:S(2)}, u32[]{:S(2)}) collective-permute-start(bf16[384,640]{1,0:T(8,128)(2,1)S(1)} %broadcast_select_fusion), channel_id=1, source_target_pairs={{0,1},{1,2},{2,3},{3,0},{4,7},{5,4},{6,5},{7,6},{8,9},{9,10},{10,1... | collective-permute-start | bytes 1474568 | tf_op jit(solution)/shard_map/ppermute | solution.py:651
  43.3 1.9 copy-start.2
  45.2 1.9 copy-start.4
  47.1 5.4 %copy-start.6 = (bf16[640,2560]{1,0:T(8,128)(2,1)S(1)}, bf16[640,2560]{1,0:T(8,128)(2,1)}, u32[]{:S(2)}) copy-start(bf16[640,2560]{1,0:T(8,128)(2,1)} %copy-done.5) | copy-start | bytes 9830404
  47.1 5.4 %copy-start.21 = (bf16[384,640]{1,0:T(8,128)(2,1)S(1)}, bf16[384,640]{1,0:T(8,128)(2,1)}, u32[]{:S(2)}) copy-start(bf16[384,640]{1,0:T(8,128)(2,1)} %refs_4_.1) | copy-start | bytes 1474564
  57.9 2.6 %copy-start.15 = (bf16[384,640]{1,0:T(8,128)(2,1)}, bf16[384,640]{1,0:T(8,128)(2,1)S(1)}, u32[]{:S(2)}) copy-start(bf16[384,640]{1,0:T(8,128)(2,1)S(1)} %get-tuple-element.59.query_ref) | copy-start | bytes 1474564
  57.9 2.6 %copy-start.19 = (bf16[384,640]{1,0:T(8,128)(2,1)}, bf16[384,640]{1,0:T(8,128)(2,1)S(1)}, u32[]{:S(2)}) copy-start(bf16[384,640]{1,0:T(8,128)(2,1)S(1)} %collective-permute-done.5.shard_ref.refs_7_) | copy-start | bytes 1474564
  60.5 9.6 %copy-start.28 = (bf16[384,640]{1,0:T(8,128)(2,1)}, bf16[384,640]{1,0:T(8,128)(2,1)S(1)}, u32[]{:S(2)}) copy-start(bf16[384,640]{1,0:T(8,128)(2,1)S(1)} %get-tuple-element.62.gated_ref) | copy-start | bytes 1474564
  60.5 30.6 %all-to-all-start = ((bf16[32,60,384]{2,1,0:T(8,128)(2,1)}), bf16[32,60,384]{2,1,0:T(8,128)(2,1)}, u32[]{:S(2)}, u32[]{:S(2)}) async-start(bf16[32,60,384]{2,1,0:T(8,128)(2,1)} %get-tuple-element.60.after_ref), calls=%async_computation | async-start | bytes 3145728 | tf_op jit(solution)/shard_map/all_to_all | solution.py:753
  67.9 5.3 %copy-start.18 = (bf16[384,640]{1,0:T(8,128)(2,1)S(1)}, bf16[384,640]{1,0:T(8,128)(2,1)}, u32[]{:S(2)}) copy-start(bf16[384,640]{1,0:T(8,128)(2,1)} %refs_0_.5) | copy-start | bytes 1474564
  68.0 5.3 %copy-start.20 = (bf16[384,640]{1,0:T(8,128)(2,1)S(1)}, bf16[384,640]{1,0:T(8,128)(2,1)}, u32[]{:S(2)}) copy-start(bf16[384,640]{1,0:T(8,128)(2,1)} %copy-done.19) | copy-start | bytes 1474564
  68.0 5.3 %copy-start.22 = (bf16[384,640]{1,0:T(8,128)(2,1)S(1)}, bf16[384,640]{1,0:T(8,128)(2,1)}, u32[]{:S(2)}) copy-start(bf16[384,640]{1,0:T(8,128)(2,1)} %refs_4_.1) | copy-start | bytes 1474564
  68.0 161.6 %reduce-scatter.2.cloned.1.call-start = ((), (), s32[]{:S(2)}) async-start(), calls=%async_computation.3 | async-start | bytes 4915200 | tf_op jit(solution)/shard_map/reduce_scatter | solution.py:785
  79.0 1.3 copy-start.31
  80.2 1.3 copy-start.33
  91.1 1.3 copy-start.27
  110.8 27.8 %copy-start.16 = (bf16[384,640]{1,0:T(8,128)(2,1)S(1)}, bf16[384,640]{1,0:T(8,128)(2,1)}, u32[]{:S(2)}) copy-start(bf16[384,640]{1,0:T(8,128)(2,1)} %copy-done.15) | copy-start | bytes 1474564
  110.8 27.8 %copy-start.29 = (bf16[384,640]{1,0:T(8,128)(2,1)S(1)}, bf16[384,640]{1,0:T(8,128)(2,1)}, u32[]{:S(2)}) copy-start(bf16[384,640]{1,0:T(8,128)(2,1)} %copy-done.28) | copy-start | bytes 1474564
  138.6 1.5 copy-start.34
  140.1 4.5 %copy-start.32 = (bf16[4,640,384]{2,1,0:T(8,128)(2,1)S(1)}, bf16[4,640,384]{2,1,0:T(8,128)(2,1)}, u32[]{:S(2)}) copy-start(bf16[4,640,384]{2,1,0:T(8,128)(2,1)} %copy-done.31) | copy-start | bytes 5898244
  144.7 14.9 %copy-start.12 = (bf16[2560,640]{1,0:T(8,128)(2,1)S(1)}, bf16[2560,640]{1,0:T(8,128)(2,1)}, u32[]{:S(2)}) copy-start(bf16[2560,640]{1,0:T(8,128)(2,1)} %refs_5_.1) | copy-start | bytes 9830404
  144.7 14.9 %copy-start.14 = (bf16[640,2560]{1,0:T(8,128)(2,1)S(1)}, bf16[640,2560]{1,0:T(8,128)(2,1)}, u32[]{:S(2)}) copy-start(bf16[640,2560]{1,0:T(8,128)(2,1)} %refs_8_.1) | copy-start | bytes 9830404
  149.3 3.4 %copy-start.23 = (bf16[16,80,640]{2,1,0:T(8,128)(2,1)}, bf16[16,80,640]{2,1,0:T(8,128)(2,1)S(1)}, u32[]{:S(2)}) copy-start(bf16[16,80,640]{2,1,0:T(8,128)(2,1)S(1)} %get-tuple-element.79) | copy-start | bytes 4915204
  149.3 10.3 %copy-start.10 = (bf16[2560,640]{1,0:T(8,128)(2,1)S(1)}, bf16[2560,640]{1,0:T(8,128)(2,1)}, u32[]{:S(2)}) copy-start(bf16[2560,640]{1,0:T(8,128)(2,1)} %refs_7_.1) | copy-start | bytes 9830404
  153.8 5.8 %copy-start.8 = (bf16[2560,640]{1,0:T(8,128)(2,1)S(1)}, bf16[2560,640]{1,0:T(8,128)(2,1)}, u32[]{:S(2)}) copy-start(bf16[2560,640]{1,0:T(8,128)(2,1)} %refs_6_.1) | copy-start | bytes 9830404
  168.7 1.9 copy-start
  170.6 4.2 %collective-permute-start.10 = (bf16[16,80,640]{2,1,0:T(8,128)(2,1)}, bf16[16,80,640]{2,1,0:T(8,128)(2,1)}, u32[]{:S(2)}, u32[]{:S(2)}) collective-permute-start(bf16[16,80,640]{2,1,0:T(8,128)(2,1)} %copy-done.38), channel_id=1, source_target_pairs={{0,4},{1,5},{2,6},{3,7},{4,0},{5,1},{6,2},{7,3},{8,12},{9,13},{10,... | collective-permute-start | bytes 4915208 | tf_op jit(solution)/shard_map/ppermute | solution.py:651
  171.4 5.8 %collective-permute-start.6 = (bf16[16,80,640]{2,1,0:T(8,128)(2,1)}, bf16[16,80,640]{2,1,0:T(8,128)(2,1)}, u32[]{:S(2)}, u32[]{:S(2)}) collective-permute-start(bf16[16,80,640]{2,1,0:T(8,128)(2,1)} %copy-done.36), channel_id=1, source_target_pairs={{0,4},{1,5},{2,6},{3,7},{4,0},{5,1},{6,2},{7,3},{8,12},{9,13},{10,... | collective-permute-start | bytes 4915208 | tf_op jit(solution)/shard_map/ppermute | solution.py:651
  171.5 8.1 %collective-permute-start.18 = (bf16[16,80,640]{2,1,0:T(8,128)(2,1)}, bf16[16,80,640]{2,1,0:T(8,128)(2,1)}, u32[]{:S(2)}, u32[]{:S(2)}) collective-permute-start(bf16[16,80,640]{2,1,0:T(8,128)(2,1)} %copy-done.37), channel_id=1, source_target_pairs={{0,4},{1,5},{2,6},{3,7},{4,0},{5,1},{6,2},{7,3},{8,12},{9,13},{10,... | collective-permute-start | bytes 4915208 | tf_op jit(solution)/shard_map/ppermute | solution.py:651
  171.9 10.0 %collective-permute-start.14 = (bf16[16,80,640]{2,1,0:T(8,128)(2,1)}, bf16[16,80,640]{2,1,0:T(8,128)(2,1)}, u32[]{:S(2)}, u32[]{:S(2)}) collective-permute-start(bf16[16,80,640]{2,1,0:T(8,128)(2,1)} %copy-done.35), channel_id=1, source_target_pairs={{0,4},{1,5},{2,6},{3,7},{4,0},{5,1},{6,2},{7,3},{8,12},{9,13},{10,... | collective-permute-start | bytes 4915208 | tf_op jit(solution)/shard_map/ppermute | solution.py:651
  176.7 9.5 %collective-permute-start.11 = (bf16[4,80,640]{2,1,0:T(8,128)(2,1)}, bf16[4,80,640]{2,1,0:T(8,128)(2,1)}, u32[]{:S(2)}, u32[]{:S(2)}) collective-permute-start(bf16[4,80,640]{2,1,0:T(8,128)(2,1)} %fusion.16), channel_id=1, source_target_pairs={{0,32},{1,33},{2,34},{3,35},{4,100},{5,101},{6,102},{7,103},{8,40}... | collective-permute-start | bytes 1228808 | tf_op jit(solution)/shard_map/ppermute | solution.py:651
  176.8 5.1 %copy-start.24 = (bf16[16,80,640]{2,1,0:T(8,128)(2,1)S(1)}, bf16[16,80,640]{2,1,0:T(8,128)(2,1)}, u32[]{:S(2)}) copy-start(bf16[16,80,640]{2,1,0:T(8,128)(2,1)} %copy-done.23) | copy-start | bytes 4915204
  178.9 11.6 %collective-permute-start.7 = (bf16[4,80,640]{2,1,0:T(8,128)(2,1)S(1)}, bf16[4,80,640]{2,1,0:T(8,128)(2,1)S(1)}, u32[]{:S(2)}, u32[]{:S(2)}) collective-permute-start(bf16[4,80,640]{2,1,0:T(8,128)(2,1)S(1)} %fusion.12), channel_id=1, source_target_pairs={{0,32},{1,33},{2,34},{3,35},{4,100},{5,101},{6,102},{7,103},{8,40}... | collective-permute-start | bytes 1228808 | tf_op jit(solution)/shard_map/ppermute | solution.py:651
  180.8 11.0 %collective-permute-start.19 = (bf16[4,80,640]{2,1,0:T(8,128)(2,1)S(1)}, bf16[4,80,640]{2,1,0:T(8,128)(2,1)S(1)}, u32[]{:S(2)}, u32[]{:S(2)}) collective-permute-start(bf16[4,80,640]{2,1,0:T(8,128)(2,1)S(1)} %fusion.24), channel_id=1, source_target_pairs={{0,8},{1,9},{2,10},{3,11},{4,28},{5,29},{6,30},{7,31},{8,16},{9,17... | collective-permute-start | bytes 1228808 | tf_op jit(solution)/shard_map/ppermute | solution.py:651
  183.0 8.7 %copy-start.26 = (bf16[16,80,640]{2,1,0:T(8,128)(2,1)S(1)}, bf16[16,80,640]{2,1,0:T(8,128)(2,1)}, u32[]{:S(2)}) copy-start(bf16[16,80,640]{2,1,0:T(8,128)(2,1)} %copy-done.25) | copy-start | bytes 4915204
  183.0 11.6 %collective-permute-start.15 = (bf16[4,80,640]{2,1,0:T(8,128)(2,1)S(1)}, bf16[4,80,640]{2,1,0:T(8,128)(2,1)S(1)}, u32[]{:S(2)}, u32[]{:S(2)}) collective-permute-start(bf16[4,80,640]{2,1,0:T(8,128)(2,1)S(1)} %fusion.20), channel_id=1, source_target_pairs={{0,8},{1,9},{2,10},{3,11},{4,28},{5,29},{6,30},{7,31},{8,16},{9,17... | collective-permute-start | bytes 1228808 | tf_op jit(solution)/shard_map/ppermute | solution.py:651
  187.5 9.2 %collective-permute-start.12 = (bf16[4,80,640]{2,1,0:T(8,128)(2,1)S(1)}, bf16[4,80,640]{2,1,0:T(8,128)(2,1)S(1)}, u32[]{:S(2)}, u32[]{:S(2)}) collective-permute-start(bf16[4,80,640]{2,1,0:T(8,128)(2,1)S(1)} %fusion.8), channel_id=1, source_target_pairs={{0,32},{1,33},{2,34},{3,35},{4,100},{5,101},{6,102},{7,103},{8,40}... | collective-permute-start | bytes 1228808 | tf_op jit(solution)/shard_map/ppermute | solution.py:651
  191.6 16.2 %collective-permute-start.8 = (bf16[4,80,640]{2,1,0:T(8,128)(2,1)S(1)}, bf16[4,80,640]{2,1,0:T(8,128)(2,1)S(1)}, u32[]{:S(2)}, u32[]{:S(2)}) collective-permute-start(bf16[4,80,640]{2,1,0:T(8,128)(2,1)S(1)} %fusion.11), channel_id=1, source_target_pairs={{0,32},{1,33},{2,34},{3,35},{4,100},{5,101},{6,102},{7,103},{8,40}... | collective-permute-start | bytes 1228808 | tf_op jit(solution)/shard_map/ppermute | solution.py:651
  192.9 9.2 %collective-permute-start.20 = (bf16[4,80,640]{2,1,0:T(8,128)(2,1)S(1)}, bf16[4,80,640]{2,1,0:T(8,128)(2,1)S(1)}, u32[]{:S(2)}, u32[]{:S(2)}) collective-permute-start(bf16[4,80,640]{2,1,0:T(8,128)(2,1)S(1)} %fusion.2), channel_id=1, source_target_pairs={{0,8},{1,9},{2,10},{3,11},{4,28},{5,29},{6,30},{7,31},{8,16},{9,17... | collective-permute-start | bytes 1228808 | tf_op jit(solution)/shard_map/ppermute | solution.py:651
  195.8 10.8 %collective-permute-start.16 = (bf16[4,80,640]{2,1,0:T(8,128)(2,1)S(1)}, bf16[4,80,640]{2,1,0:T(8,128)(2,1)S(1)}, u32[]{:S(2)}, u32[]{:S(2)}) collective-permute-start(bf16[4,80,640]{2,1,0:T(8,128)(2,1)S(1)} %fusion.5), channel_id=1, source_target_pairs={{0,8},{1,9},{2,10},{3,11},{4,28},{5,29},{6,30},{7,31},{8,16},{9,17... | collective-permute-start | bytes 1228808 | tf_op jit(solution)/shard_map/ppermute | solution.py:651
  197.8 24.7 %collective-permute-start.13 = (bf16[4,80,640]{2,1,0:T(8,128)(2,1)S(1)}, bf16[4,80,640]{2,1,0:T(8,128)(2,1)S(1)}, u32[]{:S(2)}, u32[]{:S(2)}) collective-permute-start(bf16[4,80,640]{2,1,0:T(8,128)(2,1)S(1)} %fusion.7), channel_id=1, source_target_pairs={{0,32},{1,33},{2,34},{3,35},{4,100},{5,101},{6,102},{7,103},{8,40}... | collective-permute-start | bytes 1228808 | tf_op jit(solution)/shard_map/ppermute | solution.py:651
  203.3 9.2 %collective-permute-start.21 = (bf16[4,80,640]{2,1,0:T(8,128)(2,1)S(1)}, bf16[4,80,640]{2,1,0:T(8,128)(2,1)S(1)}, u32[]{:S(2)}, u32[]{:S(2)}) collective-permute-start(bf16[4,80,640]{2,1,0:T(8,128)(2,1)S(1)} %fusion.1), channel_id=1, source_target_pairs={{0,8},{1,9},{2,10},{3,11},{4,28},{5,29},{6,30},{7,31},{8,16},{9,17... | collective-permute-start | bytes 1228808 | tf_op jit(solution)/shard_map/ppermute | solution.py:651
  207.7 9.2 %collective-permute-start.17 = (bf16[4,80,640]{2,1,0:T(8,128)(2,1)S(1)}, bf16[4,80,640]{2,1,0:T(8,128)(2,1)S(1)}, u32[]{:S(2)}, u32[]{:S(2)}) collective-permute-start(bf16[4,80,640]{2,1,0:T(8,128)(2,1)S(1)} %fusion.4), channel_id=1, source_target_pairs={{0,8},{1,9},{2,10},{3,11},{4,28},{5,29},{6,30},{7,31},{8,16},{9,17... | collective-permute-start | bytes 1228808 | tf_op jit(solution)/shard_map/ppermute | solution.py:651
  209.0 14.9 %collective-permute-start.9 = (bf16[4,80,640]{2,1,0:T(8,128)(2,1)S(1)}, bf16[4,80,640]{2,1,0:T(8,128)(2,1)S(1)}, u32[]{:S(2)}, u32[]{:S(2)}) collective-permute-start(bf16[4,80,640]{2,1,0:T(8,128)(2,1)S(1)} %fusion.10), channel_id=1, source_target_pairs={{0,32},{1,33},{2,34},{3,35},{4,100},{5,101},{6,102},{7,103},{8,40}... | collective-permute-start | bytes 1228808 | tf_op jit(solution)/shard_map/ppermute | solution.py:651
  218.2 8.6 %collective-permute-start.24 = (bf16[2,80,640]{2,1,0:T(8,128)(2,1)S(1)}, bf16[2,80,640]{2,1,0:T(8,128)(2,1)S(1)}, u32[]{:S(2)}, u32[]{:S(2)}) collective-permute-start(bf16[2,80,640]{2,1,0:T(8,128)(2,1)S(1)} %pad_maximum_fusion.2), channel_id=1, source_target_pairs={{0,64},{1,65},{2,66},{3,67},{4,68},{5,69},{6,70},{7,71},{8,72},{9,... | collective-permute-start | bytes 614408 | tf_op jit(solution)/shard_map/ppermute | solution.py:651
  220.1 8.2 %collective-permute-start.23 = (bf16[2,80,640]{2,1,0:T(8,128)(2,1)S(1)}, bf16[2,80,640]{2,1,0:T(8,128)(2,1)S(1)}, u32[]{:S(2)}, u32[]{:S(2)}) collective-permute-start(bf16[2,80,640]{2,1,0:T(8,128)(2,1)S(1)} %pad_maximum_fusion.1), channel_id=1, source_target_pairs={{0,96},{1,97},{2,98},{3,99},{4,100},{5,101},{6,102},{7,103},{8,104... | collective-permute-start | bytes 614408 | tf_op jit(solution)/shard_map/ppermute | solution.py:651
  221.7 7.0 %collective-permute-start.22 = (bf16[2,80,640]{2,1,0:T(8,128)(2,1)S(1)}, bf16[2,80,640]{2,1,0:T(8,128)(2,1)S(1)}, u32[]{:S(2)}, u32[]{:S(2)}) collective-permute-start(bf16[2,80,640]{2,1,0:T(8,128)(2,1)S(1)} %pad_maximum_fusion), channel_id=1, source_target_pairs={{0,32},{1,33},{2,34},{3,35},{4,36},{5,37},{6,38},{7,39},{8,40},{9,... | collective-permute-start | bytes 614408 | tf_op jit(solution)/shard_map/ppermute | solution.py:651
  225.1 8.7 %collective-permute-start.27 = (bf16[2,80,640]{2,1,0:T(8,128)(2,1)S(1)}, bf16[2,80,640]{2,1,0:T(8,128)(2,1)S(1)}, u32[]{:S(2)}, u32[]{:S(2)}) collective-permute-start(bf16[2,80,640]{2,1,0:T(8,128)(2,1)S(1)} %pad_maximum_fusion.5), channel_id=1, source_target_pairs={{0,16},{1,17},{2,18},{3,19},{4,20},{5,21},{6,22},{7,23},{8,24},{9,... | collective-permute-start | bytes 614408 | tf_op jit(solution)/shard_map/ppermute | solution.py:651
  225.2 8.5 %collective-permute-start.26 = (bf16[2,80,640]{2,1,0:T(8,128)(2,1)S(1)}, bf16[2,80,640]{2,1,0:T(8,128)(2,1)S(1)}, u32[]{:S(2)}, u32[]{:S(2)}) collective-permute-start(bf16[2,80,640]{2,1,0:T(8,128)(2,1)S(1)} %pad_maximum_fusion.4), channel_id=1, source_target_pairs={{0,24},{1,25},{2,26},{3,27},{4,28},{5,29},{6,30},{7,31},{8,0},{9,1... | collective-permute-start | bytes 614408 | tf_op jit(solution)/shard_map/ppermute | solution.py:651
  226.8 8.5 %collective-permute-start.25 = (bf16[2,80,640]{2,1,0:T(8,128)(2,1)S(1)}, bf16[2,80,640]{2,1,0:T(8,128)(2,1)S(1)}, u32[]{:S(2)}, u32[]{:S(2)}) collective-permute-start(bf16[2,80,640]{2,1,0:T(8,128)(2,1)S(1)} %pad_maximum_fusion.3), channel_id=1, source_target_pairs={{0,8},{1,9},{2,10},{3,11},{4,12},{5,13},{6,14},{7,15},{8,16},{9,17... | collective-permute-start | bytes 614408 | tf_op jit(solution)/shard_map/ppermute | solution.py:651
  (6 other events, 6.7 us)
Sparse Core Ops, SparseCore 0:
  170.8 43.2 reduce-scatter.1
